TPU v7x, 32 devices: a whole 2x2x4 slice. The times are simulated.
32 devices in a mesh: ctx: 8 (over y, x, core), wsh: 4 (over z).
Axes of the slice: x: 2, y: 2, z: 4, core: 2. Of those that a mesh axis runs over, the one named last changes fastest.
Arguments:
- block_input: bfloat16 [8, 1024, 768], P('wsh', 'ctx'), may hold values from -6 to 6
- ln1_gain: bfloat16 [768], P('wsh'), may hold values from 0.5 to 1.5
- ln1_bias: bfloat16 [768], P('wsh'), may hold values from -4 to 4
- w_qkv: bfloat16 [768, 2304], P('wsh'), may hold values from -0.21875 to 0.21875
- bias_query: bfloat16 [768], P('wsh'), may hold values from -4 to 4
- bias_value: bfloat16 [768], P('wsh'), may hold values from -1.5 to 1.5
- w_out: bfloat16 [768, 768], P('wsh'), may hold values from -6 to 6
- bias_out: bfloat16 [768], P('wsh'), may hold values from -4 to 4
- ln2_gain: bfloat16 [768], P('wsh'), may hold values from 0.5 to 1.5
- ln2_bias: bfloat16 [768], P('wsh'), may hold values from -4 to 4
- w_up: bfloat16 [768, 3072], P('wsh'), may hold values from -0.21875 to 0.21875
- bias_up: bfloat16 [3072], P('wsh'), may hold values from -6 to 6
- w_down: bfloat16 [3072, 768], P('wsh'), may hold values from -0.109375 to 0.109375
- bias_down: bfloat16 [768], P('wsh'), may hold values from -4 to 4
- pair_of_device: int32 [8], replicated, may hold values from 0 to 7, each once
- cotangent: bfloat16 [8, 1024, 768], P('wsh', 'ctx'), may hold values from -6 to 6
Outputs:
- output: bfloat16 [8, 1024, 768], P('wsh', 'ctx')
- grad_input: float32 [8, 1024, 768], P('wsh', 'ctx')
- grad_ln1_gain: float32 [768], P('wsh')
- grad_ln1_bias: float32 [768], P('wsh')
- grad_qkv: float32 [768, 2304], P('wsh')
- grad_bias_query: float32 [768], P('wsh')
- grad_bias_value: float32 [768], P('wsh')
- grad_out: float32 [768, 768], P('wsh')
- grad_bias_out: float32 [768], P('wsh')
- grad_ln2_gain: float32 [768], P('wsh')
- grad_ln2_bias: float32 [768], P('wsh')
- grad_up: float32 [768, 3072], P('wsh')
- grad_bias_up: float32 [3072], P('wsh')
- grad_down: float32 [3072, 768], P('wsh')
- grad_bias_down: float32 [768], P('wsh')
Inputs may be any that keep to these rules, and one draw needn't show every extreme that they name: Each of 0 to 7 appears once; device i of ctx holds, for each of its sequences, the blocks pair_of_device[i] and 15 - pair_of_device[i] of 64 tokens, the lower one first.
All inputs are finite; a program needn't handle non-finite values.
Results may differ from a plain program's by a relative error of at most 0.017.
Values may be sent and summed in bfloat16 or wider, within the bound.
A program may use at most 384 MiB of HBM per device.

v0:
```python
import math

import jax
import jax.numpy as jnp
from jax import lax
from jax.sharding import PartitionSpec as P

HEADS = 12


EPSILON = 1e-05
MASKED = -1000000000.0
LOWEST = -1e30


def layer_norm(values, gain, shift):
    center = jnp.mean(values, axis=-1, keepdims=True)
    offset = values - center
    spread = jnp.mean(offset * offset, axis=-1, keepdims=True)
    return offset * lax.rsqrt(spread + EPSILON) * gain + shift


def gelu_tanh(values):
    return jax.nn.gelu(values, approximate=True)


def key_positions(row_index, pair_table, block_len):
    places = pair_table.shape[0]
    owner = row_index // (2 * block_len)
    inner = row_index % (2 * block_len)
    hits = owner[:, None] == jnp.arange(places, dtype=jnp.int32)[None, :]
    chosen = jnp.sum(jnp.where(hits, pair_table[None, :], 0), axis=1)
    which = jnp.where(inner < block_len, chosen, 2 * places - 1 - chosen)
    return which * block_len + inner % block_len


def lower_rows(array, block_len):
    seq_count, row_total, feature = array.shape
    paired = array.reshape(seq_count, row_total // (2 * block_len), 2, block_len, feature)
    return paired[:, :, 0].reshape(seq_count, row_total // 2, feature)


def lower_spots(spots, block_len):
    return spots.reshape(-1, 2, block_len)[:, 0].reshape(-1)


def online_step(state, query, query_pos, keys, values, key_pos, scale):
    accum, top_score, total = state
    scores = jnp.einsum("sqhd,skhd->shqk", query, keys, preferred_element_type=jnp.float32) * scale
    scores = jnp.where(
        key_pos[None, None, None, :] <= query_pos[None, None, :, None], scores, MASKED
    )
    new_top = jnp.maximum(top_score, jnp.max(scores, axis=-1))
    fading = jnp.exp(top_score - new_top)
    weights = jnp.exp(scores - new_top[..., None])
    total = total * fading + jnp.sum(weights, axis=-1)
    accum = accum * fading[..., None] + jnp.einsum(
        "shqk,skhd->shqd", weights.astype(jnp.bfloat16), values, preferred_element_type=jnp.float32
    )
    return (accum, new_top, total)


def scores_back(query, query_pos, log_total, delta, grad_head, keys, values, key_pos, scale):
    scores = jnp.einsum("sqhd,skhd->shqk", query, keys, preferred_element_type=jnp.float32) * scale
    scores = jnp.where(
        key_pos[None, None, None, :] <= query_pos[None, None, :, None], scores, MASKED
    )
    probs = jnp.exp(scores - log_total[..., None])
    grad_probs = jnp.einsum(
        "sqhd,skhd->shqk", grad_head, values, preferred_element_type=jnp.float32
    )
    grad_scores = (probs * (grad_probs - delta[..., None])).astype(jnp.bfloat16)
    return (probs.astype(jnp.bfloat16), grad_scores)


def body(
    block_input,
    ln1_gain,
    ln1_bias,
    w_qkv,
    bias_query,
    bias_value,
    w_out,
    bias_out,
    ln2_gain,
    ln2_bias,
    w_up,
    bias_up,
    w_down,
    bias_down,
    pair_of_device,
    cotangent,
):
    gathered_params = (
        lax.all_gather(ln1_gain, "wsh", axis=0, tiled=True),
        lax.all_gather(ln1_bias, "wsh", axis=0, tiled=True),
        lax.all_gather(w_qkv, "wsh", axis=0, tiled=True),
        lax.all_gather(bias_query, "wsh", axis=0, tiled=True),
        lax.all_gather(bias_value, "wsh", axis=0, tiled=True),
        lax.all_gather(w_out, "wsh", axis=0, tiled=True),
        lax.all_gather(bias_out, "wsh", axis=0, tiled=True),
        lax.all_gather(ln2_gain, "wsh", axis=0, tiled=True),
        lax.all_gather(ln2_bias, "wsh", axis=0, tiled=True),
        lax.all_gather(w_up, "wsh", axis=0, tiled=True),
        lax.all_gather(bias_up, "wsh", axis=0, tiled=True),
        lax.all_gather(w_down, "wsh", axis=0, tiled=True),
        lax.all_gather(bias_down, "wsh", axis=0, tiled=True),
    )
    (
        gain_first,
        shift_first,
        whole_qkv,
        query_shift,
        value_shift,
        whole_out,
        out_shift,
        gain_second,
        shift_second,
        whole_up,
        up_shift,
        whole_down,
        down_shift,
    ) = gathered_params
    gain_first = gain_first.astype(jnp.float32)
    shift_first = shift_first.astype(jnp.float32)
    query_shift = query_shift.astype(jnp.float32)
    value_shift = value_shift.astype(jnp.float32)
    out_shift = out_shift.astype(jnp.float32)
    gain_second = gain_second.astype(jnp.float32)
    shift_second = shift_second.astype(jnp.float32)
    up_shift = up_shift.astype(jnp.float32)
    down_shift = down_shift.astype(jnp.float32)
    seq_count, row_count, model_width = block_input.shape
    block_len = row_count // 2
    head_count = HEADS
    head_size = model_width // head_count
    scale = head_size ** (-0.5)
    places = lax.axis_size("ctx")
    own_index = lax.axis_index("ctx")
    own_pair = jnp.sum(
        jnp.where(jnp.arange(places, dtype=jnp.int32) == own_index, pair_of_device, 0)
    )
    offsets = jnp.arange(block_len, dtype=jnp.int32)
    qpos_low = own_pair * block_len + offsets
    qpos_up = (2 * places - 1 - own_pair) * block_len + offsets
    inputs_f = block_input.astype(jnp.float32)
    normed_f, ln_one_back = jax.vjp(layer_norm, inputs_f, gain_first, shift_first)
    normed = normed_f.astype(jnp.bfloat16)
    qkv_shift = jnp.concatenate([query_shift, jnp.zeros_like(query_shift), value_shift])
    qkv = (jnp.dot(normed, whole_qkv, preferred_element_type=jnp.float32) + qkv_shift).astype(
        jnp.bfloat16
    )
    queries = qkv[..., :model_width].reshape(seq_count, row_count, head_count, head_size)
    query_low = queries[:, :block_len]
    query_up = queries[:, block_len:]
    kv_local = qkv[..., model_width:]

    def split_keys(slab_rows):
        keys = slab_rows[..., :model_width].reshape(seq_count, -1, head_count, head_size)
        values = slab_rows[..., model_width:].reshape(seq_count, -1, head_count, head_size)
        return (keys, values)

    empty_state = (
        jnp.zeros((seq_count, head_count, block_len, head_size), jnp.float32),
        jnp.full((seq_count, head_count, block_len), LOWEST, jnp.float32),
        jnp.zeros((seq_count, head_count, block_len), jnp.float32),
    )
    slab = lax.all_gather(kv_local, "ctx", axis=1, tiled=True)
    row_total = slab.shape[1]
    stride = math.gcd(row_total, max(row_count, 512))

    def turn(index, running):
        offset_row = index * stride
        sub_rows = lax.dynamic_slice_in_dim(slab, offset_row, stride, 1)
        key_pos = key_positions(
            offset_row + jnp.arange(stride, dtype=jnp.int32), pair_of_device, block_len
        )
        keys, values = split_keys(sub_rows)
        low_keys, low_values = split_keys(lower_rows(sub_rows, block_len))
        low_pos = lower_spots(key_pos, block_len)
        state_low = online_step(
            running[0], query_low, qpos_low, low_keys, low_values, low_pos, scale
        )
        state_up = online_step(running[1], query_up, qpos_up, keys, values, key_pos, scale)
        return (state_low, state_up)

    states = lax.fori_loop(0, row_total // stride, turn, (empty_state, empty_state))

    def finish(state):
        accum, top_score, total = state
        return (accum / total[..., None], top_score + jnp.log(total))

    attended_low, log_low = finish(states[0])
    attended_up, log_up = finish(states[1])
    attended = jnp.transpose(jnp.concatenate([attended_low, attended_up], axis=2), (0, 2, 1, 3))
    attended_bf = attended.reshape(seq_count, row_count, model_width).astype(jnp.bfloat16)
    middle = (
        inputs_f + jnp.dot(attended_bf, whole_out, preferred_element_type=jnp.float32) + out_shift
    )
    normed_two_f, ln_two_back = jax.vjp(layer_norm, middle, gain_second, shift_second)
    normed_two = normed_two_f.astype(jnp.bfloat16)
    hidden = jnp.dot(normed_two, whole_up, preferred_element_type=jnp.float32) + up_shift
    active_f, gelu_back = jax.vjp(gelu_tanh, hidden)
    active = active_f.astype(jnp.bfloat16)
    output = (
        middle + jnp.dot(active, whole_down, preferred_element_type=jnp.float32) + down_shift
    ).astype(jnp.bfloat16)
    cotangent_f = cotangent.astype(jnp.float32)
    grad_down = jnp.einsum("srf,srd->fd", active, cotangent, preferred_element_type=jnp.float32)
    grad_bias_down = jnp.sum(cotangent_f, axis=(0, 1))
    grad_active = jnp.einsum(
        "srd,fd->srf", cotangent, whole_down, preferred_element_type=jnp.float32
    )
    grad_hidden = gelu_back(grad_active)[0].astype(jnp.bfloat16)
    grad_up = jnp.einsum("srd,srf->df", normed_two, grad_hidden, preferred_element_type=jnp.float32)
    grad_bias_up = jnp.sum(grad_hidden.astype(jnp.float32), axis=(0, 1))
    grad_normed_two = jnp.einsum(
        "srf,df->srd", grad_hidden, whole_up, preferred_element_type=jnp.float32
    )
    grad_middle_part, grad_ln2_gain, grad_ln2_bias = ln_two_back(grad_normed_two)
    grad_middle = cotangent_f + grad_middle_part
    grad_branch = grad_middle.astype(jnp.bfloat16)
    grad_out = jnp.einsum(
        "sri,sro->io", attended_bf, grad_branch, preferred_element_type=jnp.float32
    )
    grad_bias_out = jnp.sum(grad_branch.astype(jnp.float32), axis=(0, 1))
    grad_attended = jnp.einsum(
        "sro,io->sri", grad_branch, whole_out, preferred_element_type=jnp.float32
    ).astype(jnp.bfloat16)
    grad_heads = grad_attended.reshape(seq_count, row_count, head_count, head_size)
    grad_low = grad_heads[:, :block_len]
    grad_high = grad_heads[:, block_len:]
    delta = jnp.einsum("sqhd,sqhd->shq", grad_heads.astype(jnp.float32), attended)
    delta_low = delta[:, :, :block_len]
    delta_up = delta[:, :, block_len:]
    gathered = lax.all_gather(kv_local, "ctx", axis=1, tiled=True)
    total_rows = gathered.shape[1]

    def back_sub(sub_rows, first_row):
        stride = sub_rows.shape[1]
        key_pos = key_positions(
            first_row + jnp.arange(stride, dtype=jnp.int32), pair_of_device, block_len
        )
        keys, values = split_keys(sub_rows)
        low_keys, low_values = split_keys(lower_rows(sub_rows, block_len))
        low_pos = lower_spots(key_pos, block_len)
        probs_up, dscore_up = scores_back(
            query_up, qpos_up, log_up, delta_up, grad_high, keys, values, key_pos, scale
        )
        probs_low, dscore_low = scores_back(
            query_low, qpos_low, log_low, delta_low, grad_low, low_keys, low_values, low_pos, scale
        )
        return (keys, low_keys, probs_up, dscore_up, probs_low, dscore_low)

    def query_terms(parts):
        keys, low_keys, probs_up, dscore_up, probs_low, dscore_low = parts
        term_low = (
            jnp.einsum("shqk,skhd->sqhd", dscore_low, low_keys, preferred_element_type=jnp.float32)
            * scale
        )
        term_up = (
            jnp.einsum("shqk,skhd->sqhd", dscore_up, keys, preferred_element_type=jnp.float32)
            * scale
        )
        return (term_low, term_up)

    def key_value_terms(parts):
        keys, low_keys, probs_up, dscore_up, probs_low, dscore_low = parts
        stride = keys.shape[1]
        dkey_all = (
            jnp.einsum("shqk,sqhd->kshd", dscore_up, query_up, preferred_element_type=jnp.float32)
            * scale
        )
        dvalue_all = jnp.einsum(
            "shqk,sqhd->kshd", probs_up, grad_high, preferred_element_type=jnp.float32
        )
        dkey_low = (
            jnp.einsum("shqk,sqhd->kshd", dscore_low, query_low, preferred_element_type=jnp.float32)
            * scale
        )
        dvalue_low = jnp.einsum(
            "shqk,sqhd->kshd", probs_low, grad_low, preferred_element_type=jnp.float32
        )
        both_all = jnp.concatenate(
            [
                dkey_all.reshape(stride, seq_count, model_width),
                dvalue_all.reshape(stride, seq_count, model_width),
            ],
            axis=-1,
        )
        both_low = jnp.concatenate(
            [
                dkey_low.reshape(stride // 2, seq_count, model_width),
                dvalue_low.reshape(stride // 2, seq_count, model_width),
            ],
            axis=-1,
        )
        split_all = both_all.reshape(stride // row_count, 2, block_len, seq_count, 2 * model_width)
        merged = jnp.stack(
            [
                split_all[:, 0]
                + both_low.reshape(stride // row_count, block_len, seq_count, 2 * model_width),
                split_all[:, 1],
            ],
            axis=1,
        )
        return merged.reshape(stride, seq_count, 2 * model_width)

    zero_query = jnp.zeros((seq_count, block_len, head_count, head_size), jnp.float32)
    full_stride = math.gcd(total_rows, max(row_count, 512))

    def query_turn(index, running):
        first_row = index * full_stride
        sub_rows = lax.dynamic_slice_in_dim(gathered, first_row, full_stride, 1)
        term_low, term_up = query_terms(back_sub(sub_rows, first_row))
        return (running[0] + term_low, running[1] + term_up)

    dquery_low, dquery_up = lax.fori_loop(
        0, total_rows // full_stride, query_turn, (zero_query, zero_query)
    )
    row_total = row_count * lax.axis_size("ctx")
    key_stride = math.gcd(row_total, max(row_count, 512))

    def rows_turn(running, index):
        offset_row = index * key_stride
        sub_rows = lax.dynamic_slice_in_dim(gathered, offset_row, key_stride, 1)
        return (running, key_value_terms(back_sub(sub_rows, offset_row)))

    ignored, pieces = lax.scan(
        rows_turn, None, jnp.arange(row_total // key_stride, dtype=jnp.int32)
    )
    summed = lax.psum_scatter(
        pieces.reshape(row_total, seq_count, 2 * model_width),
        "ctx",
        scatter_dimension=0,
        tiled=True,
    )
    grad_kv = jnp.transpose(summed, (1, 0, 2)).astype(jnp.bfloat16)
    grad_query = (
        jnp.concatenate([dquery_low, dquery_up], axis=1)
        .reshape(seq_count, row_count, model_width)
        .astype(jnp.bfloat16)
    )
    grad_rows = jnp.concatenate([grad_query, grad_kv], axis=-1)
    grad_qkv = jnp.einsum("srd,sre->de", normed, grad_rows, preferred_element_type=jnp.float32)
    grad_bias_query = jnp.sum(grad_query.astype(jnp.float32), axis=(0, 1))
    grad_bias_value = jnp.sum(grad_kv[..., model_width:].astype(jnp.float32), axis=(0, 1))
    grad_normed = jnp.einsum(
        "sre,de->srd", grad_rows, whole_qkv, preferred_element_type=jnp.float32
    )
    grad_input_part, grad_ln1_gain, grad_ln1_bias = ln_one_back(grad_normed)
    grad_input = grad_middle + grad_input_part
    owned = (
        lax.psum_scatter(
            grad_ln1_gain.astype(jnp.bfloat16), "wsh", scatter_dimension=0, tiled=True
        ).astype(jnp.float32),
        lax.psum_scatter(
            grad_ln1_bias.astype(jnp.bfloat16), "wsh", scatter_dimension=0, tiled=True
        ).astype(jnp.float32),
        lax.psum_scatter(
            grad_qkv.astype(jnp.bfloat16), "wsh", scatter_dimension=0, tiled=True
        ).astype(jnp.float32),
        lax.psum_scatter(
            grad_bias_query.astype(jnp.bfloat16), "wsh", scatter_dimension=0, tiled=True
        ).astype(jnp.float32),
        lax.psum_scatter(
            grad_bias_value.astype(jnp.bfloat16), "wsh", scatter_dimension=0, tiled=True
        ).astype(jnp.float32),
        lax.psum_scatter(
            grad_out.astype(jnp.bfloat16), "wsh", scatter_dimension=0, tiled=True
        ).astype(jnp.float32),
        lax.psum_scatter(
            grad_bias_out.astype(jnp.bfloat16), "wsh", scatter_dimension=0, tiled=True
        ).astype(jnp.float32),
        lax.psum_scatter(
            grad_ln2_gain.astype(jnp.bfloat16), "wsh", scatter_dimension=0, tiled=True
        ).astype(jnp.float32),
        lax.psum_scatter(
            grad_ln2_bias.astype(jnp.bfloat16), "wsh", scatter_dimension=0, tiled=True
        ).astype(jnp.float32),
        lax.psum_scatter(
            grad_up.astype(jnp.bfloat16), "wsh", scatter_dimension=0, tiled=True
        ).astype(jnp.float32),
        lax.psum_scatter(
            grad_bias_up.astype(jnp.bfloat16), "wsh", scatter_dimension=0, tiled=True
        ).astype(jnp.float32),
        lax.psum_scatter(
            grad_down.astype(jnp.bfloat16), "wsh", scatter_dimension=0, tiled=True
        ).astype(jnp.float32),
        lax.psum_scatter(
            grad_bias_down.astype(jnp.bfloat16), "wsh", scatter_dimension=0, tiled=True
        ).astype(jnp.float32),
    )
    owned = lax.psum(tuple(owned), "ctx")
    return (output, grad_input) + tuple(owned)


def solution(mesh):
    in_specs = (
        P("wsh", "ctx", None),
        P("wsh"),
        P("wsh"),
        P("wsh", None),
        P("wsh"),
        P("wsh"),
        P("wsh", None),
        P("wsh"),
        P("wsh"),
        P("wsh"),
        P("wsh", None),
        P("wsh"),
        P("wsh", None),
        P("wsh"),
        P(),
        P("wsh", "ctx", None),
    )
    out_specs = (
        P("wsh", "ctx", None),
        P("wsh", "ctx", None),
        P("wsh"),
        P("wsh"),
        P("wsh", None),
        P("wsh"),
        P("wsh"),
        P("wsh", None),
        P("wsh"),
        P("wsh"),
        P("wsh"),
        P("wsh", None),
        P("wsh"),
        P("wsh", None),
        P("wsh"),
    )
    return jax.shard_map(body, mesh=mesh, in_specs=in_specs, out_specs=out_specs, check_vma=False)
```

profile of v0, /device:TPU:0, one launch (start us, length us, event | category | flops | bytes accessed | tf_op | source)
XLA Modules:
  0.0 1204.5 jit_solution(6926989747983245150)
XLA Ops:
  15.8 21.3 %all-reduce.19 = (bf16[768]{0:T(1024)(128)(2,1)S(1)}, bf16[768]{0:T(1024)(128)(2,1)S(1)}, bf16[768]{0:T(1024)(128)(2,1)S(1)}, bf16[768]{0:T(1024)(128)(2,1)S(1)}...) all-reduce(bf16[768]{0:T(1024)(128)(2,1)S(1)} %dynamic-update-slice, ...), channel_id=1, replica_groups=mesh['ctx'=8,'wsh'=4] {'wsh'}, use_global_device_ids=true, to_apply=%add.3 | all-reduce | flops 5376 | bytes 21504
  40.1 42.4 %all-gather.7.cloned.1.call-done = bf16[768,2304]{1,0:T(8,128)(2,1)} async-done(((bf16[192,2304]{1,0:T(8,128)(2,1)}), bf16[768,2304]{1,0:T(8,128)(2,1)}) %all-gather.7.cloned.1.call-update) | async-done | bytes 3538960 | tf_op jit(solution)/shard_map/all_gather | solution.py:97
  82.5 3.3 fusion.117
  92.7 13.4 %all-gather = bf16[4,1,768]{2,1,0:T(2,128)(2,1)S(1)} all-gather(bf16[1,1,768]{2,1,0:T(2,128)(2,1)S(1)} %reshape.722), channel_id=1, replica_groups=mesh['ctx'=8,'wsh'=4] {'wsh'}, dimensions={0}, use_global_device_ids=true | all-gather | bytes 7680 | tf_op jit(solution)/shard_map/all_gather | solution.py:105
  109.6 21.6 %all-gather.9.cloned.1.call-done = bf16[2,1024,1536]{2,1,0:T(8,128)(2,1)} async-done(((bf16[2,128,1536]{2,1,0:T(8,128)(2,1)}), bf16[2,1024,1536]{2,1,0:T(8,128)(2,1)}) %all-gather.9.cloned.1.call-update) | async-done | bytes 6291472 | tf_op jit(solution)/shard_map/all_gather | solution.py:168
  131.2 54.0 %while.61 = (s32[]{:T(128)}, f32[2,12,64,64]{3,2,1,0:T(8,128)}, f32[2,12,64]{2,1,0:T(8,128)}, f32[2,12,64]{2,1,0:T(8,128)}, f32[2,12,64,64]{3,2,1,0:T(8,128)}, /...) while((s32[]{:T(128)}, f32[2,12,64,64]{3,2,1,0:T(8,128)}, ...), condition=%wide.region_9.10_spmd.clone, body=%wide.region_3.9_spmd.clone.sunk | while | flops 314112128 | bytes 81302960 | solution.py:187
  138.3 3.9 constant_dynamic-slice_fusion.18
  150.5 2.7 copy.240
  153.3 3.7 fusion.307
  165.3 3.8 constant_dynamic-slice_fusion.18
  178.1 2.7 copy.240
  180.8 3.8 fusion.307
  193.0 60.3 %all-gather.13.cloned.1.call-done = bf16[768,3072]{1,0:T(8,128)(2,1)} async-done(((bf16[192,3072]{1,0:T(8,128)(2,1)}), bf16[768,3072]{1,0:T(8,128)(2,1)}) %all-gather.13.cloned.1.call-update) | async-done | bytes 4718608 | tf_op jit(solution)/shard_map/all_gather | solution.py:104
  253.3 5.5 fusion.114
  258.7 83.8 %all-gather.15.cloned.1.call-done = bf16[3072,768]{1,0:T(8,128)(2,1)} async-done(((bf16[768,768]{1,0:T(8,128)(2,1)}), bf16[3072,768]{1,0:T(8,128)(2,1)}) %all-gather.15.cloned.1.call-update) | async-done | bytes 4718608 | tf_op jit(solution)/shard_map/all_gather | solution.py:106
  342.6 7.5 fusion.177
  360.1 325.0 %while.60 = (s32[]{:T(128)}, f32[2,512,2,1536]{3,1,0,2:T(8,128)}, s32[2]{0:T(128)S(1)}, s32[8]{0:T(128)}, bf16[2,1024,1536]{2,1,0:T(8,128)(2,1)}, /*index=5*/bf1...) while((s32[]{:T(128)}, f32[2,512,2,1536]{3,1,0,2:T(8,128)}, ...), condition=%wide.region_19.20_spmd.clone, body=%wide.region_17.19_spmd.clone.sunk | while | flops 619027584 | bytes 180458000 | solution.py:329
  376.1 3.3 constant_dynamic-slice_fusion.15
  388.1 4.9 multiply_bitcast_fusion.4
  393.0 7.5 concatenate.51
  400.6 7.7 constant_dynamic-update-slice_fusion.6
  408.2 2.6 convolution_bitcast_fusion.4
  410.8 7.7 concatenate.52
  418.5 7.8 constant_dynamic-update-slice_fusion.7
  431.5 2.8 concatenate.53
  436.6 3.7 multiply_bitcast_fusion.5
  440.4 3.8 concatenate.54
  444.1 46.6 %slice_add_fusion.2 = (f32[4,1,64,2,1536]{2,1,0,4,3:T(1,128)S(1)}, f32[4,1,64,2,1536]{2,1,0,4,3:T(1,128)S(1)}) fusion(f32[4,2,64,2,1536]{2,1,0,4,3:T(2,128)} %constant_dynamic-update-slice_fusion.7, f32[4,1,64,2,768]{2,1,0,4,3:T(1,128)S(1)} %bitcast.383, f32[4,1,64,2,768]{2,1,0,4,3:T(1,128)} %bitcast.384), kind=kLoop, calls=%fused_computation.7.clone.1 | loop fusion | flops 1572864 | bytes 15728640 | tf_op jit(solution)/shard_map/while/body/eval_jaxpr/add | solution.py:301
  490.7 15.4 %pad_maximum_fusion.7 = f32[4,2,64,2,1536]{2,1,0,4,3:T(2,128)} fusion(f32[4,1,64,2,1536]{2,1,0,4,3:T(1,128)S(1)} %get-tuple-element.1803, f32[4,1,64,2,1536]{2,1,0,4,3:T(1,128)S(1)} %get-tuple-element.1804), kind=kLoop, calls=%fused_computation.6.clone.1 | loop fusion | flops 1572864 | bytes 12582912 | tf_op jit(solution)/shard_map/while/body/eval_jaxpr/stack | solution.py:299
  506.2 17.7 %copy.236 = f32[4,2,64,2,1536]{4,2,1,0,3:T(8,128)} copy(f32[4,2,64,2,1536]{2,1,0,4,3:T(2,128)} %pad_maximum_fusion.7) | data formatting | bytes 12582912 | tf_op jit(solution)/shard_map/while/body/eval_jaxpr/stack | solution.py:299
  523.9 5.9 constant_dynamic-update-slice_fusion.8
  531.0 3.3 constant_dynamic-slice_fusion.15
  543.0 4.9 multiply_bitcast_fusion.4
  547.9 7.5 concatenate.51
  555.5 7.7 constant_dynamic-update-slice_fusion.6
  563.1 2.6 convolution_bitcast_fusion.4
  565.8 7.7 concatenate.52
  573.5 7.8 constant_dynamic-update-slice_fusion.7
  586.4 2.8 concatenate.53
  591.6 3.7 multiply_bitcast_fusion.5
  595.3 3.8 concatenate.54
  599.0 46.6 %slice_add_fusion.2 = (f32[4,1,64,2,1536]{2,1,0,4,3:T(1,128)S(1)}, f32[4,1,64,2,1536]{2,1,0,4,3:T(1,128)S(1)}) fusion(f32[4,2,64,2,1536]{2,1,0,4,3:T(2,128)} %constant_dynamic-update-slice_fusion.7, f32[4,1,64,2,768]{2,1,0,4,3:T(1,128)S(1)} %bitcast.383, f32[4,1,64,2,768]{2,1,0,4,3:T(1,128)} %bitcast.384), kind=kLoop, calls=%fused_computation.7.clone.1 | loop fusion | flops 1572864 | bytes 15728640 | tf_op jit(solution)/shard_map/while/body/eval_jaxpr/add | solution.py:301
  645.7 15.4 %pad_maximum_fusion.7 = f32[4,2,64,2,1536]{2,1,0,4,3:T(2,128)} fusion(f32[4,1,64,2,1536]{2,1,0,4,3:T(1,128)S(1)} %get-tuple-element.1803, f32[4,1,64,2,1536]{2,1,0,4,3:T(1,128)S(1)} %get-tuple-element.1804), kind=kLoop, calls=%fused_computation.6.clone.1 | loop fusion | flops 1572864 | bytes 12582912 | tf_op jit(solution)/shard_map/while/body/eval_jaxpr/stack | solution.py:299
  661.1 17.7 %copy.236 = f32[4,2,64,2,1536]{4,2,1,0,3:T(8,128)} copy(f32[4,2,64,2,1536]{2,1,0,4,3:T(2,128)} %pad_maximum_fusion.7) | data formatting | bytes 12582912 | tf_op jit(solution)/shard_map/while/body/eval_jaxpr/stack | solution.py:299
  678.8 5.9 constant_dynamic-update-slice_fusion.8
  687.8 3.7 bitcast_convert_fusion.1
  694.4 5.0 bitcast_convert_fusion
  702.4 51.6 %while.62 = (s32[]{:T(128)}, f32[2,64,12,64]{1,3,2,0:T(8,128)}, f32[2,64,12,64]{1,3,2,0:T(8,128)}, bf16[2,1024,1536]{2,1,0:T(8,128)(2,1)}, s32[8]{0:T(128)}, /*i...) while((s32[]{:T(128)}, f32[2,64,12,64]{1,3,2,0:T(8,128)}, ...), condition=%wide.region_16.17_spmd.clone, body=%wide.region_14.16_spmd.clone.sunk | while | flops 460758144 | bytes 47346784 | solution.py:318
  709.5 2.9 fusion.321
  712.3 3.7 constant_dynamic-slice_fusion.20
  722.9 5.3 fusion.324
  735.3 3.2 fusion.321
  738.5 3.3 constant_dynamic-slice_fusion.20
  748.6 5.4 fusion.324
  756.2 20.0 %reduce-scatter.6.cloned.1.call-done = f32[128,2,1536]{2,0,1:T(8,128)} async-done(((f32[1024,2,1536]{2,0,1:T(8,128)}), f32[128,2,1536]{2,0,1:T(8,128)}) %reduce-scatter.6.cloned.1.call-update) | async-done | bytes 1572880 | tf_op jit(solution)/shard_map/reduce_scatter | solution.py:332
  777.7 3.0 bitcast_convert_fusion.2
  783.0 25.3 %reduce-scatter.10.cloned.1.call-done = bf16[192,768]{1,0:T(8,128)(2,1)} async-done(((bf16[768,768]{1,0:T(8,128)(2,1)}), bf16[192,768]{1,0:T(8,128)(2,1)}) %reduce-scatter.10.cloned.1.call-update) | async-done | bytes 294928 | tf_op jit(solution)/shard_map/reduce_scatter | solution.py:369
  808.3 86.3 %reduce-scatter.12.cloned.1.call-done = bf16[192,3072]{1,0:T(8,128)(2,1)} async-done(((bf16[768,3072]{1,0:T(8,128)(2,1)}), bf16[192,3072]{1,0:T(8,128)(2,1)}) %reduce-scatter.12.cloned.1.call-update) | async-done | bytes 1179664 | tf_op jit(solution)/shard_map/reduce_scatter | solution.py:381
  894.6 88.1 %reduce-scatter.14.cloned.1.call-done = bf16[768,768]{1,0:T(8,128)(2,1)} async-done(((bf16[3072,768]{1,0:T(8,128)(2,1)}), bf16[768,768]{1,0:T(8,128)(2,1)}) %reduce-scatter.14.cloned.1.call-update) | async-done | bytes 1179664 | tf_op jit(solution)/shard_map/reduce_scatter | solution.py:387
  983.3 3.9 fusion.163
  987.7 19.9 %all-reduce.18 = (bf16[768]{0:T(1024)(128)(2,1)S(1)}, bf16[768]{0:T(1024)(128)(2,1)S(1)}, bf16[768]{0:T(1024)(128)(2,1)S(1)}, bf16[768]{0:T(1024)(128)(2,1)S(1)}...) all-reduce(bf16[768]{0:T(1024)(128)(2,1)} %copy-done.77, ...), channel_id=1, replica_groups=mesh['ctx'=8,'wsh'=4] {'wsh'}, use_global_device_ids=true, to_apply=%add.7 | all-reduce | flops 9984 | bytes 39936
  1009.6 5.3 fusion.137
  1014.8 37.9 %reduce-scatter.8.cloned.1.call-done = bf16[192,2304]{1,0:T(8,128)(2,1)} async-done(((bf16[768,2304]{1,0:T(8,128)(2,1)}), bf16[192,2304]{1,0:T(8,128)(2,1)}) %reduce-scatter.8.cloned.1.call-update) | async-done | bytes 884752 | tf_op jit(solution)/shard_map/reduce_scatter | solution.py:360
  1052.7 144.7 %all-reduce.21 = (f32[192]{0:T(256)}, f32[192]{0:T(256)}, f32[192,2304]{1,0:T(8,128)}, f32[192]{0:T(256)}, f32[192]{0:T(256)}, /*index=5*/f32[192,768]{1,0:T(8,1...) all-reduce(f32[192]{0:T(256)S(1)} %dynamic-slice_convert_fusion.8, ...), channel_id=1, replica_groups=mesh['ctx'=8,'wsh'=4] {'ctx'}, use_global_device_ids=true, to_apply=%region_25.26 | all-reduce | flops 1771776 | bytes 10635264 | tf_op jit(solution)/shard_map/psum | solution.py:394
  (481 shorter events, 147.3 us)
Async XLA Ops:
  7.2 75.3 %all-gather.7.cloned.1.call-start = ((), (), s32[]{:S(2)}) async-start(), calls=%async_computation.5 | async-start | bytes 4423680 | tf_op jit(solution)/shard_map/all_gather | solution.py:97
  7.9 123.3 %all-gather.9.cloned.1.call-start = ((), (), s32[]{:S(2)}) async-start(), calls=%async_computation.6 | async-start | bytes 7077888 | tf_op jit(solution)/shard_map/all_gather | solution.py:168
  37.1 48.8 %copy-start.78 = (f32[768]{0:T(1024)}, f32[768]{0:T(1024)S(1)}, u32[]{:S(2)}) copy-start(f32[768]{0:T(1024)S(1)} %convert_element_type.223) | copy-start | bytes 9220
  37.1 48.7 %copy-start.63 = (f32[768]{0:T(1024)}, f32[768]{0:T(1024)S(1)}, u32[]{:S(2)}) copy-start(f32[768]{0:T(1024)S(1)} %convert_element_type.222) | copy-start | bytes 9220
  38.3 47.6 %copy-start.65 = (f32[2,128]{1,0:T(2,128)}, f32[2,128]{1,0:T(2,128)S(1)}, u32[]{:S(2)}) copy-start(f32[2,128]{1,0:T(2,128)S(1)} %broadcast_multiply_fusion.1) | copy-start | bytes 3076
  40.1 45.8 %copy-start.69 = (f32[2,128]{1,0:T(2,128)}, f32[2,128]{1,0:T(2,128)S(1)}, u32[]{:S(2)}) copy-start(f32[2,128]{1,0:T(2,128)S(1)} %fusion.158) | copy-start | bytes 3076
  85.9 6.8 copy-start.80
  86.9 103.8 %all-gather.11.cloned.1.call-start = ((), (), s32[]{:S(2)}) async-start(), calls=%async_computation.7 | async-start | bytes 1474560 | tf_op jit(solution)/shard_map/all_gather | solution.py:100
  87.6 165.7 %all-gather.13.cloned.1.call-start = ((), (), s32[]{:S(2)}) async-start(), calls=%async_computation.8 | async-start | bytes 5898240 | tf_op jit(solution)/shard_map/all_gather | solution.py:104
  88.2 254.4 %all-gather.15.cloned.1.call-start = ((), (), s32[]{:S(2)}) async-start(), calls=%async_computation.9 | async-start | bytes 5898240 | tf_op jit(solution)/shard_map/all_gather | solution.py:106
  88.8 687.4 %reduce-scatter.6.cloned.1.call-start = ((), (), s32[]{:S(2)}) async-start(), calls=%async_computation.10 | async-start | bytes 14155776 | tf_op jit(solution)/shard_map/reduce_scatter | solution.py:332
  107.8 23.5 %copy-start.14 = (bf16[2,64,12,64]{1,3,2,0:T(8,128)(2,1)}, bf16[2,64,12,64]{1,3,2,0:T(8,128)(2,1)S(1)}, u32[]{:S(2)}) copy-start(bf16[2,64,12,64]{1,3,2,0:T(8,128)(2,1)S(1)} %get-tuple-element.1916) | copy-start | bytes 589828
  145.5 3.5 copy-start
  153.3 3.7 copy-start.23
  172.6 4.0 copy-start
  172.7 3.9 copy-start.22
  180.8 3.8 copy-start.23
  185.3 3.8 copy-start.44
  185.3 3.8 copy-start.48
  186.7 4.0 copy-start.17
  186.7 4.0 copy-start.67
  190.4 62.8 %copy-start.50 = (f32[768]{0:T(1024)S(1)}, f32[768]{0:T(1024)}, u32[]{:S(2)}) copy-start(f32[768]{0:T(1024)} %convert_element_type.231) | copy-start | bytes 9220
  190.4 62.8 %copy-start.52 = (f32[768]{0:T(1024)S(1)}, f32[768]{0:T(1024)}, u32[]{:S(2)}) copy-start(f32[768]{0:T(1024)} %convert_element_type.232) | copy-start | bytes 9220
  190.6 68.1 %copy-start.26 = (bf16[2,128,12,64]{1,3,2,0:T(8,128)(2,1)}, bf16[2,128,12,64]{1,3,2,0:T(8,128)(2,1)S(1)}, u32[]{:S(2)}) copy-start(bf16[2,128,12,64]{1,3,2,0:T(8,128)(2,1)S(1)} %bitcast_convert_fusion.4) | copy-start | bytes 1179652
  192.7 159.6 %copy-start.11 = (f32[2,128,768]{2,1,0:T(8,128)}, f32[2,128,768]{2,1,0:T(8,128)S(1)}, u32[]{:S(2)}) copy-start(f32[2,128,768]{2,1,0:T(8,128)S(1)} %get-tuple-element.1523) | copy-start | bytes 2359300
  192.7 159.6 %copy-start.58 = (f32[2,128]{1,0:T(2,128)}, f32[2,128]{1,0:T(2,128)S(1)}, u32[]{:S(2)}) copy-start(f32[2,128]{1,0:T(2,128)S(1)} %broadcast_multiply_fusion) | copy-start | bytes 3076
  192.9 60.3 %copy-start.73 = (f32[2,128]{1,0:T(2,128)}, f32[2,128]{1,0:T(2,128)S(1)}, u32[]{:S(2)}) copy-start(f32[2,128]{1,0:T(2,128)S(1)} %multiply_reduce_fusion.2) | copy-start | bytes 3076
  192.9 159.4 %copy-start.61 = (f32[2,128]{1,0:T(2,128)}, f32[2,128]{1,0:T(2,128)S(1)}, u32[]{:S(2)}) copy-start(f32[2,128]{1,0:T(2,128)S(1)} %fusion.159) | copy-start | bytes 3076
  253.3 89.3 %copy-start.34 = (bf16[2,128,768]{2,1,0:T(8,128)(2,1)S(1)}, bf16[2,128,768]{2,1,0:T(8,128)(2,1)}, u32[]{:S(2)}) copy-start(bf16[2,128,768]{2,1,0:T(8,128)(2,1)} %param.37) | copy-start | bytes 1179652
  342.6 7.5 copy-start.24
  352.6 5.5 copy-start.20
  354.3 4.6 copy-start.33
  354.3 4.6 copy-start.45
  354.3 4.6 copy-start.49
  400.6 7.7 copy-start.4
  400.6 7.7 copy-start.19
  410.8 15.5 %slice-start = ((s8[6291456]{0:T(1024)(128)(4,1)}), s8[2097152]{0:T(1024)(128)(4,1)S(1)}, s32[]{:S(2)}) async-start(s8[6291456]{0:T(1024)(128)(4,1)} %bitcast.380), calls=%async_computation.15 | async-start | bytes 4194304 | tf_op jit(solution)/shard_map/while
  418.5 7.8 slice-start.1
  523.9 5.9 copy-start.83
  555.5 7.7 copy-start.4
  555.5 7.7 copy-start.19
  565.8 15.5 %slice-start = ((s8[6291456]{0:T(1024)(128)(4,1)}), s8[2097152]{0:T(1024)(128)(4,1)S(1)}, s32[]{:S(2)}) async-start(s8[6291456]{0:T(1024)(128)(4,1)} %bitcast.380), calls=%async_computation.15 | async-start | bytes 4194304 | tf_op jit(solution)/shard_map/while
  573.5 7.8 slice-start.1
  678.8 5.9 copy-start.83
  685.2 123.0 %reduce-scatter.10.cloned.1.call-start = ((), (), s32[]{:S(2)}) async-start(), calls=%async_computation.12 | async-start | bytes 1474560 | tf_op jit(solution)/shard_map/reduce_scatter | solution.py:369
  687.7 206.8 %reduce-scatter.12.cloned.1.call-start = ((), (), s32[]{:S(2)}) async-start(), calls=%async_computation.13 | async-start | bytes 5898240 | tf_op jit(solution)/shard_map/reduce_scatter | solution.py:381
  691.6 291.1 %reduce-scatter.14.cloned.1.call-start = ((), (), s32[]{:S(2)}) async-start(), calls=%async_computation.14 | async-start | bytes 5898240 | tf_op jit(solution)/shard_map/reduce_scatter | solution.py:387
  699.5 353.3 %reduce-scatter.8.cloned.1.call-start = ((), (), s32[]{:S(2)}) async-start(), calls=%async_computation.11 | async-start | bytes 4423680 | tf_op jit(solution)/shard_map/reduce_scatter | solution.py:360
  708.7 7.4 copy-start.54
  734.5 7.2 copy-start.54
  754.0 23.6 %copy-start.18 = (bf16[2,128,768]{2,1,0:T(8,128)(2,1)S(1)}, bf16[2,128,768]{2,1,0:T(8,128)(2,1)}, u32[]{:S(2)}) copy-start(bf16[2,128,768]{2,1,0:T(8,128)(2,1)} %param.22) | copy-start | bytes 1179652
  754.0 23.7 %copy-start.64 = (f32[768]{0:T(1024)S(1)}, f32[768]{0:T(1024)}, u32[]{:S(2)}) copy-start(f32[768]{0:T(1024)} %copy-done.63) | copy-start | bytes 9220
  754.0 23.7 %copy-start.66 = (f32[2,128]{1,0:T(2,128)S(1)}, f32[2,128]{1,0:T(2,128)}, u32[]{:S(2)}) copy-start(f32[2,128]{1,0:T(2,128)} %copy-done.65) | copy-start | bytes 3076
  754.0 23.7 %copy-start.70 = (f32[2,128]{1,0:T(2,128)S(1)}, f32[2,128]{1,0:T(2,128)}, u32[]{:S(2)}) copy-start(f32[2,128]{1,0:T(2,128)} %copy-done.69) | copy-start | bytes 3076
  754.0 23.7 %copy-start.79 = (f32[768]{0:T(1024)S(1)}, f32[768]{0:T(1024)}, u32[]{:S(2)}) copy-start(f32[768]{0:T(1024)} %copy-done.78) | copy-start | bytes 9220
  782.3 200.4 %copy-start.77 = (bf16[768]{0:T(1024)(128)(2,1)}, bf16[768]{0:T(1024)(128)(2,1)S(1)}, u32[]{:S(2)}) copy-start(bf16[768]{0:T(1024)(128)(2,1)S(1)} %dynamic-update-slice.7) | copy-start | bytes 4612
  983.3 3.9 copy-start.72
  983.3 24.9 %copy-start.21 = (f32[2,128,768]{2,1,0:T(8,128)S(1)}, f32[2,128,768]{2,1,0:T(8,128)}, u32[]{:S(2)}) copy-start(f32[2,128,768]{2,1,0:T(8,128)} %copy-done.20) | copy-start | bytes 2359300
  983.3 24.9 %copy-start.37 = (bf16[2,128,768]{2,1,0:T(8,128)(2,1)S(1)}, bf16[2,128,768]{2,1,0:T(8,128)(2,1)}, u32[]{:S(2)}) copy-start(bf16[2,128,768]{2,1,0:T(8,128)(2,1)} %param.37) | copy-start | bytes 1179652
  983.3 24.9 %copy-start.76 = (f32[2,128]{1,0:T(2,128)S(1)}, f32[2,128]{1,0:T(2,128)}, u32[]{:S(2)}) copy-start(f32[2,128]{1,0:T(2,128)} %copy-done.75) | copy-start | bytes 3076
  987.2 22.3 %copy-start.13 = (f32[2,128,768]{2,1,0:T(8,128)S(1)}, f32[2,128,768]{2,1,0:T(8,128)}, u32[]{:S(2)}) copy-start(f32[2,128,768]{2,1,0:T(8,128)} %copy-done.11) | copy-start | bytes 2359300
  1009.6 43.2 %copy-start.40 = (bf16[192,3072]{1,0:T(8,128)(2,1)S(1)}, bf16[192,3072]{1,0:T(8,128)(2,1)}, u32[]{:S(2)}) copy-start(bf16[192,3072]{1,0:T(8,128)(2,1)} %reduce-scatter.12.cloned.1.call-done) | copy-start | bytes 3538948
  1009.6 43.2 %copy-start.41 = (bf16[768,768]{1,0:T(8,128)(2,1)S(1)}, bf16[768,768]{1,0:T(8,128)(2,1)}, u32[]{:S(2)}) copy-start(bf16[768,768]{1,0:T(8,128)(2,1)} %reduce-scatter.14.cloned.1.call-done) | copy-start | bytes 3538948
  1009.6 43.2 %copy-start.57 = (bf16[192,768]{1,0:T(8,128)(2,1)S(1)}, bf16[192,768]{1,0:T(8,128)(2,1)}, u32[]{:S(2)}) copy-start(bf16[192,768]{1,0:T(8,128)(2,1)} %reduce-scatter.10.cloned.1.call-done) | copy-start | bytes 884740
  (59 other events, 108.0 us)
Sparse Core Ops, SparseCore 0:
  9.6 72.8 all-gather.6
  87.0 44.1 all-gather.8
  132.8 30.4 all-gather.10
  164.7 88.5 all-gather.12
  254.7 87.8 all-gather.14
  685.3 90.8 reduce-scatter.5
  779.0 29.1 reduce-scatter.9
  810.6 83.9 reduce-scatter.11
  896.9 85.7 reduce-scatter.13
  984.8 67.8 reduce-scatter.7
where the time goes:
time: 1210 us; the launch traced here: 1200 us
  waiting for transfers between devices  468 us (39%)
  local copies, waits for them, and re-layouts  227 us (19%)
  blocking collectives  199 us (16%)
  other arithmetic  160 us (13%)
  matrix products  114 us (9%)
  between operations  18.4 us (2%)
  loops' own time  17.6 us (1%)
    psum x1, blocking collectives, body(): owned = lax.psum(tuple(owned), 'ctx')  145 us
    add x2, other arithmetic, key_value_terms(): split_all[:, 0]  93.2 us
    reduce_scatter x1, waiting for transfers between devices, body(): lax.psum_scatter(grad_down.astype(jnp.bfloat16), 'wsh', scatter_dimension...  88.1 us
    reduce_scatter x1, waiting for transfers between devices, body(): lax.psum_scatter(grad_up.astype(jnp.bfloat16), 'wsh', scatter_dimension=0...  86.3 us
    all_gather x1, waiting for transfers between devices, body(): lax.all_gather(w_down, 'wsh', axis=0, tiled=True)  83.8 us
    all_gather x1, waiting for transfers between devices, body(): lax.all_gather(w_up, 'wsh', axis=0, tiled=True)  60.3 us
    concatenate x6, local copies, waits for them, and re-layouts, key_value_terms(): jnp.concatenate([dkey_all.reshape(stride, seq_count, model_width), dvalue...  46 us
    all_gather x1, waiting for transfers between devices, body(): lax.all_gather(w_qkv, 'wsh', axis=0, tiled=True)  42.4 us
  transfers between devices with their start and end apart: 10, of which 9 were waited for; matrix products, arithmetic and copies ran while one was open for 14% of the time, Pallas kernels for 0%

commit v1 on v0

v1 whole, which is shorter than its diff:
```python
import functools
import math

import jax
import jax.numpy as jnp
from jax import lax
from jax.experimental import pallas as pl
from jax.experimental.pallas import tpu as pltpu
from jax.sharding import PartitionSpec as P

HEADS = 12


EPSILON = 1e-05
MASKED = -1000000000.0
LOWEST = -1e30


def layer_norm(values, gain, shift):
    center = jnp.mean(values, axis=-1, keepdims=True)
    offset = values - center
    spread = jnp.mean(offset * offset, axis=-1, keepdims=True)
    return offset * lax.rsqrt(spread + EPSILON) * gain + shift


def gelu_tanh(values):
    return jax.nn.gelu(values, approximate=True)


def key_positions(row_index, pair_table, block_len):
    places = pair_table.shape[0]
    owner = row_index // (2 * block_len)
    inner = row_index % (2 * block_len)
    hits = owner[:, None] == jnp.arange(places, dtype=jnp.int32)[None, :]
    chosen = jnp.sum(jnp.where(hits, pair_table[None, :], 0), axis=1)
    which = jnp.where(inner < block_len, chosen, 2 * places - 1 - chosen)
    return which * block_len + inner % block_len


def lower_rows(array, block_len):
    seq_count, row_total, feature = array.shape
    paired = array.reshape(seq_count, row_total // (2 * block_len), 2, block_len, feature)
    return paired[:, :, 0].reshape(seq_count, row_total // 2, feature)


def lower_spots(spots, block_len):
    return spots.reshape(-1, 2, block_len)[:, 0].reshape(-1)


def online_step(state, query, query_pos, keys, values, key_pos, scale):
    accum, top_score, total = state
    scores = jnp.einsum("sqhd,skhd->shqk", query, keys, preferred_element_type=jnp.float32) * scale
    scores = jnp.where(
        key_pos[None, None, None, :] <= query_pos[None, None, :, None], scores, MASKED
    )
    new_top = jnp.maximum(top_score, jnp.max(scores, axis=-1))
    fading = jnp.exp(top_score - new_top)
    weights = jnp.exp(scores - new_top[..., None])
    total = total * fading + jnp.sum(weights, axis=-1)
    accum = accum * fading[..., None] + jnp.einsum(
        "shqk,skhd->shqd", weights.astype(jnp.bfloat16), values, preferred_element_type=jnp.float32
    )
    return (accum, new_top, total)


def scores_back(query, query_pos, log_total, delta, grad_head, keys, values, key_pos, scale):
    scores = jnp.einsum("sqhd,skhd->shqk", query, keys, preferred_element_type=jnp.float32) * scale
    scores = jnp.where(
        key_pos[None, None, None, :] <= query_pos[None, None, :, None], scores, MASKED
    )
    probs = jnp.exp(scores - log_total[..., None])
    grad_probs = jnp.einsum(
        "sqhd,skhd->shqk", grad_head, values, preferred_element_type=jnp.float32
    )
    grad_scores = (probs * (grad_probs - delta[..., None])).astype(jnp.bfloat16)
    return (probs.astype(jnp.bfloat16), grad_scores)


CHUNK = 256


def to_natural(order_ref, source_ref, target_ref, block_len):
    for block in range(source_ref.shape[0] // block_len):
        start = pl.multiple_of(order_ref[block] * block_len, block_len)
        target_ref[pl.ds(block * block_len, block_len), :] = source_ref[pl.ds(start, block_len), :]


def from_natural(order_ref, source_ref, target_ref, block_len):
    for block in range(source_ref.shape[0] // block_len):
        start = pl.multiple_of(order_ref[block] * block_len, block_len)
        target_ref[pl.ds(start, block_len), :] = source_ref[pl.ds(block * block_len, block_len), :]


def causal_scores(query, keys, first):
    scores = lax.dot_general(
        query, keys, (((1,), (1,)), ((), ())), preferred_element_type=jnp.float32
    )
    rows = lax.broadcasted_iota(jnp.int32, scores.shape, 0) + first
    columns = lax.broadcasted_iota(jnp.int32, scores.shape, 1)
    return jnp.where(columns <= rows, scores, MASKED)


def attend_kernel(head_size, block_len, order_ref, x_ref, out_ref, exact_ref, lse_ref, rows_ref, near_ref):
    total, width = x_ref.shape
    group = width // 3
    chunk = min(CHUNK, total)
    scale = head_size ** (-0.5)
    to_natural(order_ref, x_ref, rows_ref, block_len)
    for head in range(group // head_size):
        spot = head * head_size
        for first in range(0, total, chunk):
            last = first + chunk
            query = rows_ref[first:last, spot : spot + head_size] * jnp.bfloat16(scale)
            keys = rows_ref[:last, group + spot : group + spot + head_size]
            values = rows_ref[:last, 2 * group + spot : 2 * group + spot + head_size]
            scores = causal_scores(query, keys, first)
            top = jnp.max(scores, axis=1, keepdims=True)
            weights = jnp.exp(scores - top)
            amount = jnp.sum(weights, axis=1, keepdims=True)
            mixed = jnp.dot(
                weights.astype(jnp.bfloat16), values, preferred_element_type=jnp.float32
            ) * (1.0 / amount)
            exact_ref[first:last, spot : spot + head_size] = mixed
            near_ref[first:last, spot : spot + head_size] = mixed.astype(jnp.bfloat16)
            lse_ref[first:last, head : head + 1] = top + jnp.log(amount)
    from_natural(order_ref, near_ref, out_ref, block_len)


def attend_back_kernel(
    head_size, block_len, order_ref, x_ref, grad_ref, exact_ref, lse_ref, out_ref,
    rows_ref, near_ref, back_ref, key_ref, value_ref,
):
    total, width = x_ref.shape
    group = width // 3
    chunk = min(CHUNK, total)
    scale = head_size ** (-0.5)
    to_natural(order_ref, x_ref, rows_ref, block_len)
    to_natural(order_ref, grad_ref, near_ref, block_len)
    for head in range(group // head_size):
        spot = head * head_size
        for first in reversed(range(0, total, chunk)):
            last = first + chunk
            query = rows_ref[first:last, spot : spot + head_size] * jnp.bfloat16(scale)
            keys = rows_ref[:last, group + spot : group + spot + head_size]
            values = rows_ref[:last, 2 * group + spot : 2 * group + spot + head_size]
            grad = near_ref[first:last, spot : spot + head_size]
            exact = exact_ref[first:last, spot : spot + head_size]
            delta = jnp.sum(grad.astype(jnp.float32) * exact, axis=1, keepdims=True)
            scores = causal_scores(query, keys, first)
            probs = jnp.exp(scores - lse_ref[first:last, head : head + 1])
            grad_probs = lax.dot_general(
                grad, values, (((1,), (1,)), ((), ())), preferred_element_type=jnp.float32
            )
            grad_scores = (probs * (grad_probs - delta)).astype(jnp.bfloat16)
            grad_query = jnp.dot(grad_scores, keys, preferred_element_type=jnp.float32) * scale
            back_ref[first:last, spot : spot + head_size] = grad_query.astype(jnp.bfloat16)
            grad_keys = lax.dot_general(
                grad_scores, query, (((0,), (0,)), ((), ())), preferred_element_type=jnp.float32
            )
            grad_values = lax.dot_general(
                probs.astype(jnp.bfloat16), grad, (((0,), (0,)), ((), ())),
                preferred_element_type=jnp.float32,
            )
            if last == total:
                key_ref[...] = grad_keys
                value_ref[...] = grad_values
            else:
                key_ref[:last, :] += grad_keys
                value_ref[:last, :] += grad_values
        back_ref[:, group + spot : group + spot + head_size] = key_ref[...].astype(jnp.bfloat16)
        back_ref[:, 2 * group + spot : 2 * group + spot + head_size] = value_ref[...].astype(jnp.bfloat16)
    from_natural(order_ref, back_ref, out_ref, block_len)


def in_vmem():
    return pl.BlockSpec(memory_space=pltpu.VMEM)


def in_smem():
    return pl.BlockSpec(memory_space=pltpu.SMEM)


def attend(order, rows, head_size, block_len):
    total, width = rows.shape
    group = width // 3
    return pl.pallas_call(
        functools.partial(attend_kernel, head_size, block_len),
        out_shape=(
            jax.ShapeDtypeStruct((total, group), jnp.bfloat16),
            jax.ShapeDtypeStruct((total, group), jnp.float32),
            jax.ShapeDtypeStruct((total, 128), jnp.float32),
        ),
        in_specs=[in_smem(), in_vmem()],
        out_specs=(in_vmem(), in_vmem(), in_vmem()),
        scratch_shapes=[
            pltpu.VMEM((total, width), jnp.bfloat16),
            pltpu.VMEM((total, group), jnp.bfloat16),
        ],
        compiler_params=pltpu.CompilerParams(vmem_limit_bytes=40 * 1024 * 1024),
    )(order, rows)


def attend_back(order, rows, grad, exact, lse, head_size, block_len):
    total, width = rows.shape
    group = width // 3
    return pl.pallas_call(
        functools.partial(attend_back_kernel, head_size, block_len),
        out_shape=jax.ShapeDtypeStruct((total, width), jnp.bfloat16),
        in_specs=[in_smem(), in_vmem(), in_vmem(), in_vmem(), in_vmem()],
        out_specs=in_vmem(),
        scratch_shapes=[
            pltpu.VMEM((total, width), jnp.bfloat16),
            pltpu.VMEM((total, group), jnp.bfloat16),
            pltpu.VMEM((total, width), jnp.bfloat16),
            pltpu.VMEM((total, head_size), jnp.float32),
            pltpu.VMEM((total, head_size), jnp.float32),
        ],
        compiler_params=pltpu.CompilerParams(vmem_limit_bytes=48 * 1024 * 1024),
    )(order, rows, grad, exact, lse)


def spread_out(array, seq_count, groups, parts):
    row_count, width = array.shape[1], array.shape[2] // parts
    cut = array.reshape(seq_count, row_count, parts, groups, width // groups)
    cut = jnp.transpose(cut, (0, 3, 1, 2, 4))
    cut = cut.reshape(seq_count * groups, row_count, parts * (width // groups))
    moved = lax.all_to_all(cut, "ctx", 0, 0, tiled=True)
    return moved.reshape(seq_count * groups * row_count, parts * (width // groups))


def bring_back(array, seq_count, groups, parts):
    places = seq_count * groups
    row_count, width = array.shape[0] // places, array.shape[1] // parts
    moved = lax.all_to_all(array.reshape(places, row_count, parts * width), "ctx", 0, 0, tiled=True)
    cut = moved.reshape(seq_count, groups, row_count, parts, width)
    cut = jnp.transpose(cut, (0, 2, 3, 1, 4))
    return cut.reshape(seq_count, row_count, parts * groups * width)


def whole_weight(part):
    places = lax.axis_size("ctx")
    rows = part.shape[0]
    if rows % places:
        return lax.all_gather(part, "wsh", axis=0, tiled=True)
    share = rows // places
    own = lax.dynamic_slice_in_dim(part, lax.axis_index("ctx") * share, share, 0)
    return lax.all_gather(own, ("wsh", "ctx"), axis=0, tiled=True)


def owned_gradient(grad):
    places = lax.axis_size("ctx")
    near = grad.astype(jnp.bfloat16)
    if near.shape[0] % (places * lax.axis_size("wsh")):
        part = lax.psum_scatter(near, "wsh", scatter_dimension=0, tiled=True).astype(jnp.float32)
        return lax.psum(part, "ctx")
    part = lax.psum_scatter(near, ("wsh", "ctx"), scatter_dimension=0, tiled=True)
    return lax.all_gather(part, "ctx", axis=0, tiled=True).astype(jnp.float32)


def loop_attend(qkv, pair_of_device, block_len, qpos_low, qpos_up, scale):
    seq_count, row_count = qkv.shape[0], qkv.shape[1]
    model_width = qkv.shape[2] // 3
    head_count = HEADS
    head_size = model_width // head_count
    queries = qkv[..., :model_width].reshape(seq_count, row_count, head_count, head_size)
    query_low = queries[:, :block_len]
    query_up = queries[:, block_len:]
    kv_local = qkv[..., model_width:]

    def split_keys(slab_rows):
        keys = slab_rows[..., :model_width].reshape(seq_count, -1, head_count, head_size)
        values = slab_rows[..., model_width:].reshape(seq_count, -1, head_count, head_size)
        return (keys, values)

    empty_state = (
        jnp.zeros((seq_count, head_count, block_len, head_size), jnp.float32),
        jnp.full((seq_count, head_count, block_len), LOWEST, jnp.float32),
        jnp.zeros((seq_count, head_count, block_len), jnp.float32),
    )
    slab = lax.all_gather(kv_local, "ctx", axis=1, tiled=True)
    row_total = slab.shape[1]
    stride = math.gcd(row_total, max(row_count, 512))

    def turn(index, running):
        offset_row = index * stride
        sub_rows = lax.dynamic_slice_in_dim(slab, offset_row, stride, 1)
        key_pos = key_positions(
            offset_row + jnp.arange(stride, dtype=jnp.int32), pair_of_device, block_len
        )
        keys, values = split_keys(sub_rows)
        low_keys, low_values = split_keys(lower_rows(sub_rows, block_len))
        low_pos = lower_spots(key_pos, block_len)
        state_low = online_step(
            running[0], query_low, qpos_low, low_keys, low_values, low_pos, scale
        )
        state_up = online_step(running[1], query_up, qpos_up, keys, values, key_pos, scale)
        return (state_low, state_up)

    states = lax.fori_loop(0, row_total // stride, turn, (empty_state, empty_state))

    def finish(state):
        accum, top_score, total = state
        return (accum / total[..., None], top_score + jnp.log(total))

    attended_low, log_low = finish(states[0])
    attended_up, log_up = finish(states[1])
    attended = jnp.transpose(jnp.concatenate([attended_low, attended_up], axis=2), (0, 2, 1, 3))
    return attended, (query_low, query_up, kv_local, split_keys, log_low, log_up)


def loop_attend_back(kept, grad_heads, attended, pair_of_device, block_len, qpos_low, qpos_up, scale):
    query_low, query_up, kv_local, split_keys, log_low, log_up = kept
    seq_count, row_count, head_count, head_size = grad_heads.shape
    model_width = head_count * head_size
    grad_low = grad_heads[:, :block_len]
    grad_high = grad_heads[:, block_len:]
    delta = jnp.einsum("sqhd,sqhd->shq", grad_heads.astype(jnp.float32), attended)
    delta_low = delta[:, :, :block_len]
    delta_up = delta[:, :, block_len:]
    gathered = lax.all_gather(kv_local, "ctx", axis=1, tiled=True)
    total_rows = gathered.shape[1]

    def back_sub(sub_rows, first_row):
        stride = sub_rows.shape[1]
        key_pos = key_positions(
            first_row + jnp.arange(stride, dtype=jnp.int32), pair_of_device, block_len
        )
        keys, values = split_keys(sub_rows)
        low_keys, low_values = split_keys(lower_rows(sub_rows, block_len))
        low_pos = lower_spots(key_pos, block_len)
        probs_up, dscore_up = scores_back(
            query_up, qpos_up, log_up, delta_up, grad_high, keys, values, key_pos, scale
        )
        probs_low, dscore_low = scores_back(
            query_low, qpos_low, log_low, delta_low, grad_low, low_keys, low_values, low_pos, scale
        )
        return (keys, low_keys, probs_up, dscore_up, probs_low, dscore_low)

    def query_terms(parts):
        keys, low_keys, probs_up, dscore_up, probs_low, dscore_low = parts
        term_low = (
            jnp.einsum("shqk,skhd->sqhd", dscore_low, low_keys, preferred_element_type=jnp.float32)
            * scale
        )
        term_up = (
            jnp.einsum("shqk,skhd->sqhd", dscore_up, keys, preferred_element_type=jnp.float32)
            * scale
        )
        return (term_low, term_up)

    def key_value_terms(parts):
        keys, low_keys, probs_up, dscore_up, probs_low, dscore_low = parts
        stride = keys.shape[1]
        dkey_all = (
            jnp.einsum("shqk,sqhd->kshd", dscore_up, query_up, preferred_element_type=jnp.float32)
            * scale
        )
        dvalue_all = jnp.einsum(
            "shqk,sqhd->kshd", probs_up, grad_high, preferred_element_type=jnp.float32
        )
        dkey_low = (
            jnp.einsum("shqk,sqhd->kshd", dscore_low, query_low, preferred_element_type=jnp.float32)
            * scale
        )
        dvalue_low = jnp.einsum(
            "shqk,sqhd->kshd", probs_low, grad_low, preferred_element_type=jnp.float32
        )
        both_all = jnp.concatenate(
            [
                dkey_all.reshape(stride, seq_count, model_width),
                dvalue_all.reshape(stride, seq_count, model_width),
            ],
            axis=-1,
        )
        both_low = jnp.concatenate(
            [
                dkey_low.reshape(stride // 2, seq_count, model_width),
                dvalue_low.reshape(stride // 2, seq_count, model_width),
            ],
            axis=-1,
        )
        split_all = both_all.reshape(stride // row_count, 2, block_len, seq_count, 2 * model_width)
        merged = jnp.stack(
            [
                split_all[:, 0]
                + both_low.reshape(stride // row_count, block_len, seq_count, 2 * model_width),
                split_all[:, 1],
            ],
            axis=1,
        )
        return merged.reshape(stride, seq_count, 2 * model_width)

    zero_query = jnp.zeros((seq_count, block_len, head_count, head_size), jnp.float32)
    full_stride = math.gcd(total_rows, max(row_count, 512))

    def query_turn(index, running):
        first_row = index * full_stride
        sub_rows = lax.dynamic_slice_in_dim(gathered, first_row, full_stride, 1)
        term_low, term_up = query_terms(back_sub(sub_rows, first_row))
        return (running[0] + term_low, running[1] + term_up)

    dquery_low, dquery_up = lax.fori_loop(
        0, total_rows // full_stride, query_turn, (zero_query, zero_query)
    )
    row_total = row_count * lax.axis_size("ctx")
    key_stride = math.gcd(row_total, max(row_count, 512))

    def rows_turn(running, index):
        offset_row = index * key_stride
        sub_rows = lax.dynamic_slice_in_dim(gathered, offset_row, key_stride, 1)
        return (running, key_value_terms(back_sub(sub_rows, offset_row)))

    ignored, pieces = lax.scan(
        rows_turn, None, jnp.arange(row_total // key_stride, dtype=jnp.int32)
    )
    summed = lax.psum_scatter(
        pieces.reshape(row_total, seq_count, 2 * model_width),
        "ctx",
        scatter_dimension=0,
        tiled=True,
    )
    grad_kv = jnp.transpose(summed, (1, 0, 2)).astype(jnp.bfloat16)
    grad_query = (
        jnp.concatenate([dquery_low, dquery_up], axis=1)
        .reshape(seq_count, row_count, model_width)
        .astype(jnp.bfloat16)
    )
    return jnp.concatenate([grad_query, grad_kv], axis=-1)


def body(
    block_input,
    ln1_gain,
    ln1_bias,
    w_qkv,
    bias_query,
    bias_value,
    w_out,
    bias_out,
    ln2_gain,
    ln2_bias,
    w_up,
    bias_up,
    w_down,
    bias_down,
    pair_of_device,
    cotangent,
):
    small = (
        ln1_gain, ln1_bias, bias_query, bias_value, bias_out, ln2_gain, ln2_bias, bias_down, bias_up,
    )
    packed = lax.all_gather(jnp.concatenate(small).reshape(1, -1), "wsh", axis=0, tiled=True)
    packed = packed.astype(jnp.float32)
    whole_small = []
    start = 0
    for one in small:
        whole_small.append(packed[:, start : start + one.shape[0]].reshape(-1))
        start += one.shape[0]
    (
        gain_first,
        shift_first,
        query_shift,
        value_shift,
        out_shift,
        gain_second,
        shift_second,
        down_shift,
        up_shift,
    ) = whole_small
    whole_qkv = whole_weight(w_qkv)
    whole_out = whole_weight(w_out)
    whole_up = whole_weight(w_up)
    whole_down = whole_weight(w_down)
    seq_count, row_count, model_width = block_input.shape
    block_len = row_count // 2
    head_count = HEADS
    head_size = model_width // head_count
    scale = head_size ** (-0.5)
    places = lax.axis_size("ctx")
    own_index = lax.axis_index("ctx")
    own_pair = jnp.sum(
        jnp.where(jnp.arange(places, dtype=jnp.int32) == own_index, pair_of_device, 0)
    )
    offsets = jnp.arange(block_len, dtype=jnp.int32)
    qpos_low = own_pair * block_len + offsets
    qpos_up = (2 * places - 1 - own_pair) * block_len + offsets
    by_heads = places % seq_count == 0 and head_count % (places // seq_count) == 0
    inputs_f = block_input.astype(jnp.float32)
    normed_f, ln_one_back = jax.vjp(layer_norm, inputs_f, gain_first, shift_first)
    normed = normed_f.astype(jnp.bfloat16)
    qkv_shift = jnp.concatenate([query_shift, jnp.zeros_like(query_shift), value_shift])
    qkv = (jnp.dot(normed, whole_qkv, preferred_element_type=jnp.float32) + qkv_shift).astype(
        jnp.bfloat16
    )
    if by_heads:
        groups = places // seq_count
        blocks = jnp.arange(2 * places, dtype=jnp.int32)
        sought = jnp.minimum(blocks, 2 * places - 1 - blocks)
        hits = pair_of_device[None, :] == sought[:, None]
        holder = jnp.sum(jnp.where(hits, jnp.arange(places, dtype=jnp.int32)[None, :], 0), axis=1)
        order = 2 * holder + (blocks >= places).astype(jnp.int32)
        head_rows = spread_out(qkv, seq_count, groups, 3)
        mixed, exact, lse = attend(order, head_rows, head_size, block_len)
        attended_bf = bring_back(mixed, seq_count, groups, 1)
    else:
        attended, kept = loop_attend(
            qkv, pair_of_device, block_len, qpos_low, qpos_up, scale
        )
        attended_bf = attended.reshape(seq_count, row_count, model_width).astype(jnp.bfloat16)
    middle = (
        inputs_f + jnp.dot(attended_bf, whole_out, preferred_element_type=jnp.float32) + out_shift
    )
    normed_two_f, ln_two_back = jax.vjp(layer_norm, middle, gain_second, shift_second)
    normed_two = normed_two_f.astype(jnp.bfloat16)
    hidden = jnp.dot(normed_two, whole_up, preferred_element_type=jnp.float32) + up_shift
    active_f, gelu_back = jax.vjp(gelu_tanh, hidden)
    active = active_f.astype(jnp.bfloat16)
    output = (
        middle + jnp.dot(active, whole_down, preferred_element_type=jnp.float32) + down_shift
    ).astype(jnp.bfloat16)
    cotangent_f = cotangent.astype(jnp.float32)
    grad_down = jnp.einsum("srf,srd->fd", active, cotangent, preferred_element_type=jnp.float32)
    grad_bias_down = jnp.sum(cotangent_f, axis=(0, 1))
    grad_active = jnp.einsum(
        "srd,fd->srf", cotangent, whole_down, preferred_element_type=jnp.float32
    )
    grad_hidden = gelu_back(grad_active)[0].astype(jnp.bfloat16)
    grad_up = jnp.einsum("srd,srf->df", normed_two, grad_hidden, preferred_element_type=jnp.float32)
    grad_bias_up = jnp.sum(grad_hidden.astype(jnp.float32), axis=(0, 1))
    grad_normed_two = jnp.einsum(
        "srf,df->srd", grad_hidden, whole_up, preferred_element_type=jnp.float32
    )
    grad_middle_part, grad_ln2_gain, grad_ln2_bias = ln_two_back(grad_normed_two)
    grad_middle = cotangent_f + grad_middle_part
    grad_branch = grad_middle.astype(jnp.bfloat16)
    grad_out = jnp.einsum(
        "sri,sro->io", attended_bf, grad_branch, preferred_element_type=jnp.float32
    )
    grad_bias_out = jnp.sum(grad_branch.astype(jnp.float32), axis=(0, 1))
    grad_attended = jnp.einsum(
        "sro,io->sri", grad_branch, whole_out, preferred_element_type=jnp.float32
    ).astype(jnp.bfloat16)
    if by_heads:
        grad_back = spread_out(grad_attended, seq_count, groups, 1)
        grad_head_rows = attend_back(order, head_rows, grad_back, exact, lse, head_size, block_len)
        grad_rows = bring_back(grad_head_rows, seq_count, groups, 3)
    else:
        grad_rows = loop_attend_back(
            kept,
            grad_attended.reshape(seq_count, row_count, head_count, head_size),
            attended, pair_of_device, block_len, qpos_low, qpos_up, scale,
        )
    grad_qkv = jnp.einsum("srd,sre->de", normed, grad_rows, preferred_element_type=jnp.float32)
    row_sums = jnp.sum(grad_rows.astype(jnp.float32), axis=(0, 1))
    grad_bias_query = row_sums[:model_width]
    grad_bias_value = row_sums[2 * model_width :]
    grad_normed = jnp.einsum(
        "sre,de->srd", grad_rows, whole_qkv, preferred_element_type=jnp.float32
    )
    grad_input_part, grad_ln1_gain, grad_ln1_bias = ln_one_back(grad_normed)
    grad_input = grad_middle + grad_input_part
    vectors = (
        grad_ln1_gain, grad_ln1_bias, grad_bias_query, grad_bias_value, grad_bias_out,
        grad_ln2_gain, grad_ln2_bias, grad_bias_down, grad_bias_up,
    )
    shards = lax.axis_size("wsh")
    stacked = jnp.concatenate([one.reshape(shards, -1) for one in vectors], axis=1)
    summed = lax.psum(stacked, ("wsh", "ctx"))
    mine = lax.dynamic_slice_in_dim(summed, lax.axis_index("wsh"), 1, 0)[0]
    own = []
    start = 0
    for one in vectors:
        size = one.shape[0] // shards
        own.append(mine[start : start + size])
        start += size
    (
        own_ln1_gain, own_ln1_bias, own_bias_query, own_bias_value, own_bias_out,
        own_ln2_gain, own_ln2_bias, own_bias_down, own_bias_up,
    ) = own
    return (
        output,
        grad_input,
        own_ln1_gain,
        own_ln1_bias,
        owned_gradient(grad_qkv),
        own_bias_query,
        own_bias_value,
        owned_gradient(grad_out),
        own_bias_out,
        own_ln2_gain,
        own_ln2_bias,
        owned_gradient(grad_up),
        own_bias_up,
        owned_gradient(grad_down),
        own_bias_down,
    )


def solution(mesh):
    in_specs = (
        P("wsh", "ctx", None),
        P("wsh"),
        P("wsh"),
        P("wsh", None),
        P("wsh"),
        P("wsh"),
        P("wsh", None),
        P("wsh"),
        P("wsh"),
        P("wsh"),
        P("wsh", None),
        P("wsh"),
        P("wsh", None),
        P("wsh"),
        P(),
        P("wsh", "ctx", None),
    )
    out_specs = (
        P("wsh", "ctx", None),
        P("wsh", "ctx", None),
        P("wsh"),
        P("wsh"),
        P("wsh", None),
        P("wsh"),
        P("wsh"),
        P("wsh", None),
        P("wsh"),
        P("wsh"),
        P("wsh"),
        P("wsh", None),
        P("wsh"),
        P("wsh", None),
        P("wsh"),
    )
    return jax.shard_map(body, mesh=mesh, in_specs=in_specs, out_specs=out_specs, check_vma=False)
```

time: 1210 us -> 781 us (0.65)
  local copies, waits for them, and re-layouts: 227 us -> 35.5 us
  other arithmetic: 160 us -> 15.3 us
  blocking collectives: 199 us -> 104 us
  matrix products: 114 us -> 49.2 us
  waiting for transfers between devices: 468 us -> 527 us
  loops' own time: 17.6 us -> 0 us
  Pallas kernels: 0 us -> 14.6 us
    psum x1, blocking collectives: 145 us -> 40.4 us  [body(): summed = lax.psum(stacked, ('wsh', 'ctx'))]
    add x26 -> x1, other arithmetic: 102 us -> 0.01 us  [body(): order = 2 * holder + (blocks >= places).astype(jnp.int32)]
    dot_general x28 -> x0, matrix products: 69.8 us -> none  [the longest x8 12.2 us: scores_back(): jnp.einsum('sqhd,skhd->shqk', query, keys, preferred_element_type=jnp.flo...]
    concatenate x10 -> x2, local copies, waits for them, and re-layouts: 59.2 us -> 6.21 us  [the longest x1 6.11 us: body(): jnp.concatenate(small).reshape(1, -1)]
    slice x44 -> x5, local copies, waits for them, and re-layouts: 53.6 us -> 2.03 us  [the longest x2 1.35 us: body(): own.append(mine[start:start + size])]
    unnamed x2 -> x0, blocking collectives: 41.2 us -> none
    while x120 -> x0, local copies, waits for them, and re-layouts: 35.5 us -> none
    another operation x2 -> x0, local copies, waits for them, and re-layouts: 35.4 us -> none  [key_value_terms(): jnp.stack([split_all[:, 0] + both_low.reshape(stride // row_count, block_...]
  transfers between devices with their start and end apart: 10 -> 13, of which waited for: 9 -> 12; matrix products, arithmetic and copies ran while one was open for 14% -> 10% of each run, Pallas kernels for 0% -> 2%
where the time goes in v1:
time: 781 us; the launch traced here: 773 us
  waiting for transfers between devices  527 us (67%)
  blocking collectives  104 us (13%)
  matrix products  49.2 us (6%)
  local copies, waits for them, and re-layouts  35.5 us (5%)
  other arithmetic  15.3 us (2%)
  between operations  15.1 us (2%)
  Pallas kernels  14.6 us (2%)
  starting transfers between devices  12.2 us (2%)
    reduce_scatter x4, waiting for transfers between devices, owned_gradient(): lax.psum_scatter(near, ('wsh', 'ctx'), scatter_dimension=0, tiled=True)  290 us
    all_gather x4, waiting for transfers between devices, whole_weight(): return lax.all_gather(own, ('wsh', 'ctx'), axis=0, tiled=True)  178 us
    psum x1, blocking collectives, body(): summed = lax.psum(stacked, ('wsh', 'ctx'))  40.4 us
    all_gather x2, waiting for transfers between devices, owned_gradient(): return lax.all_gather(part, 'ctx', axis=0, tiled=True).astype(jnp.float32)  35.8 us
    all_to_all x1, blocking collectives, bring_back(): lax.all_to_all(array.reshape(places, row_count, parts * width), 'ctx', 0,...  28.7 us
    all_to_all x2, waiting for transfers between devices, spread_out(): moved = lax.all_to_all(cut, 'ctx', 0, 0, tiled=True)  23.4 us
    all_gather x2, blocking collectives, owned_gradient(): return lax.all_gather(part, 'ctx', axis=0, tiled=True).astype(jnp.float32)  20.2 us
  transfers between devices with their start and end apart: 13, of which 12 were waited for; matrix products, arithmetic and copies ran while one was open for 10% of the time, Pallas kernels for 2%

profile of v1, /device:TPU:0, one launch (start us, length us, event | category | flops | bytes accessed | tf_op | source)
XLA Modules:
  0.0 773.3 jit_solution(855821903254743746)
XLA Ops:
  7.2 1.6 constant_dynamic-slice_fusion.4
  9.0 1.4 constant_dynamic-slice_fusion.3
  11.2 1.6 constant_dynamic-slice_fusion.1
  12.8 6.1 concatenate.9
  18.9 14.8 %all-gather.1 = bf16[4,1,2304]{2,1,0:T(2,128)(2,1)S(1)} all-gather(bf16[1,1,2304]{2,1,0:T(2,128)(2,1)S(1)} %reshape.219), channel_id=2, replica_groups=mesh['ctx'=8,'wsh'=4] {'wsh'}, dimensions={0}, use_global_device_ids=true | all-gather | bytes 23040 | tf_op jit(solution)/shard_map/all_gather | solution.py:452
  34.8 1.1 convert_reduce_fusion.2
  35.9 1.2 fusion.48
  37.2 37.2 %all-gather.9.cloned.1.call-done = bf16[768,2304]{1,0:T(8,128)(2,1)} async-done(((bf16[24,2304]{1,0:T(8,128)(2,1)}), bf16[768,2304]{1,0:T(8,128)(2,1)}) %all-gather.9.cloned.1.call-update) | async-done | bytes 3538960 | tf_op jit(solution)/shard_map/all_gather | solution.py:247
  74.4 3.3 fusion.14
  77.8 0.7 copy.67
  78.5 1.1 copy.68
  79.6 3.6 all-to-all-start
  83.3 16.9 %all-to-all-done = bf16[8,128,576]{1,2,0:T(8,128)(2,1)S(1)} async-done(((bf16[8,128,576]{1,2,0:T(8,128)(2,1)}), bf16[8,128,576]{1,2,0:T(8,128)(2,1)S(1)}, u32[]{:S(2)}, u32[]{:S(2)}) %all-to-all-start) | async-done | bytes 1179680 | tf_op jit(solution)/shard_map/all_to_all | solution.py:227
  100.2 0.7 copy.69
  100.9 5.9 shard_map.271
  106.8 1.0 copy-done.2
  107.7 0.8 copy-done.4
  108.5 1.0 copy.70
  109.5 3.5 all-to-all-start.1
  113.4 17.8 %all-gather.11.cloned.1.call-done = bf16[768,768]{1,0:T(8,128)(2,1)} async-done(((bf16[24,768]{1,0:T(8,128)(2,1)}), bf16[768,768]{1,0:T(8,128)(2,1)}) %all-gather.11.cloned.1.call-update) | async-done | bytes 1179664 | tf_op jit(solution)/shard_map/all_gather | solution.py:247
  131.2 2.0 fusion.63
  133.5 62.9 %all-gather.13.cloned.1.call-done = bf16[768,3072]{1,0:T(8,128)(2,1)} async-done(((bf16[24,3072]{1,0:T(8,128)(2,1)}), bf16[768,3072]{1,0:T(8,128)(2,1)}) %all-gather.13.cloned.1.call-update) | async-done | bytes 4718608 | tf_op jit(solution)/shard_map/all_gather | solution.py:247
  196.4 5.5 fusion.11
  201.9 59.7 %all-gather.15.cloned.1.call-done = bf16[3072,768]{1,0:T(8,128)(2,1)} async-done(((bf16[96,768]{1,0:T(8,128)(2,1)}), bf16[3072,768]{1,0:T(8,128)(2,1)}) %all-gather.15.cloned.1.call-update) | async-done | bytes 4718608 | tf_op jit(solution)/shard_map/all_gather | solution.py:247
  261.6 7.4 convert_reduce_fusion
  269.0 1.1 copy-done.17
  270.1 3.8 bitcast_convert_fusion.1
  274.0 6.3 bitcast_convert_fusion
  280.3 5.2 multiply_reduce_fusion
  286.0 0.8 convert_reduce_fusion.4
  286.9 1.3 convolution_convert_fusion
  288.1 1.9 copy.72
  290.1 4.1 all-to-all-start.2
  294.2 1.5 bitcast_convert_fusion.3
  296.0 6.5 all-to-all-done.2
  302.5 1.2 copy.73
  303.7 1.2 copy-done.3
  305.0 1.0 copy-done.5
  306.0 8.7 %shard_map.272 = bf16[1024,576]{1,0:T(8,128)(2,1)S(1)} custom-call(s32[16]{0:T(128)S(1)} %fusion.56.order_ref, bf16[1024,576]{1,0:T(8,128)(2,1)S(1)} %bitcast.100, bf16[1024,192]{1,0:T(8,128)(2,1)S(1)} %bitcast.102, f32[1024,192]{1,0:T(8,128)S(1)} %copy-done.3, f32[1024,128]{1,0:T(8,128)S(1)} %copy-done.5), custom_call_target="tpu_custom_call" | custom-call | tf_op jit(solution)/shard_map/pallas_call | solution.py:206
  314.8 1.4 copy.74
  316.2 28.7 %all_to_all.20 = bf16[8,128,576]{1,2,0:T(8,128)(2,1)S(1)} all-to-all(bf16[8,128,576]{1,2,0:T(8,128)(2,1)} %copy.74), channel_id=1, replica_groups=mesh['ctx'=8,'wsh'=4] {'ctx'}, dimensions={0} | all-to-all | bytes 2359296 | tf_op jit(solution)/shard_map/all_to_all | solution.py:234
  345.0 3.1 bitcast_convert_fusion.2
  348.1 43.6 %reduce-scatter.9.cloned.1.call-done = bf16[24,3072]{1,0:T(8,128)(2,1)} async-done(((bf16[768,3072]{1,0:T(8,128)(2,1)}), bf16[24,3072]{1,0:T(8,128)(2,1)}) %reduce-scatter.9.cloned.1.call-update) | async-done | bytes 147472 | tf_op jit(solution)/shard_map/reduce_scatter | solution.py:256
  392.1 1.4 add.144
  394.1 1.3 reshape.213
  395.5 1.3 reshape.214
  396.8 1.3 reshape.216
  398.1 6.0 fusion.34
  404.1 100.0 %reduce-scatter.11.cloned.1.call-done = bf16[96,768]{1,0:T(8,128)(2,1)} async-done(((bf16[3072,768]{1,0:T(8,128)(2,1)}), bf16[96,768]{1,0:T(8,128)(2,1)}) %reduce-scatter.11.cloned.1.call-update) | async-done | bytes 147472 | tf_op jit(solution)/shard_map/reduce_scatter | solution.py:256
  504.2 3.9 fusion.57
  508.1 0.8 copy-done.14
  509.5 0.8 reshape.211
  510.3 2.5 convert_reduce_fusion.3
  513.5 40.4 %psum.7 = f32[4,2304]{1,0:T(4,128)S(1)} all-reduce(f32[4,2304]{1,0:T(4,128)S(1)} %concatenate.11), channel_id=1, replica_groups=mesh['ctx'=8,'wsh'=4] {'wsh','ctx'}, use_global_device_ids=true, to_apply=%region_17.18 | all-reduce | flops 9216 | bytes 73728 | tf_op jit(solution)/shard_map/psum | solution.py:568
  555.3 49.9 %reduce-scatter.7.cloned.1.call-done = bf16[24,768]{1,0:T(8,128)(2,1)} async-done(((bf16[768,768]{1,0:T(8,128)(2,1)}), bf16[24,768]{1,0:T(8,128)(2,1)}) %reduce-scatter.7.cloned.1.call-update) | async-done | bytes 36880 | tf_op jit(solution)/shard_map/reduce_scatter | solution.py:256
  605.1 9.5 %all_gather.33 = bf16[192,768]{1,0:T(8,128)(2,1)S(1)} all-gather(bf16[24,768]{1,0:T(8,128)(2,1)} %reduce-scatter.7.cloned.1.call-done), channel_id=1, replica_groups=mesh['ctx'=8,'wsh'=4] {'ctx'}, dimensions={0}, use_global_device_ids=true | all-gather | bytes 331776 | tf_op jit(solution)/shard_map/all_gather | solution.py:257
  614.6 0.9 convert_element_type.88
  615.5 96.9 %reduce-scatter.5.cloned.1.call-done = bf16[24,2304]{1,0:T(8,128)(2,1)} async-done(((bf16[768,2304]{1,0:T(8,128)(2,1)}), bf16[24,2304]{1,0:T(8,128)(2,1)}) %reduce-scatter.5.cloned.1.call-update) | async-done | bytes 110608 | tf_op jit(solution)/shard_map/reduce_scatter | solution.py:256
  712.4 10.7 %all_gather.32 = bf16[192,2304]{1,0:T(8,128)(2,1)S(1)} all-gather(bf16[24,2304]{1,0:T(8,128)(2,1)} %reduce-scatter.5.cloned.1.call-done), channel_id=1, replica_groups=mesh['ctx'=8,'wsh'=4] {'ctx'}, dimensions={0}, use_global_device_ids=true | all-gather | bytes 995328 | tf_op jit(solution)/shard_map/all_gather | solution.py:257
  723.1 1.3 convert_element_type.86
  724.5 12.9 %all-gather.17.cloned.1.call-done = bf16[192,3072]{1,0:T(8,128)(2,1)} async-done(((bf16[24,3072]{1,0:T(8,128)(2,1)}), bf16[192,3072]{1,0:T(8,128)(2,1)}) %all-gather.17.cloned.1.call-update) | async-done | bytes 1179664 | tf_op jit(solution)/shard_map/all_gather | solution.py:257
  737.4 2.9 convert_element_type.90
  740.3 22.9 %all-gather.19.cloned.1.call-done = bf16[768,768]{1,0:T(8,128)(2,1)} async-done(((bf16[96,768]{1,0:T(8,128)(2,1)}), bf16[768,768]{1,0:T(8,128)(2,1)}) %all-gather.19.cloned.1.call-update) | async-done | bytes 1179664 | tf_op jit(solution)/shard_map/all_gather | solution.py:257
  763.2 2.8 convert_element_type.92
  (112 shorter events, 7.5 us)
Async XLA Ops:
  7.2 3.3 copy-start
  7.2 67.2 %all-gather.9.cloned.1.call-start = ((), (), s32[]{:S(2)}) async-start(), calls=%async_computation.8 | async-start | bytes 3649536 | tf_op jit(solution)/shard_map/all_gather | solution.py:247
  8.9 122.3 %all-gather.11.cloned.1.call-start = ((), (), s32[]{:S(2)}) async-start(), calls=%async_computation.9 | async-start | bytes 1216512 | tf_op jit(solution)/shard_map/all_gather | solution.py:247
  10.4 186.0 %all-gather.13.cloned.1.call-start = ((), (), s32[]{:S(2)}) async-start(), calls=%async_computation.10 | async-start | bytes 4866048 | tf_op jit(solution)/shard_map/all_gather | solution.py:247
  11.2 250.4 %all-gather.15.cloned.1.call-start = ((), (), s32[]{:S(2)}) async-start(), calls=%async_computation.11 | async-start | bytes 4866048 | tf_op jit(solution)/shard_map/all_gather | solution.py:247
  37.1 40.6 %copy-start.25 = (f32[2,128]{1,0:T(2,128)}, f32[2,128]{1,0:T(2,128)S(1)}, u32[]{:S(2)}) copy-start(f32[2,128]{1,0:T(2,128)S(1)} %fusion.48) | copy-start | bytes 3076
  37.2 40.6 %copy-start.19 = (f32[2,128]{1,0:T(2,128)}, f32[2,128]{1,0:T(2,128)S(1)}, u32[]{:S(2)}) copy-start(f32[2,128]{1,0:T(2,128)S(1)} %fusion.54) | copy-start | bytes 3076
  77.7 5.5 copy-start.28
  79.6 20.6 %all-to-all-start = ((bf16[8,128,576]{1,2,0:T(8,128)(2,1)}), bf16[8,128,576]{1,2,0:T(8,128)(2,1)S(1)}, u32[]{:S(2)}, u32[]{:S(2)}) async-start(bf16[8,128,576]{1,2,0:T(8,128)(2,1)} %bitcast.3), calls=%async_computation | async-start | bytes 2359296 | tf_op jit(solution)/shard_map/all_to_all | solution.py:227
  83.2 48.0 %copy-start.8 = (bf16[2,128,768]{2,1,0:T(8,128)(2,1)S(1)}, bf16[2,128,768]{2,1,0:T(8,128)(2,1)}, u32[]{:S(2)}) copy-start(bf16[2,128,768]{2,1,0:T(8,128)(2,1)} %param.16) | copy-start | bytes 1179652
  106.8 1.0 copy-start.2
  107.7 0.8 copy-start.4
  109.5 21.7 %all-to-all-start.1 = ((bf16[8,128,192]{1,2,0:T(8,128)(2,1)}), bf16[8,128,192]{1,2,0:T(8,128)(2,1)S(1)}, u32[]{:S(2)}, u32[]{:S(2)}) async-start(bf16[8,128,192]{1,2,0:T(8,128)(2,1)} %copy.70), calls=%async_computation.1 | async-start | bytes 786432 | tf_op jit(solution)/shard_map/all_to_all | solution.py:234
  113.0 278.8 %reduce-scatter.9.cloned.1.call-start = ((), (), s32[]{:S(2)}) async-start(), calls=%async_computation.14 | async-start | bytes 4866048 | tf_op jit(solution)/shard_map/reduce_scatter | solution.py:256
  131.2 70.7 %copy-start.12 = (bf16[8,128,192]{1,2,0:T(8,128)(2,1)}, bf16[8,128,192]{1,2,0:T(8,128)(2,1)S(1)}, u32[]{:S(2)}) copy-start(bf16[8,128,192]{1,2,0:T(8,128)(2,1)S(1)} %all-to-all-done.1) | copy-start | bytes 1179652
  133.2 152.3 %copy-start.6 = (f32[2,128,768]{2,1,0:T(8,128)}, f32[2,128,768]{2,1,0:T(8,128)S(1)}, u32[]{:S(2)}) copy-start(f32[2,128,768]{2,1,0:T(8,128)S(1)} %get-tuple-element.53) | copy-start | bytes 2359300
  133.5 128.1 %copy-start.15 = (bf16[2,128,768]{2,1,0:T(8,128)(2,1)S(1)}, bf16[2,128,768]{2,1,0:T(8,128)(2,1)}, u32[]{:S(2)}) copy-start(bf16[2,128,768]{2,1,0:T(8,128)(2,1)} %param.31) | copy-start | bytes 1179652
  269.0 1.1 copy-start.17
  273.9 230.2 %reduce-scatter.11.cloned.1.call-start = ((), (), s32[]{:S(2)}) async-start(), calls=%async_computation.16 | async-start | bytes 4866048 | tf_op jit(solution)/shard_map/reduce_scatter | solution.py:256
  280.3 5.6 copy-start.16
  285.5 1.4 copy-start.11
  285.9 9.8 %copy-start.9 = (f32[2,128,768]{2,1,0:T(8,128)}, f32[2,128,768]{2,1,0:T(8,128)S(1)}, u32[]{:S(2)}) copy-start(f32[2,128,768]{2,1,0:T(8,128)S(1)} %get-tuple-element.31) | copy-start | bytes 2359300
  285.9 8.3 %copy-start.13 = (bf16[8,128,192]{1,2,0:T(8,128)(2,1)S(1)}, bf16[8,128,192]{1,2,0:T(8,128)(2,1)}, u32[]{:S(2)}) copy-start(bf16[8,128,192]{1,2,0:T(8,128)(2,1)} %copy-done.12) | copy-start | bytes 1179652
  285.9 9.8 %copy-start.27 = (f32[2,128]{1,0:T(2,128)}, f32[2,128]{1,0:T(2,128)S(1)}, u32[]{:S(2)}) copy-start(f32[2,128]{1,0:T(2,128)S(1)} %negate_multiply_fusion.1) | copy-start | bytes 3076
  290.1 12.5 %all-to-all-start.2 = ((bf16[8,128,192]{1,2,0:T(8,128)(2,1)}), bf16[8,128,192]{1,2,0:T(8,128)(2,1)}, u32[]{:S(2)}, u32[]{:S(2)}) async-start(bf16[8,128,192]{1,2,0:T(8,128)(2,1)} %bitcast.111), calls=%async_computation.2 | async-start | bytes 786432 | tf_op jit(solution)/shard_map/all_to_all | solution.py:227
  294.2 311.0 %reduce-scatter.7.cloned.1.call-start = ((), (), s32[]{:S(2)}) async-start(), calls=%async_computation.13 | async-start | bytes 1216512 | tf_op jit(solution)/shard_map/reduce_scatter | solution.py:256
  295.7 416.6 %reduce-scatter.5.cloned.1.call-start = ((), (), s32[]{:S(2)}) async-start(), calls=%async_computation.12 | async-start | bytes 3649536 | tf_op jit(solution)/shard_map/reduce_scatter | solution.py:256
  303.7 1.3 copy-start.3
  305.0 1.1 copy-start.5
  314.8 30.2 %copy-start.20 = (f32[2,128]{1,0:T(2,128)S(1)}, f32[2,128]{1,0:T(2,128)}, u32[]{:S(2)}) copy-start(f32[2,128]{1,0:T(2,128)} %copy-done.19) | copy-start | bytes 3076
  348.1 45.4 %copy-start.21 = (f32[768]{0:T(1024)S(1)}, f32[768]{0:T(1024)}, u32[]{:S(2)}) copy-start(f32[768]{0:T(1024)} %get-tuple-element.28) | copy-start | bytes 9220
  348.1 50.1 %copy-start.7 = (f32[2,128,768]{2,1,0:T(8,128)S(1)}, f32[2,128,768]{2,1,0:T(8,128)}, u32[]{:S(2)}) copy-start(f32[2,128,768]{2,1,0:T(8,128)} %copy-done.6) | copy-start | bytes 2359300
  348.1 389.3 %all-gather.17.cloned.1.call-start = ((), (), s32[]{:S(2)}) async-start(), calls=%async_computation.15 | async-start | bytes 1327104 | tf_op jit(solution)/shard_map/all_gather | solution.py:257
  391.8 371.4 %all-gather.19.cloned.1.call-start = ((), (), s32[]{:S(2)}) async-start(), calls=%async_computation.17 | async-start | bytes 1327104 | tf_op jit(solution)/shard_map/all_gather | solution.py:257
  504.1 3.9 copy-start.26
  504.2 6.1 copy-start.10
  508.1 0.9 copy-start.14
  508.1 5.3 copy-start.18
  508.1 5.3 copy-start.22
  508.1 5.3 copy-start.23
  508.1 5.3 copy-start.24
  723.1 42.9 %copy-start.1 = (bf16[192,3072]{1,0:T(8,128)(2,1)S(1)}, bf16[192,3072]{1,0:T(8,128)(2,1)}, u32[]{:S(2)}) copy-start(bf16[192,3072]{1,0:T(8,128)(2,1)} %param.26) | copy-start | bytes 3538948
Sparse Core Ops, SparseCore 0:
  11.5 62.8 all-gather.8
  77.9 53.2 all-gather.10
  134.1 62.1 all-gather.12
  199.1 62.4 all-gather.14
  274.0 117.6 reduce-scatter.8
  398.0 106.0 reduce-scatter.10
  509.8 95.2 reduce-scatter.6
  610.5 101.8 reduce-scatter.4
  714.3 23.0 all-gather.16
  739.1 24.0 all-gather.18

commit v2 on v1

--- a/solution.py
+++ b/solution.py
@@ -237,24 +237,91 @@
     return cut.reshape(seq_count, row_count, parts * groups * width)
 
 
-def whole_weight(part):
-    places = lax.axis_size("ctx")
+def bit_count(size):
+    return size.bit_length() - 1
+
+
+def even_powers():
+    return all((lax.axis_size(name) & (lax.axis_size(name) - 1)) == 0 for name in ("ctx", "wsh"))
+
+
+def swap(array, axis_name, bit):
+    flip = 1 << bit
+    pairs = [(index, index ^ flip) for index in range(lax.axis_size(axis_name))]
+    return lax.ppermute(array, axis_name, pairs)
+
+
+def halve(array, axis_name, lead, bits, order):
+    left = sorted(order, reverse=True)
+    for bit in order:
+        dim = lead + left.index(bit)
+        mine = (lax.axis_index(axis_name) >> bit) & 1
+        away = lax.dynamic_index_in_dim(array, 1 - mine, dim, keepdims=False)
+        kept = lax.dynamic_index_in_dim(array, mine, dim, keepdims=False)
+        came = swap(away, axis_name, bit)
+        array = (kept.astype(jnp.float32) + came.astype(jnp.float32)).astype(array.dtype)
+        left.remove(bit)
+    return array
+
+
+def double(array, axis_name, lead, order):
+    held = []
+    for bit in order:
+        came = swap(array, axis_name, bit)
+        held = sorted(held + [bit], reverse=True)
+        first = ((lax.axis_index(axis_name) >> bit) & 1) == 0
+        array = jnp.stack(
+            [jnp.where(first, array, came), jnp.where(first, came, array)],
+            axis=lead + held.index(bit),
+        )
+    return array
+
+
+def bit_order(bits, turned):
+    rest = list(range(1, bits))
+    return [0] + (rest[::-1] if turned else rest)
+
+
+def whole_weight(part, turned=False):
+    places, shards = lax.axis_size("ctx"), lax.axis_size("wsh")
     rows = part.shape[0]
-    if rows % places:
+    if rows % (8 * places) or not even_powers():
         return lax.all_gather(part, "wsh", axis=0, tiled=True)
     share = rows // places
     own = lax.dynamic_slice_in_dim(part, lax.axis_index("ctx") * share, share, 0)
-    return lax.all_gather(own, ("wsh", "ctx"), axis=0, tiled=True)
-
-
-def owned_gradient(grad):
-    places = lax.axis_size("ctx")
+    z_bits = bit_count(shards)
+    own = double(own, "wsh", 0, list(range(z_bits))[::-1])
+    own = double(own, "ctx", z_bits, bit_order(bit_count(places), turned)[::-1])
+    return own.reshape(shards * rows, part.shape[1])
+
+
+def owned_gradient(grad, turned=False):
+    places, shards = lax.axis_size("ctx"), lax.axis_size("wsh")
     near = grad.astype(jnp.bfloat16)
-    if near.shape[0] % (places * lax.axis_size("wsh")):
+    rows, width = near.shape
+    if rows % (8 * places * shards) or not even_powers():
         part = lax.psum_scatter(near, "wsh", scatter_dimension=0, tiled=True).astype(jnp.float32)
         return lax.psum(part, "ctx")
-    part = lax.psum_scatter(near, ("wsh", "ctx"), scatter_dimension=0, tiled=True)
-    return lax.all_gather(part, "ctx", axis=0, tiled=True).astype(jnp.float32)
+    z_bits, bits = bit_count(shards), bit_count(places)
+    share = rows // (places * shards)
+    near = near.reshape((2,) * (z_bits + bits) + (share, width))
+    order = bit_order(bits, turned)
+    near = halve(near, "ctx", z_bits, bits, order)
+    near = halve(near, "wsh", 0, z_bits, list(range(z_bits)))
+    near = double(near, "ctx", 0, order[::-1])
+    return near.reshape(rows // shards, width).astype(jnp.float32)
+
+
+def owned_vectors(stacked):
+    if not even_powers():
+        summed = lax.psum(stacked, ("wsh", "ctx"))
+        return lax.dynamic_slice_in_dim(summed, lax.axis_index("wsh"), 1, 0)[0]
+    z_bits = bit_count(lax.axis_size("wsh"))
+    mine = stacked.reshape((2,) * z_bits + (1, stacked.shape[1]))
+    mine = halve(mine, "wsh", 0, z_bits, list(range(z_bits)))
+    for bit in range(bit_count(lax.axis_size("ctx"))):
+        mine = mine + swap(mine, "ctx", bit)
+    return mine[0]
 
 
 def loop_attend(qkv, pair_of_device, block_len, qpos_low, qpos_up, scale):
@@ -467,10 +534,13 @@
         down_shift,
         up_shift,
     ) = whole_small
-    whole_qkv = whole_weight(w_qkv)
-    whole_out = whole_weight(w_out)
+    half = w_qkv.shape[1] // 2
+    whole_qkv = jnp.concatenate(
+        [whole_weight(w_qkv[:, :half], True), whole_weight(w_qkv[:, half:])], axis=1
+    )
+    whole_out = whole_weight(w_out, True)
     whole_up = whole_weight(w_up)
-    whole_down = whole_weight(w_down)
+    whole_down = whole_weight(w_down, True)
     seq_count, row_count, model_width = block_input.shape
     block_len = row_count // 2
     head_count = HEADS
@@ -565,8 +635,7 @@
     )
     shards = lax.axis_size("wsh")
     stacked = jnp.concatenate([one.reshape(shards, -1) for one in vectors], axis=1)
-    summed = lax.psum(stacked, ("wsh", "ctx"))
-    mine = lax.dynamic_slice_in_dim(summed, lax.axis_index("wsh"), 1, 0)[0]
+    mine = owned_vectors(stacked)
     own = []
     start = 0
     for one in vectors:
@@ -582,16 +651,22 @@
         grad_input,
         own_ln1_gain,
         own_ln1_bias,
-        owned_gradient(grad_qkv),
+        jnp.concatenate(
+            [
+                owned_gradient(grad_qkv[:, :half], True),
+                owned_gradient(grad_qkv[:, half:]),
+            ],
+            axis=1,
+        ),
         own_bias_query,
         own_bias_value,
-        owned_gradient(grad_out),
+        owned_gradient(grad_out, True),
         own_bias_out,
         own_ln2_gain,
         own_ln2_bias,
         owned_gradient(grad_up),
         own_bias_up,
-        owned_gradient(grad_down),
+        owned_gradient(grad_down, True),
         own_bias_down,
     )
 

time: 781 us -> 396 us (0.51)
  waiting for transfers between devices: 527 us -> 152 us
  blocking collectives: 104 us -> 18.5 us
  starting transfers between devices: 12.2 us -> 78.9 us
  other arithmetic: 15.3 us -> 41.2 us
  matrix products: 49.2 us -> 31.8 us
  local copies, waits for them, and re-layouts: 35.5 us -> 49.9 us
  between operations: 15.1 us -> 2.98 us
    reduce_scatter x4 -> x0, waiting for transfers between devices: 290 us -> none  [owned_gradient(): lax.psum_scatter(near, ('wsh', 'ctx'), scatter_dimension=0, tiled=True)]
    all_gather x6 -> x0, waiting for transfers between devices: 213 us -> none  [the longest x4 178 us: whole_weight(): return lax.all_gather(own, ('wsh', 'ctx'), axis=0, tiled=True)]
    ppermute x0 -> x70, waiting for transfers between devices: none -> 144 us  [swap(): return lax.ppermute(array, axis_name, pairs)]
    ppermute x0 -> x70, starting transfers between devices: none -> 60.6 us  [swap(): return lax.ppermute(array, axis_name, pairs)]
    psum x1 -> x0, blocking collectives: 40.4 us -> none  [body(): summed = lax.psum(stacked, ('wsh', 'ctx'))]
    all_to_all x1 -> x0, blocking collectives: 28.7 us -> none  [bring_back(): lax.all_to_all(array.reshape(places, row_count, parts * width), 'ctx', 0,...]
    another operation x0 -> x77, other arithmetic: none -> 23.1 us  [double(): jnp.stack([jnp.where(first, array, came), jnp.where(first, came, array)],...]
    all_to_all x2, waiting for transfers between devices: 23.4 us -> 1.79 us  [spread_out(): moved = lax.all_to_all(cut, 'ctx', 0, 0, tiled=True)]
  transfers between devices with their start and end apart: 13 -> 74, of which waited for: 12 -> 42; matrix products, arithmetic and copies ran while one was open for 10% -> 24% of each run, Pallas kernels for 2% -> 4%
where the time goes in v2:
time: 396 us; the launch traced here: 390 us
  waiting for transfers between devices  152 us (38%)
  starting transfers between devices  78.9 us (20%)
  local copies, waits for them, and re-layouts  49.9 us (13%)
  other arithmetic  41.2 us (10%)
  matrix products  31.8 us (8%)
  blocking collectives  18.5 us (5%)
  Pallas kernels  14.6 us (4%)
    ppermute x70, waiting for transfers between devices, swap(): return lax.ppermute(array, axis_name, pairs)  144 us
    ppermute x70, starting transfers between devices, swap(): return lax.ppermute(array, axis_name, pairs)  60.6 us
    another operation x77, other arithmetic, double(): jnp.stack([jnp.where(first, array, came), jnp.where(first, came, array)],...  23.1 us
    all_gather x1, blocking collectives, body(): lax.all_gather(jnp.concatenate(small).reshape(1, -1), 'wsh', axis=0, tile...  18.5 us
    convert_element_type x25, other arithmetic, halve(): (kept.astype(jnp.float32) + came.astype(jnp.float32)).astype(array.dtype)  11 us
    unnamed x142, local copies, waits for them, and re-layouts  10.6 us
    all_to_all x2, starting transfers between devices, bring_back(): lax.all_to_all(array.reshape(places, row_count, parts * width), 'ctx', 0,...  10 us
    squeeze x26, local copies, waits for them, and re-layouts, halve(): away = lax.dynamic_index_in_dim(array, 1 - mine, dim, keepdims=False)  9.43 us
  transfers between devices with their start and end apart: 74, of which 42 were waited for; matrix products, arithmetic and copies ran while one was open for 24% of the time, Pallas kernels for 4%

profile of v2, /device:TPU:0, one launch (start us, length us, event | category | flops | bytes accessed | tf_op | source)
XLA Modules:
  0.0 389.6 jit_solution(7991475599039952113)
XLA Ops:
  2.1 4.1 %collective-permute-start.5 = (bf16[24,1152]{1,0:T(8,128)(2,1)S(1)}, bf16[24,1152]{1,0:T(8,128)(2,1)S(1)}, u32[]{:S(2)}, u32[]{:S(2)}) collective-permute-start(bf16[24,1152]{1,0:T(8,128)(2,1)S(1)} %constant_dynamic-slice_fusion.7), channel_id=1, source_target_pairs={{0,2},{1,3},{2,0},{3,1},{4,6},{5,7},{6,4},{7,5},{8,10},{9,11},{10,... | collective-permute-start | bytes 165896 | tf_op jit(solution)/shard_map/ppermute | solution.py:251
  7.0 2.8 collective-permute-start.10
  11.9 2.9 collective-permute-start.15
  14.9 18.5 %all-gather.1 = bf16[4,1,2304]{2,1,0:T(2,128)(2,1)S(1)} all-gather(bf16[1,1,2304]{2,1,0:T(2,128)(2,1)S(1)} %reshape.350), channel_id=2, replica_groups=mesh['ctx'=8,'wsh'=4] {'wsh'}, dimensions={0}, use_global_device_ids=true | all-gather | bytes 23040 | tf_op jit(solution)/shard_map/all_gather | solution.py:519
  37.8 2.1 collective-permute-start.6
  40.1 2.2 collective-permute-done.11
  51.0 4.7 %collective-permute-done.7 = bf16[2,2,24,1152]{3,2,0,1:T(8,128)(2,1)S(1)} collective-permute-done((bf16[2,2,24,1152]{3,2,0,1:T(8,128)(2,1)S(1)}, bf16[2,2,24,1152]{3,2,0,1:T(8,128)(2,1)S(1)}, u32[]{:S(2)}, u32[]{:S(2)}) %collective-permute-start.7) | collective-permute-done | bytes 221216 | tf_op jit(solution)/shard_map/ppermute | solution.py:251
  63.0 5.9 %collective-permute-done.8 = bf16[2,2,2,24,1152]{4,3,0,1,2:T(8,128)(2,1)S(1)} collective-permute-done((bf16[2,2,2,24,1152]{4,3,0,1,2:T(8,128)(2,1)S(1)}, bf16[2,2,2,24,1152]{4,3,0,1,2:T(8,128)(2,1)S(1)}, u32[]{:S(2)}, u32[]{:S(2)}) %collective-permute-start.8) | collective-permute-done | bytes 442400 | tf_op jit(solution)/shard_map/ppermute | solution.py:251
  69.2 2.2 collective-permute-done.3
  71.7 4.6 %collective-permute-done.22 = bf16[2,2,96,768]{3,2,0,1:T(8,128)(2,1)S(1)} collective-permute-done((bf16[2,2,96,768]{3,2,0,1:T(8,128)(2,1)S(1)}, bf16[2,2,96,768]{3,2,0,1:T(8,128)(2,1)S(1)}, u32[]{:S(2)}, u32[]{:S(2)}) %collective-permute-start.22) | collective-permute-done | bytes 589856 | tf_op jit(solution)/shard_map/ppermute | solution.py:251
  79.1 3.7 collective-permute-done.17
  87.9 2.2 fusion.2
  90.1 2.4 copy.116
  92.5 2.4 copy.117
  94.9 4.6 %all-to-all-start = ((bf16[8,128,576]{1,2,0:T(8,128)(2,1)}), bf16[8,128,576]{1,2,0:T(8,128)(2,1)}, u32[]{:S(2)}, u32[]{:S(2)}) async-start(bf16[8,128,576]{1,2,0:T(8,128)(2,1)} %bitcast.419), calls=%async_computation | async-start | bytes 2359296 | tf_op jit(solution)/shard_map/all_to_all | solution.py:227
  99.4 9.0 %collective-permute-done.23 = bf16[2,2,2,96,768]{4,3,0,1,2:T(8,128)(2,1)} collective-permute-done((bf16[2,2,2,96,768]{4,3,0,1,2:T(8,128)(2,1)}, bf16[2,2,2,96,768]{4,3,0,1,2:T(8,128)(2,1)}, u32[]{:S(2)}, u32[]{:S(2)}) %collective-permute-start.23) | collective-permute-done | bytes 1179680 | tf_op jit(solution)/shard_map/ppermute | solution.py:251
  109.9 1.8 pad_maximum_fusion.3
  113.5 1.8 pad_maximum_fusion.2
  116.3 1.7 all-to-all-done
  118.0 1.7 copy.118
  119.7 5.9 %shard_map.271 = (bf16[1024,192]{1,0:T(8,128)(2,1)S(1)}, f32[1024,192]{1,0:T(8,128)S(1)}, f32[1024,128]{1,0:T(8,128)S(1)}) custom-call(s32[16]{0:T(128)S(1)} %fusion.57.order_ref, bf16[1024,576]{1,0:T(8,128)(2,1)S(1)} %bitcast.393), custom_call_target="tpu_custom_call" | custom-call | tf_op jit(solution)/shard_map/pallas_call | solution.py:186
  128.3 5.7 %all-to-all-start.1 = ((bf16[8,128,192]{1,2,0:T(8,128)(2,1)}), bf16[8,128,192]{1,2,0:T(8,128)(2,1)S(1)}, u32[]{:S(2)}, u32[]{:S(2)}) async-start(bf16[8,128,192]{1,2,0:T(8,128)(2,1)} %copy.119), calls=%async_computation.1 | async-start | bytes 786432 | tf_op jit(solution)/shard_map/all_to_all | solution.py:234
  136.4 5.9 %all-to-all-done.1 = bf16[8,128,192]{1,2,0:T(8,128)(2,1)S(1)} async-done(((bf16[8,128,192]{1,2,0:T(8,128)(2,1)}), bf16[8,128,192]{1,2,0:T(8,128)(2,1)S(1)}, u32[]{:S(2)}, u32[]{:S(2)}) %all-to-all-start.1) | async-done | bytes 393248 | tf_op jit(solution)/shard_map/all_to_all | solution.py:234
  142.3 2.1 fusion.68
  144.6 2.0 select_bitcast_fusion.1
  149.4 2.0 select_bitcast_fusion.3
  154.1 3.7 convert_reduce_fusion
  157.8 2.3 multiply_reduce_fusion
  163.8 2.2 collective-permute-done.46
  168.1 6.3 %fusion.17 = bf16[2,128,768]{2,1,0:T(8,128)(2,1)} fusion(f32[2,128,768]{2,1,0:T(8,128)S(1)} %get-tuple-element.139, bf16[3072,768,1]{1,0,2:T(8,128)(2,1)} %bitcast.418, f32[768]{0:T(1024)S(1)} %add.324, f32[2,128,3072]{2,1,0:T(8,128)} %copy-done.23), kind=kOutput, calls=%fused_computation.50 | convolution fusion | flops 1215627264 | bytes 9047040 | tf_op jit(solution)/shard_map/dot_general | solution.py:589
  174.4 2.2 collective-permute-done.47
  177.4 4.5 %bitcast_convert_fusion = bf16[3072,768]{1,0:T(8,128)(2,1)} fusion(bf16[2,128,768]{2,1,0:T(8,128)(2,1)S(1)} %copy-done.34, f32[2,128,3072]{2,1,0:T(8,128)S(1)} %copy-done.24), kind=kOutput, calls=%fused_computation | convolution fusion | flops 1217396736 | bytes 8257536 | tf_op jit(solution)/shard_map/srf,srd->fd/dot_general | solution.py:592
  184.1 3.7 all-to-all-start.2
  190.7 5.2 %bitcast_convert_fusion.1 = bf16[768,3072]{1,0:T(8,128)(2,1)} fusion(bf16[2,128,3072]{2,1,0:T(8,128)(2,1)} %copy-done.36, f32[2,128,768]{2,1,0:T(8,128)S(1)} %get-tuple-element.139, f32[768]{0:T(1024)S(1)} %add.314, f32[768]{0:T(1024)S(1)} %mul.177, f32[2,128]{1,0:T(2,128)S(1)} %fusion.56, f32[2,128]{1,0:T(2,128)S(1)} %broadcast_multiply_fusion), kind=kOutput, calls=%fused_computation.1 | convolution fusion | flops 1211301888 | bytes 7086080 | tf_op jit(solution)/shard_map/srd,srf->df/dot_general | solution.py:598
  198.5 8.7 %shard_map.272 = bf16[1024,576]{1,0:T(8,128)(2,1)S(1)} custom-call(s32[16]{0:T(128)S(1)} %fusion.57.order_ref, bf16[1024,576]{1,0:T(8,128)(2,1)S(1)} %bitcast.394, bf16[1024,192]{1,0:T(8,128)(2,1)S(1)} %bitcast.396, f32[1024,192]{1,0:T(8,128)S(1)} %copy-done.1, f32[1024,128]{1,0:T(8,128)S(1)} %copy-done.3), custom_call_target="tpu_custom_call" | custom-call | tf_op jit(solution)/shard_map/pallas_call | solution.py:206
  208.7 4.3 %all-to-all-start.3 = ((bf16[8,128,576]{1,2,0:T(8,128)(2,1)}), bf16[8,128,576]{1,2,0:T(8,128)(2,1)S(1)}, u32[]{:S(2)}, u32[]{:S(2)}) async-start(bf16[8,128,576]{1,2,0:T(8,128)(2,1)} %copy.126), calls=%async_computation.3 | async-start | bytes 2359296 | tf_op jit(solution)/shard_map/all_to_all | solution.py:234
  213.8 2.1 collective-permute-start.51
  215.9 3.3 dynamic-slice_bitcast_fusion.1
  221.2 8.3 %collective-permute-done.51 = bf16[24,768]{1,0:T(8,128)(2,1)S(1)} collective-permute-done((bf16[24,768]{1,0:T(8,128)(2,1)S(1)}, bf16[24,768]{1,0:T(8,128)(2,1)S(1)}, u32[]{:S(2)}, u32[]{:S(2)}) %collective-permute-start.51) | collective-permute-done | bytes 36896 | tf_op jit(solution)/shard_map/ppermute | solution.py:251
  231.0 3.2 dynamic-slice_bitcast_fusion
  237.1 1.8 fusion.60
  247.7 2.6 collective-permute-done.25
  252.1 2.9 collective-permute-done.26
  258.0 2.1 collective-permute-done.28
  261.7 2.2 collective-permute-done.29
  267.0 3.0 fusion.1
  271.7 2.4 fusion
  275.2 3.4 collective-permute-done.39
  281.2 25.1 %collective-permute-done.40 = bf16[2,2,24,1152]{3,2,1,0:T(8,128)(2,1)S(1)} collective-permute-done((bf16[2,2,24,1152]{3,2,1,0:T(8,128)(2,1)S(1)}, bf16[2,2,24,1152]{3,2,1,0:T(8,128)(2,1)S(1)}, u32[]{:S(2)}, u32[]{:S(2)}) %collective-permute-start.40) | collective-permute-done | bytes 221216 | tf_op jit(solution)/shard_map/ppermute | solution.py:251
  308.7 2.6 collective-permute-done.41
  311.3 2.0 collective-permute-start.42
  314.8 2.2 collective-permute-done.42
  317.7 1.7 collective-permute-done.34
  321.3 2.1 collective-permute-start.44
  323.8 2.4 collective-permute-done.44
  326.3 2.2 collective-permute-done.36
  331.5 2.0 collective-permute-start.64
  333.5 12.6 %collective-permute-done.56 = bf16[2,2,24,3072]{3,2,1,0:T(8,128)(2,1)S(1)} collective-permute-done((bf16[2,2,24,3072]{3,2,1,0:T(8,128)(2,1)S(1)}, bf16[2,2,24,3072]{3,2,1,0:T(8,128)(2,1)S(1)}, u32[]{:S(2)}, u32[]{:S(2)}) %collective-permute-start.56) | collective-permute-done | bytes 589856 | tf_op jit(solution)/shard_map/ppermute | solution.py:251
  348.6 7.7 %collective-permute-done.57 = bf16[2,24,3072]{2,1,0:T(8,128)(2,1)S(1)} collective-permute-done((bf16[2,24,3072]{2,1,0:T(8,128)(2,1)S(1)}, bf16[2,24,3072]{2,1,0:T(8,128)(2,1)S(1)}, u32[]{:S(2)}, u32[]{:S(2)}) %collective-permute-start.57) | collective-permute-done | bytes 294944 | tf_op jit(solution)/shard_map/ppermute | solution.py:251
  357.1 6.4 %collective-permute-done.65 = bf16[2,96,768]{2,1,0:T(8,128)(2,1)S(1)} collective-permute-done((bf16[2,96,768]{2,1,0:T(8,128)(2,1)S(1)}, bf16[2,96,768]{2,1,0:T(8,128)(2,1)S(1)}, u32[]{:S(2)}, u32[]{:S(2)}) %collective-permute-start.65) | collective-permute-done | bytes 294944 | tf_op jit(solution)/shard_map/ppermute | solution.py:251
  363.9 3.3 collective-permute-done.58
  367.3 4.1 %collective-permute-done.66 = bf16[96,768]{1,0:T(8,128)(2,1)S(1)} collective-permute-done((bf16[96,768]{1,0:T(8,128)(2,1)S(1)}, bf16[96,768]{1,0:T(8,128)(2,1)S(1)}, u32[]{:S(2)}, u32[]{:S(2)}) %collective-permute-start.66) | collective-permute-done | bytes 147488 | tf_op jit(solution)/shard_map/ppermute | solution.py:251
  373.7 4.6 %collective-permute-done.67 = bf16[96,768]{1,0:T(8,128)(2,1)S(1)} collective-permute-done((bf16[96,768]{1,0:T(8,128)(2,1)S(1)}, bf16[96,768]{1,0:T(8,128)(2,1)S(1)}, u32[]{:S(2)}, u32[]{:S(2)}) %collective-permute-start.67) | collective-permute-done | bytes 147488 | tf_op jit(solution)/shard_map/ppermute | solution.py:251
  378.7 4.2 %collective-permute-done.60 = bf16[2,24,3072]{2,1,0:T(8,128)(2,1)S(1)} collective-permute-done((bf16[2,24,3072]{2,1,0:T(8,128)(2,1)S(1)}, bf16[2,24,3072]{2,1,0:T(8,128)(2,1)S(1)}, u32[]{:S(2)}, u32[]{:S(2)}) %collective-permute-start.60) | collective-permute-done | bytes 294944 | tf_op jit(solution)/shard_map/ppermute | solution.py:251
  (450 shorter events, 116.7 us)
Async XLA Ops:
  2.1 35.7 %collective-permute-start.5 = (bf16[24,1152]{1,0:T(8,128)(2,1)S(1)}, bf16[24,1152]{1,0:T(8,128)(2,1)S(1)}, u32[]{:S(2)}, u32[]{:S(2)}) collective-permute-start(bf16[24,1152]{1,0:T(8,128)(2,1)S(1)} %constant_dynamic-slice_fusion.7), channel_id=1, source_target_pairs={{0,2},{1,3},{2,0},{3,1},{4,6},{5,7},{6,4},{7,5},{8,10},{9,11},{10,... | collective-permute-start | bytes 165896 | tf_op jit(solution)/shard_map/ppermute | solution.py:251
  6.2 33.7 %collective-permute-start = (bf16[24,1152]{1,0:T(8,128)(2,1)S(1)}, bf16[24,1152]{1,0:T(8,128)(2,1)S(1)}, u32[]{:S(2)}, u32[]{:S(2)}) collective-permute-start(bf16[24,1152]{1,0:T(8,128)(2,1)S(1)} %constant_dynamic-slice_fusion.8), channel_id=1, source_target_pairs={{0,2},{1,3},{2,0},{3,1},{4,6},{5,7},{6,4},{7,5},{8,10},{9,11},{10,... | collective-permute-start | bytes 165896 | tf_op jit(solution)/shard_map/ppermute | solution.py:251
  7.0 29.9 %collective-permute-start.10 = (bf16[24,768]{1,0:T(8,128)(2,1)S(1)}, bf16[24,768]{1,0:T(8,128)(2,1)S(1)}, u32[]{:S(2)}, u32[]{:S(2)}) collective-permute-start(bf16[24,768]{1,0:T(8,128)(2,1)S(1)} %constant_dynamic-slice_fusion.6), channel_id=1, source_target_pairs={{0,2},{1,3},{2,0},{3,1},{4,6},{5,7},{6,4},{7,5},{8,10},{9,11},{10,... | collective-permute-start | bytes 110600 | tf_op jit(solution)/shard_map/ppermute | solution.py:251
  10.8 33.0 %collective-permute-start.20 = (bf16[96,768]{1,0:T(8,128)(2,1)S(1)}, bf16[96,768]{1,0:T(8,128)(2,1)S(1)}, u32[]{:S(2)}, u32[]{:S(2)}) collective-permute-start(bf16[96,768]{1,0:T(8,128)(2,1)S(1)} %constant_dynamic-slice_fusion.4), channel_id=1, source_target_pairs={{0,2},{1,3},{2,0},{3,1},{4,6},{5,7},{6,4},{7,5},{8,10},{9,11},{10,... | collective-permute-start | bytes 442376 | tf_op jit(solution)/shard_map/ppermute | solution.py:251
  11.9 33.7 %collective-permute-start.15 = (bf16[24,3072]{1,0:T(8,128)(2,1)S(1)}, bf16[24,3072]{1,0:T(8,128)(2,1)S(1)}, u32[]{:S(2)}, u32[]{:S(2)}) collective-permute-start(bf16[24,3072]{1,0:T(8,128)(2,1)S(1)} %constant_dynamic-slice_fusion.5), channel_id=1, source_target_pairs={{0,2},{1,3},{2,0},{3,1},{4,6},{5,7},{6,4},{7,5},{8,10},{9,11},{10,... | collective-permute-start | bytes 442376 | tf_op jit(solution)/shard_map/ppermute | solution.py:251
  37.7 4.5 %collective-permute-start.11 = (bf16[2,24,768]{2,1,0:T(8,128)(2,1)S(1)}, bf16[2,24,768]{2,1,0:T(8,128)(2,1)S(1)}, u32[]{:S(2)}, u32[]{:S(2)}) collective-permute-start(bf16[2,24,768]{2,1,0:T(8,128)(2,1)S(1)} %pad_maximum_fusion.35), channel_id=1, source_target_pairs={{0,1},{1,0},{2,3},{3,2},{4,5},{5,4},{6,7},{7,6},{8,9},{9,8},{10,11... | collective-permute-start | bytes 221192 | tf_op jit(solution)/shard_map/ppermute | solution.py:251
  37.8 10.2 %collective-permute-start.6 = (bf16[2,24,1152]{2,1,0:T(8,128)(2,1)S(1)}, bf16[2,24,1152]{2,1,0:T(8,128)(2,1)S(1)}, u32[]{:S(2)}, u32[]{:S(2)}) collective-permute-start(bf16[2,24,1152]{2,1,0:T(8,128)(2,1)S(1)} %pad_maximum_fusion.32), channel_id=1, source_target_pairs={{0,1},{1,0},{2,3},{3,2},{4,5},{5,4},{6,7},{7,6},{8,9},{9,8},{10,11... | collective-permute-start | bytes 331784 | tf_op jit(solution)/shard_map/ppermute | solution.py:251
  40.0 9.7 %collective-permute-start.1 = (bf16[2,24,1152]{2,1,0:T(8,128)(2,1)S(1)}, bf16[2,24,1152]{2,1,0:T(8,128)(2,1)S(1)}, u32[]{:S(2)}, u32[]{:S(2)}) collective-permute-start(bf16[2,24,1152]{2,1,0:T(8,128)(2,1)S(1)} %pad_maximum_fusion.31), channel_id=1, source_target_pairs={{0,1},{1,0},{2,3},{3,2},{4,5},{5,4},{6,7},{7,6},{8,9},{9,8},{10,11... | collective-permute-start | bytes 331784 | tf_op jit(solution)/shard_map/ppermute | solution.py:251
  42.3 8.1 %collective-permute-start.12 = (bf16[2,2,24,768]{3,2,0,1:T(8,128)(2,1)S(1)}, bf16[2,2,24,768]{3,2,0,1:T(8,128)(2,1)S(1)}, u32[]{:S(2)}, u32[]{:S(2)}) collective-permute-start(bf16[2,2,24,768]{3,2,0,1:T(8,128)(2,1)S(1)} %pad_maximum_fusion.29), channel_id=1, source_target_pairs={{0,8},{4,12},{8,0},{12,4},{16,24},{20,28},{24,16},{28,20},{1,9},{5... | collective-permute-start | bytes 442376 | tf_op jit(solution)/shard_map/ppermute | solution.py:251
  44.8 13.9 %collective-permute-start.21 = (bf16[2,96,768]{2,1,0:T(8,128)(2,1)S(1)}, bf16[2,96,768]{2,1,0:T(8,128)(2,1)S(1)}, u32[]{:S(2)}, u32[]{:S(2)}) collective-permute-start(bf16[2,96,768]{2,1,0:T(8,128)(2,1)S(1)} %pad_maximum_fusion.22), channel_id=1, source_target_pairs={{0,1},{1,0},{2,3},{3,2},{4,5},{5,4},{6,7},{7,6},{8,9},{9,8},{10,11... | collective-permute-start | bytes 884744 | tf_op jit(solution)/shard_map/ppermute | solution.py:251
  46.6 13.6 %collective-permute-start.16 = (bf16[2,24,3072]{2,1,0:T(8,128)(2,1)S(1)}, bf16[2,24,3072]{2,1,0:T(8,128)(2,1)S(1)}, u32[]{:S(2)}, u32[]{:S(2)}) collective-permute-start(bf16[2,24,3072]{2,1,0:T(8,128)(2,1)S(1)} %pad_maximum_fusion.21), channel_id=1, source_target_pairs={{0,1},{1,0},{2,3},{3,2},{4,5},{5,4},{6,7},{7,6},{8,9},{9,8},{10,11... | collective-permute-start | bytes 884744 | tf_op jit(solution)/shard_map/ppermute | solution.py:251
  48.1 7.6 %collective-permute-start.7 = (bf16[2,2,24,1152]{3,2,0,1:T(8,128)(2,1)S(1)}, bf16[2,2,24,1152]{3,2,0,1:T(8,128)(2,1)S(1)}, u32[]{:S(2)}, u32[]{:S(2)}) collective-permute-start(bf16[2,2,24,1152]{3,2,0,1:T(8,128)(2,1)S(1)} %pad_maximum_fusion.26), channel_id=1, source_target_pairs={{0,16},{4,20},{8,24},{12,28},{16,0},{20,4},{24,8},{28,12},{1,17},{... | collective-permute-start | bytes 663560 | tf_op jit(solution)/shard_map/ppermute | solution.py:251
  49.7 8.4 %collective-permute-start.2 = (bf16[2,2,24,1152]{3,2,0,1:T(8,128)(2,1)S(1)}, bf16[2,2,24,1152]{3,2,0,1:T(8,128)(2,1)S(1)}, u32[]{:S(2)}, u32[]{:S(2)}) collective-permute-start(bf16[2,2,24,1152]{3,2,0,1:T(8,128)(2,1)S(1)} %pad_maximum_fusion.25), channel_id=1, source_target_pairs={{0,8},{4,12},{8,0},{12,4},{16,24},{20,28},{24,16},{28,20},{1,9},{5... | collective-permute-start | bytes 663560 | tf_op jit(solution)/shard_map/ppermute | solution.py:251
  50.4 11.6 %collective-permute-start.13 = (bf16[2,2,2,24,768]{4,3,0,1,2:T(8,128)(2,1)S(1)}, bf16[2,2,2,24,768]{4,3,0,1,2:T(8,128)(2,1)S(1)}, u32[]{:S(2)}, u32[]{:S(2)}) collective-permute-start(bf16[2,2,2,24,768]{4,3,0,1,2:T(8,128)(2,1)S(1)} %pad_maximum_fusion.20), channel_id=1, source_target_pairs={{0,16},{4,20},{8,24},{12,28},{16,0},{20,4},{24,8},{28,12},{1,17},{... | collective-permute-start | bytes 884744 | tf_op jit(solution)/shard_map/ppermute | solution.py:251
  55.8 13.2 %collective-permute-start.8 = (bf16[2,2,2,24,1152]{4,3,0,1,2:T(8,128)(2,1)S(1)}, bf16[2,2,2,24,1152]{4,3,0,1,2:T(8,128)(2,1)S(1)}, u32[]{:S(2)}, u32[]{:S(2)}) collective-permute-start(bf16[2,2,2,24,1152]{4,3,0,1,2:T(8,128)(2,1)S(1)} %pad_maximum_fusion.17), channel_id=1, source_target_pairs={{0,8},{4,12},{8,0},{12,4},{16,24},{20,28},{24,16},{28,20},{1,9},{5... | collective-permute-start | bytes 1327112 | tf_op jit(solution)/shard_map/ppermute | solution.py:251
  58.3 13.2 %collective-permute-start.3 = (bf16[2,2,2,24,1152]{4,3,0,1,2:T(8,128)(2,1)S(1)}, bf16[2,2,2,24,1152]{4,3,0,1,2:T(8,128)(2,1)S(1)}, u32[]{:S(2)}, u32[]{:S(2)}) collective-permute-start(bf16[2,2,2,24,1152]{4,3,0,1,2:T(8,128)(2,1)S(1)} %pad_maximum_fusion.16), channel_id=1, source_target_pairs={{0,16},{4,20},{8,24},{12,28},{16,0},{20,4},{24,8},{28,12},{1,17},{... | collective-permute-start | bytes 1327112 | tf_op jit(solution)/shard_map/ppermute | solution.py:251
  58.8 17.5 %collective-permute-start.22 = (bf16[2,2,96,768]{3,2,0,1:T(8,128)(2,1)S(1)}, bf16[2,2,96,768]{3,2,0,1:T(8,128)(2,1)S(1)}, u32[]{:S(2)}, u32[]{:S(2)}) collective-permute-start(bf16[2,2,96,768]{3,2,0,1:T(8,128)(2,1)S(1)} %pad_maximum_fusion.13), channel_id=1, source_target_pairs={{0,8},{4,12},{8,0},{12,4},{16,24},{20,28},{24,16},{28,20},{1,9},{5... | collective-permute-start | bytes 1769480 | tf_op jit(solution)/shard_map/ppermute | solution.py:251
  60.4 22.4 %collective-permute-start.17 = (bf16[2,2,24,3072]{3,2,0,1:T(8,128)(2,1)S(1)}, bf16[2,2,24,3072]{3,2,0,1:T(8,128)(2,1)S(1)}, u32[]{:S(2)}, u32[]{:S(2)}) collective-permute-start(bf16[2,2,24,3072]{3,2,0,1:T(8,128)(2,1)S(1)} %pad_maximum_fusion.12), channel_id=1, source_target_pairs={{0,16},{4,20},{8,24},{12,28},{16,0},{20,4},{24,8},{28,12},{1,17},{... | collective-permute-start | bytes 1769480 | tf_op jit(solution)/shard_map/ppermute | solution.py:251
  63.0 71.0 %collective-permute-start.14 = (bf16[2,2,2,2,24,768]{5,4,0,1,3,2:T(8,128)(2,1)}, bf16[2,2,2,2,24,768]{5,4,0,1,3,2:T(8,128)(2,1)}, u32[]{:S(2)}, u32[]{:S(2)}) collective-permute-start(bf16[2,2,2,2,24,768]{5,4,0,1,3,2:T(8,128)(2,1)} %pad_maximum_fusion.11), channel_id=1, source_target_pairs={{0,4},{4,0},{8,12},{12,8},{16,20},{20,16},{24,28},{28,24},{1,5},{5... | collective-permute-start | bytes 1769480 | tf_op jit(solution)/shard_map/ppermute | solution.py:251
  69.1 16.2 %collective-permute-start.9 = (bf16[2,2,2,2,24,1152]{5,4,0,1,2,3:T(8,128)(2,1)S(1)}, bf16[2,2,2,2,24,1152]{5,4,0,1,2,3:T(8,128)(2,1)S(1)}, u32[]{:S(2)}, u32[]{:S(2)}) collective-permute-start(bf16[2,2,2,2,24,1152]{5,4,0,1,2,3:T(8,128)(2,1)S(1)} %pad_maximum_fusion.10), channel_id=1, source_target_pairs={{0,4},{4,0},{8,12},{12,8},{16,20},{20,16},{24,28},{28,24},{1,5},{5... | collective-permute-start | bytes 2654216 | tf_op jit(solution)/shard_map/ppermute | solution.py:251
  71.6 13.9 %collective-permute-start.4 = (bf16[2,2,2,2,24,1152]{5,4,0,1,2,3:T(8,128)(2,1)S(1)}, bf16[2,2,2,2,24,1152]{5,4,0,1,2,3:T(8,128)(2,1)S(1)}, u32[]{:S(2)}, u32[]{:S(2)}) collective-permute-start(bf16[2,2,2,2,24,1152]{5,4,0,1,2,3:T(8,128)(2,1)S(1)} %pad_maximum_fusion.9), channel_id=1, source_target_pairs={{0,4},{4,0},{8,12},{12,8},{16,20},{20,16},{24,28},{28,24},{1,5},{5... | collective-permute-start | bytes 2654216 | tf_op jit(solution)/shard_map/ppermute | solution.py:251
  77.6 30.8 %collective-permute-start.23 = (bf16[2,2,2,96,768]{4,3,0,1,2:T(8,128)(2,1)}, bf16[2,2,2,96,768]{4,3,0,1,2:T(8,128)(2,1)}, u32[]{:S(2)}, u32[]{:S(2)}) collective-permute-start(bf16[2,2,2,96,768]{4,3,0,1,2:T(8,128)(2,1)} %pad_maximum_fusion.8), channel_id=1, source_target_pairs={{0,16},{4,20},{8,24},{12,28},{16,0},{20,4},{24,8},{28,12},{1,17},{... | collective-permute-start | bytes 3538952 | tf_op jit(solution)/shard_map/ppermute | solution.py:251
  84.0 28.1 %collective-permute-start.18 = (bf16[2,2,2,24,3072]{4,3,0,1,2:T(8,128)(2,1)}, bf16[2,2,2,24,3072]{4,3,0,1,2:T(8,128)(2,1)}, u32[]{:S(2)}, u32[]{:S(2)}) collective-permute-start(bf16[2,2,2,24,3072]{4,3,0,1,2:T(8,128)(2,1)} %pad_maximum_fusion.7), channel_id=1, source_target_pairs={{0,8},{4,12},{8,0},{12,4},{16,24},{20,28},{24,16},{28,20},{1,9},{5... | collective-permute-start | bytes 3538952 | tf_op jit(solution)/shard_map/ppermute | solution.py:251
  94.9 23.1 %all-to-all-start = ((bf16[8,128,576]{1,2,0:T(8,128)(2,1)}), bf16[8,128,576]{1,2,0:T(8,128)(2,1)}, u32[]{:S(2)}, u32[]{:S(2)}) async-start(bf16[8,128,576]{1,2,0:T(8,128)(2,1)} %bitcast.419), calls=%async_computation | async-start | bytes 2359296 | tf_op jit(solution)/shard_map/all_to_all | solution.py:227
  112.1 32.6 %collective-permute-start.24 = (bf16[2,2,2,2,96,768]{5,4,0,1,3,2:T(8,128)(2,1)}, bf16[2,2,2,2,96,768]{5,4,0,1,3,2:T(8,128)(2,1)}, u32[]{:S(2)}, u32[]{:S(2)}) collective-permute-start(bf16[2,2,2,2,96,768]{5,4,0,1,3,2:T(8,128)(2,1)} %pad_maximum_fusion.3), channel_id=1, source_target_pairs={{0,4},{4,0},{8,12},{12,8},{16,20},{20,16},{24,28},{28,24},{1,5},{5... | collective-permute-start | bytes 7077896 | tf_op jit(solution)/shard_map/ppermute | solution.py:251
  115.7 31.8 %collective-permute-start.19 = (bf16[2,2,2,2,24,3072]{5,4,0,1,2,3:T(8,128)(2,1)}, bf16[2,2,2,2,24,3072]{5,4,0,1,2,3:T(8,128)(2,1)}, u32[]{:S(2)}, u32[]{:S(2)}) collective-permute-start(bf16[2,2,2,2,24,3072]{5,4,0,1,2,3:T(8,128)(2,1)} %pad_maximum_fusion.2), channel_id=1, source_target_pairs={{0,4},{4,0},{8,12},{12,8},{16,20},{20,16},{24,28},{28,24},{1,5},{5... | collective-permute-start | bytes 7077896 | tf_op jit(solution)/shard_map/ppermute | solution.py:251
  128.3 14.0 %all-to-all-start.1 = ((bf16[8,128,192]{1,2,0:T(8,128)(2,1)}), bf16[8,128,192]{1,2,0:T(8,128)(2,1)S(1)}, u32[]{:S(2)}, u32[]{:S(2)}) async-start(bf16[8,128,192]{1,2,0:T(8,128)(2,1)} %copy.119), calls=%async_computation.1 | async-start | bytes 786432 | tf_op jit(solution)/shard_map/all_to_all | solution.py:234
  167.5 9.1 %collective-permute-start.47 = (bf16[2,2,2,24,768]{4,3,2,1,0:T(8,128)(2,1)S(1)}, bf16[2,2,2,24,768]{4,3,2,1,0:T(8,128)(2,1)S(1)}, u32[]{:S(2)}, u32[]{:S(2)}) collective-permute-start(bf16[2,2,2,24,768]{4,3,2,1,0:T(8,128)(2,1)S(1)} %dynamic-slice_bitcast_fusion.12), channel_id=1, source_target_pairs={{0,16},{4,20},{8,24},{12,28},{16,0},{20,4},{24,8},{28,12},{1,17},{... | collective-permute-start | bytes 884744 | tf_op jit(solution)/shard_map/ppermute | solution.py:251
  176.7 5.2 %collective-permute-start.48 = (bf16[2,2,24,768]{3,2,1,0:T(8,128)(2,1)S(1)}, bf16[2,2,24,768]{3,2,1,0:T(8,128)(2,1)S(1)}, u32[]{:S(2)}, u32[]{:S(2)}) collective-permute-start(bf16[2,2,24,768]{3,2,1,0:T(8,128)(2,1)S(1)} %dynamic-slice_bitcast_fusion.17), channel_id=1, source_target_pairs={{0,8},{4,12},{8,0},{12,4},{16,24},{20,28},{24,16},{28,20},{1,9},{5... | collective-permute-start | bytes 442376 | tf_op jit(solution)/shard_map/ppermute | solution.py:251
  182.0 5.7 %collective-permute-start.49 = (bf16[2,24,768]{2,1,0:T(8,128)(2,1)S(1)}, bf16[2,24,768]{2,1,0:T(8,128)(2,1)}, u32[]{:S(2)}, u32[]{:S(2)}) collective-permute-start(bf16[2,24,768]{2,1,0:T(8,128)(2,1)S(1)} %dynamic-slice_bitcast_fusion.20), channel_id=1, source_target_pairs={{0,1},{1,0},{2,3},{3,2},{4,5},{5,4},{6,7},{7,6},{8,9},{9,8},{10,11... | collective-permute-start | bytes 221192 | tf_op jit(solution)/shard_map/ppermute | solution.py:251
  184.1 11.9 %all-to-all-start.2 = ((bf16[8,128,192]{1,2,0:T(8,128)(2,1)}), bf16[8,128,192]{1,2,0:T(8,128)(2,1)S(1)}, u32[]{:S(2)}, u32[]{:S(2)}) async-start(bf16[8,128,192]{1,2,0:T(8,128)(2,1)} %bitcast.74), calls=%async_computation.2 | async-start | bytes 786432 | tf_op jit(solution)/shard_map/all_to_all | solution.py:227
  189.3 23.7 %collective-permute-start.50 = (bf16[24,768]{1,0:T(8,128)(2,1)}, bf16[24,768]{1,0:T(8,128)(2,1)}, u32[]{:S(2)}, u32[]{:S(2)}) collective-permute-start(bf16[24,768]{1,0:T(8,128)(2,1)} %dynamic-slice_bitcast_fusion.23), channel_id=1, source_target_pairs={{0,2},{1,3},{2,0},{3,1},{4,6},{5,7},{6,4},{7,5},{8,10},{9,11},{10,... | collective-permute-start | bytes 110600 | tf_op jit(solution)/shard_map/ppermute | solution.py:251
  208.7 26.8 %all-to-all-start.3 = ((bf16[8,128,576]{1,2,0:T(8,128)(2,1)}), bf16[8,128,576]{1,2,0:T(8,128)(2,1)S(1)}, u32[]{:S(2)}, u32[]{:S(2)}) async-start(bf16[8,128,576]{1,2,0:T(8,128)(2,1)} %copy.126), calls=%async_computation.3 | async-start | bytes 2359296 | tf_op jit(solution)/shard_map/all_to_all | solution.py:234
  213.8 15.7 %collective-permute-start.51 = (bf16[24,768]{1,0:T(8,128)(2,1)S(1)}, bf16[24,768]{1,0:T(8,128)(2,1)S(1)}, u32[]{:S(2)}, u32[]{:S(2)}) collective-permute-start(bf16[24,768]{1,0:T(8,128)(2,1)S(1)} %fusion.51), channel_id=1, source_target_pairs={{0,8},{4,12},{8,0},{12,4},{16,24},{20,28},{24,16},{28,20},{1,9},{5... | collective-permute-start | bytes 110600 | tf_op jit(solution)/shard_map/ppermute | solution.py:251
  221.2 45.9 %collective-permute-start.54 = (bf16[2,2,2,2,24,3072]{5,4,3,2,1,0:T(8,128)(2,1)}, bf16[2,2,2,2,24,3072]{5,4,3,2,1,0:T(8,128)(2,1)}, u32[]{:S(2)}, u32[]{:S(2)}) collective-permute-start(bf16[2,2,2,2,24,3072]{5,4,3,2,1,0:T(8,128)(2,1)} %dynamic-slice_bitcast_fusion.1), channel_id=1, source_target_pairs={{0,4},{4,0},{8,12},{12,8},{16,20},{20,16},{24,28},{28,24},{1,5},{5... | collective-permute-start | bytes 7077896 | tf_op jit(solution)/shard_map/ppermute | solution.py:251
  229.5 4.8 %collective-permute-start.52 = (bf16[2,24,768]{2,1,0:T(8,128)(2,1)S(1)}, bf16[2,24,768]{2,1,0:T(8,128)(2,1)S(1)}, u32[]{:S(2)}, u32[]{:S(2)}) collective-permute-start(bf16[2,24,768]{2,1,0:T(8,128)(2,1)S(1)} %pad_maximum_fusion.36), channel_id=1, source_target_pairs={{0,16},{4,20},{8,24},{12,28},{16,0},{20,4},{24,8},{28,12},{1,17},{... | collective-permute-start | bytes 221192 | tf_op jit(solution)/shard_map/ppermute | solution.py:251
  234.2 37.4 %collective-permute-start.62 = (bf16[2,2,2,2,96,768]{5,4,3,2,1,0:T(8,128)(2,1)}, bf16[2,2,2,2,96,768]{5,4,3,2,1,0:T(8,128)(2,1)}, u32[]{:S(2)}, u32[]{:S(2)}) collective-permute-start(bf16[2,2,2,2,96,768]{5,4,3,2,1,0:T(8,128)(2,1)} %dynamic-slice_bitcast_fusion), channel_id=1, source_target_pairs={{0,4},{4,0},{8,12},{12,8},{16,20},{20,16},{24,28},{28,24},{1,5},{5... | collective-permute-start | bytes 7077896 | tf_op jit(solution)/shard_map/ppermute | solution.py:251
  235.0 21.4 %collective-permute-start.53 = (bf16[2,2,24,768]{3,2,1,0:T(8,128)(2,1)}, bf16[2,2,24,768]{3,2,1,0:T(8,128)(2,1)}, u32[]{:S(2)}, u32[]{:S(2)}) collective-permute-start(bf16[2,2,24,768]{3,2,1,0:T(8,128)(2,1)} %pad_maximum_fusion.30), channel_id=1, source_target_pairs={{0,4},{4,0},{8,12},{12,8},{16,20},{20,16},{24,28},{28,24},{1,5},{5... | collective-permute-start | bytes 442376 | tf_op jit(solution)/shard_map/ppermute | solution.py:251
  250.4 4.6 %collective-permute-start.26 = (f32[1,2304]{1,0:T(1,128)S(1)}, f32[1,2304]{1,0:T(1,128)S(1)}, u32[]{:S(2)}, u32[]{:S(2)}) collective-permute-start(f32[1,2304]{1,0:T(1,128)S(1)} %fusion.54), channel_id=1, source_target_pairs={{0,2},{1,3},{2,0},{3,1},{4,6},{5,7},{6,4},{7,5},{8,10},{9,11},{10,... | collective-permute-start | bytes 27656 | tf_op jit(solution)/shard_map/ppermute | solution.py:251
  252.0 13.2 %collective-permute-start.38 = (bf16[2,2,2,2,24,1152]{5,4,3,2,1,0:T(8,128)(2,1)S(1)}, bf16[2,2,2,2,24,1152]{5,4,3,2,1,0:T(8,128)(2,1)S(1)}, u32[]{:S(2)}, u32[]{:S(2)}) collective-permute-start(bf16[2,2,2,2,24,1152]{5,4,3,2,1,0:T(8,128)(2,1)S(1)} %dynamic-slice_bitcast_fusion.4), channel_id=1, source_target_pairs={{0,4},{4,0},{8,12},{12,8},{16,20},{20,16},{24,28},{28,24},{1,5},{5... | collective-permute-start | bytes 2654216 | tf_op jit(solution)/shard_map/ppermute | solution.py:251
  256.2 9.9 %collective-permute-start.30 = (bf16[2,2,2,2,24,1152]{5,4,0,1,3,2:T(8,128)(2,1)S(1)}, bf16[2,2,2,2,24,1152]{5,4,0,1,3,2:T(8,128)(2,1)S(1)}, u32[]{:S(2)}, u32[]{:S(2)}) collective-permute-start(bf16[2,2,2,2,24,1152]{5,4,0,1,3,2:T(8,128)(2,1)S(1)} %bitcast.433), channel_id=1, source_target_pairs={{0,4},{4,0},{8,12},{12,8},{16,20},{20,16},{24,28},{28,24},{1,5},{5... | collective-permute-start | bytes 2654216 | tf_op jit(solution)/shard_map/ppermute | solution.py:251
  265.4 13.2 %collective-permute-start.39 = (bf16[2,2,2,24,1152]{4,3,2,1,0:T(8,128)(2,1)S(1)}, bf16[2,2,2,24,1152]{4,3,2,1,0:T(8,128)(2,1)S(1)}, u32[]{:S(2)}, u32[]{:S(2)}) collective-permute-start(bf16[2,2,2,24,1152]{4,3,2,1,0:T(8,128)(2,1)S(1)} %dynamic-slice_bitcast_fusion.8), channel_id=1, source_target_pairs={{0,8},{4,12},{8,0},{12,4},{16,24},{20,28},{24,16},{28,20},{1,9},{5... | collective-permute-start | bytes 1327112 | tf_op jit(solution)/shard_map/ppermute | solution.py:251
  266.4 13.0 %collective-permute-start.31 = (bf16[2,2,2,24,1152]{4,3,0,1,2:T(8,128)(2,1)S(1)}, bf16[2,2,2,24,1152]{4,3,0,1,2:T(8,128)(2,1)S(1)}, u32[]{:S(2)}, u32[]{:S(2)}) collective-permute-start(bf16[2,2,2,24,1152]{4,3,0,1,2:T(8,128)(2,1)S(1)} %dynamic-slice_bitcast_fusion.9), channel_id=1, source_target_pairs={{0,16},{4,20},{8,24},{12,28},{16,0},{20,4},{24,8},{28,12},{1,17},{... | collective-permute-start | bytes 1327112 | tf_op jit(solution)/shard_map/ppermute | solution.py:251
  270.2 60.0 %collective-permute-start.55 = (bf16[2,2,2,24,3072]{4,3,2,1,0:T(8,128)(2,1)S(1)}, bf16[2,2,2,24,3072]{4,3,2,1,0:T(8,128)(2,1)S(1)}, u32[]{:S(2)}, u32[]{:S(2)}) collective-permute-start(bf16[2,2,2,24,3072]{4,3,2,1,0:T(8,128)(2,1)S(1)} %dynamic-slice_bitcast_fusion.3), channel_id=1, source_target_pairs={{0,8},{4,12},{8,0},{12,4},{16,24},{20,28},{24,16},{28,20},{1,9},{5... | collective-permute-start | bytes 3538952 | tf_op jit(solution)/shard_map/ppermute | solution.py:251
  274.2 56.7 %collective-permute-start.63 = (bf16[2,2,2,96,768]{4,3,2,1,0:T(8,128)(2,1)S(1)}, bf16[2,2,2,96,768]{4,3,2,1,0:T(8,128)(2,1)S(1)}, u32[]{:S(2)}, u32[]{:S(2)}) collective-permute-start(bf16[2,2,2,96,768]{4,3,2,1,0:T(8,128)(2,1)S(1)} %dynamic-slice_bitcast_fusion.2), channel_id=1, source_target_pairs={{0,16},{4,20},{8,24},{12,28},{16,0},{20,4},{24,8},{28,12},{1,17},{... | collective-permute-start | bytes 3538952 | tf_op jit(solution)/shard_map/ppermute | solution.py:251
  278.8 27.6 %collective-permute-start.40 = (bf16[2,2,24,1152]{3,2,1,0:T(8,128)(2,1)S(1)}, bf16[2,2,24,1152]{3,2,1,0:T(8,128)(2,1)S(1)}, u32[]{:S(2)}, u32[]{:S(2)}) collective-permute-start(bf16[2,2,24,1152]{3,2,1,0:T(8,128)(2,1)S(1)} %dynamic-slice_bitcast_fusion.13), channel_id=1, source_target_pairs={{0,16},{4,20},{8,24},{12,28},{16,0},{20,4},{24,8},{28,12},{1,17},{... | collective-permute-start | bytes 663560 | tf_op jit(solution)/shard_map/ppermute | solution.py:251
  279.6 27.8 %collective-permute-start.32 = (bf16[2,2,24,1152]{3,2,0,1:T(8,128)(2,1)S(1)}, bf16[2,2,24,1152]{3,2,0,1:T(8,128)(2,1)S(1)}, u32[]{:S(2)}, u32[]{:S(2)}) collective-permute-start(bf16[2,2,24,1152]{3,2,0,1:T(8,128)(2,1)S(1)} %dynamic-slice_bitcast_fusion.14), channel_id=1, source_target_pairs={{0,8},{4,12},{8,0},{12,4},{16,24},{20,28},{24,16},{28,20},{1,9},{5... | collective-permute-start | bytes 663560 | tf_op jit(solution)/shard_map/ppermute | solution.py:251
  306.4 4.8 %collective-permute-start.41 = (bf16[2,24,1152]{2,1,0:T(8,128)(2,1)S(1)}, bf16[2,24,1152]{2,1,0:T(8,128)(2,1)S(1)}, u32[]{:S(2)}, u32[]{:S(2)}) collective-permute-start(bf16[2,24,1152]{2,1,0:T(8,128)(2,1)S(1)} %dynamic-slice_bitcast_fusion.18), channel_id=1, source_target_pairs={{0,1},{1,0},{2,3},{3,2},{4,5},{5,4},{6,7},{7,6},{8,9},{9,8},{10,11... | collective-permute-start | bytes 331784 | tf_op jit(solution)/shard_map/ppermute | solution.py:251
  307.5 6.1 %collective-permute-start.33 = (bf16[2,24,1152]{2,1,0:T(8,128)(2,1)S(1)}, bf16[2,24,1152]{2,1,0:T(8,128)(2,1)S(1)}, u32[]{:S(2)}, u32[]{:S(2)}) collective-permute-start(bf16[2,24,1152]{2,1,0:T(8,128)(2,1)S(1)} %dynamic-slice_bitcast_fusion.19), channel_id=1, source_target_pairs={{0,1},{1,0},{2,3},{3,2},{4,5},{5,4},{6,7},{7,6},{8,9},{9,8},{10,11... | collective-permute-start | bytes 331784 | tf_op jit(solution)/shard_map/ppermute | solution.py:251
  311.3 5.7 %collective-permute-start.42 = (bf16[24,1152]{1,0:T(8,128)(2,1)S(1)}, bf16[24,1152]{1,0:T(8,128)(2,1)S(1)}, u32[]{:S(2)}, u32[]{:S(2)}) collective-permute-start(bf16[24,1152]{1,0:T(8,128)(2,1)S(1)} %dynamic-slice_bitcast_fusion.21), channel_id=1, source_target_pairs={{0,2},{1,3},{2,0},{3,1},{4,6},{5,7},{6,4},{7,5},{8,10},{9,11},{10,... | collective-permute-start | bytes 165896 | tf_op jit(solution)/shard_map/ppermute | solution.py:251
  313.7 5.7 %collective-permute-start.34 = (bf16[24,1152]{1,0:T(8,128)(2,1)S(1)}, bf16[24,1152]{1,0:T(8,128)(2,1)S(1)}, u32[]{:S(2)}, u32[]{:S(2)}) collective-permute-start(bf16[24,1152]{1,0:T(8,128)(2,1)S(1)} %dynamic-slice_bitcast_fusion.22), channel_id=1, source_target_pairs={{0,2},{1,3},{2,0},{3,1},{4,6},{5,7},{6,4},{7,5},{8,10},{9,11},{10,... | collective-permute-start | bytes 165896 | tf_op jit(solution)/shard_map/ppermute | solution.py:251
  317.0 4.2 %collective-permute-start.43 = (bf16[24,1152]{1,0:T(8,128)(2,1)S(1)}, bf16[24,1152]{1,0:T(8,128)(2,1)S(1)}, u32[]{:S(2)}, u32[]{:S(2)}) collective-permute-start(bf16[24,1152]{1,0:T(8,128)(2,1)S(1)} %fusion.49), channel_id=1, source_target_pairs={{0,16},{4,20},{8,24},{12,28},{16,0},{20,4},{24,8},{28,12},{1,17},{... | collective-permute-start | bytes 165896 | tf_op jit(solution)/shard_map/ppermute | solution.py:251
  321.3 4.8 %collective-permute-start.44 = (bf16[2,24,1152]{2,1,0:T(8,128)(2,1)S(1)}, bf16[2,24,1152]{2,1,0:T(8,128)(2,1)S(1)}, u32[]{:S(2)}, u32[]{:S(2)}) collective-permute-start(bf16[2,24,1152]{2,1,0:T(8,128)(2,1)S(1)} %pad_maximum_fusion.34), channel_id=1, source_target_pairs={{0,8},{4,12},{8,0},{12,4},{16,24},{20,28},{24,16},{28,20},{1,9},{5... | collective-permute-start | bytes 331784 | tf_op jit(solution)/shard_map/ppermute | solution.py:251
  323.7 4.8 %collective-permute-start.36 = (bf16[2,24,1152]{2,1,0:T(8,128)(2,1)S(1)}, bf16[2,24,1152]{2,1,0:T(8,128)(2,1)S(1)}, u32[]{:S(2)}, u32[]{:S(2)}) collective-permute-start(bf16[2,24,1152]{2,1,0:T(8,128)(2,1)S(1)} %pad_maximum_fusion.33), channel_id=1, source_target_pairs={{0,16},{4,20},{8,24},{12,28},{16,0},{20,4},{24,8},{28,12},{1,17},{... | collective-permute-start | bytes 331784 | tf_op jit(solution)/shard_map/ppermute | solution.py:251
  330.6 15.4 %collective-permute-start.56 = (bf16[2,2,24,3072]{3,2,1,0:T(8,128)(2,1)S(1)}, bf16[2,2,24,3072]{3,2,1,0:T(8,128)(2,1)S(1)}, u32[]{:S(2)}, u32[]{:S(2)}) collective-permute-start(bf16[2,2,24,3072]{3,2,1,0:T(8,128)(2,1)S(1)} %dynamic-slice_bitcast_fusion.6), channel_id=1, source_target_pairs={{0,16},{4,20},{8,24},{12,28},{16,0},{20,4},{24,8},{28,12},{1,17},{... | collective-permute-start | bytes 1769480 | tf_op jit(solution)/shard_map/ppermute | solution.py:251
  331.5 15.4 %collective-permute-start.64 = (bf16[2,2,96,768]{3,2,1,0:T(8,128)(2,1)S(1)}, bf16[2,2,96,768]{3,2,1,0:T(8,128)(2,1)S(1)}, u32[]{:S(2)}, u32[]{:S(2)}) collective-permute-start(bf16[2,2,96,768]{3,2,1,0:T(8,128)(2,1)S(1)} %dynamic-slice_bitcast_fusion.5), channel_id=1, source_target_pairs={{0,8},{4,12},{8,0},{12,4},{16,24},{20,28},{24,16},{28,20},{1,9},{5... | collective-permute-start | bytes 1769480 | tf_op jit(solution)/shard_map/ppermute | solution.py:251
  346.3 10.0 %collective-permute-start.57 = (bf16[2,24,3072]{2,1,0:T(8,128)(2,1)S(1)}, bf16[2,24,3072]{2,1,0:T(8,128)(2,1)S(1)}, u32[]{:S(2)}, u32[]{:S(2)}) collective-permute-start(bf16[2,24,3072]{2,1,0:T(8,128)(2,1)S(1)} %dynamic-slice_bitcast_fusion.11), channel_id=1, source_target_pairs={{0,1},{1,0},{2,3},{3,2},{4,5},{5,4},{6,7},{7,6},{8,9},{9,8},{10,11... | collective-permute-start | bytes 884744 | tf_op jit(solution)/shard_map/ppermute | solution.py:251
  347.1 16.3 %collective-permute-start.65 = (bf16[2,96,768]{2,1,0:T(8,128)(2,1)S(1)}, bf16[2,96,768]{2,1,0:T(8,128)(2,1)S(1)}, u32[]{:S(2)}, u32[]{:S(2)}) collective-permute-start(bf16[2,96,768]{2,1,0:T(8,128)(2,1)S(1)} %dynamic-slice_bitcast_fusion.10), channel_id=1, source_target_pairs={{0,1},{1,0},{2,3},{3,2},{4,5},{5,4},{6,7},{7,6},{8,9},{9,8},{10,11... | collective-permute-start | bytes 884744 | tf_op jit(solution)/shard_map/ppermute | solution.py:251
  356.4 10.8 %collective-permute-start.58 = (bf16[24,3072]{1,0:T(8,128)(2,1)S(1)}, bf16[24,3072]{1,0:T(8,128)(2,1)S(1)}, u32[]{:S(2)}, u32[]{:S(2)}) collective-permute-start(bf16[24,3072]{1,0:T(8,128)(2,1)S(1)} %dynamic-slice_bitcast_fusion.16), channel_id=1, source_target_pairs={{0,2},{1,3},{2,0},{3,1},{4,6},{5,7},{6,4},{7,5},{8,10},{9,11},{10,... | collective-permute-start | bytes 442376 | tf_op jit(solution)/shard_map/ppermute | solution.py:251
  363.5 7.9 %collective-permute-start.66 = (bf16[96,768]{1,0:T(8,128)(2,1)S(1)}, bf16[96,768]{1,0:T(8,128)(2,1)S(1)}, u32[]{:S(2)}, u32[]{:S(2)}) collective-permute-start(bf16[96,768]{1,0:T(8,128)(2,1)S(1)} %dynamic-slice_bitcast_fusion.15), channel_id=1, source_target_pairs={{0,2},{1,3},{2,0},{3,1},{4,6},{5,7},{6,4},{7,5},{8,10},{9,11},{10,... | collective-permute-start | bytes 442376 | tf_op jit(solution)/shard_map/ppermute | solution.py:251
  367.3 5.5 %collective-permute-start.59 = (bf16[24,3072]{1,0:T(8,128)(2,1)S(1)}, bf16[24,3072]{1,0:T(8,128)(2,1)S(1)}, u32[]{:S(2)}, u32[]{:S(2)}) collective-permute-start(bf16[24,3072]{1,0:T(8,128)(2,1)S(1)} %fusion.42), channel_id=1, source_target_pairs={{0,16},{4,20},{8,24},{12,28},{16,0},{20,4},{24,8},{28,12},{1,17},{... | collective-permute-start | bytes 442376 | tf_op jit(solution)/shard_map/ppermute | solution.py:251
  371.4 6.8 %collective-permute-start.67 = (bf16[96,768]{1,0:T(8,128)(2,1)S(1)}, bf16[96,768]{1,0:T(8,128)(2,1)S(1)}, u32[]{:S(2)}, u32[]{:S(2)}) collective-permute-start(bf16[96,768]{1,0:T(8,128)(2,1)S(1)} %fusion.41), channel_id=1, source_target_pairs={{0,8},{4,12},{8,0},{12,4},{16,24},{20,28},{24,16},{28,20},{1,9},{5... | collective-permute-start | bytes 442376 | tf_op jit(solution)/shard_map/ppermute | solution.py:251
  372.8 10.0 %collective-permute-start.60 = (bf16[2,24,3072]{2,1,0:T(8,128)(2,1)S(1)}, bf16[2,24,3072]{2,1,0:T(8,128)(2,1)S(1)}, u32[]{:S(2)}, u32[]{:S(2)}) collective-permute-start(bf16[2,24,3072]{2,1,0:T(8,128)(2,1)S(1)} %pad_maximum_fusion.23), channel_id=1, source_target_pairs={{0,8},{4,12},{8,0},{12,4},{16,24},{20,28},{24,16},{28,20},{1,9},{5... | collective-permute-start | bytes 884744 | tf_op jit(solution)/shard_map/ppermute | solution.py:251
  378.4 6.8 %collective-permute-start.68 = (bf16[2,96,768]{2,1,0:T(8,128)(2,1)S(1)}, bf16[2,96,768]{2,1,0:T(8,128)(2,1)S(1)}, u32[]{:S(2)}, u32[]{:S(2)}) collective-permute-start(bf16[2,96,768]{2,1,0:T(8,128)(2,1)S(1)} %pad_maximum_fusion.24), channel_id=1, source_target_pairs={{0,16},{4,20},{8,24},{12,28},{16,0},{20,4},{24,8},{28,12},{1,17},{... | collective-permute-start | bytes 884744 | tf_op jit(solution)/shard_map/ppermute | solution.py:251
  (80 other events, 456.3 us)

commit v3 on v2

--- a/solution.py
+++ b/solution.py
@@ -251,8 +251,8 @@
     return lax.ppermute(array, axis_name, pairs)
 
 
-def halve(array, axis_name, lead, bits, order):
-    left = sorted(order, reverse=True)
+def halve(array, axis_name, lead, present, order):
+    left = sorted(present, reverse=True)
     for bit in order:
         dim = lead + left.index(bit)
         mine = (lax.axis_index(axis_name) >> bit) & 1
@@ -306,10 +306,33 @@
     share = rows // (places * shards)
     near = near.reshape((2,) * (z_bits + bits) + (share, width))
     order = bit_order(bits, turned)
-    near = halve(near, "ctx", z_bits, bits, order)
-    near = halve(near, "wsh", 0, z_bits, list(range(z_bits)))
+    near = halve(near, "ctx", z_bits, order, order)
+    return finish_sum(near, order)
+
+
+def can_stage(grad):
+    places, shards = lax.axis_size("ctx"), lax.axis_size("wsh")
+    return even_powers() and places >= 8 and grad.shape[0] % (8 * places * shards) == 0
+
+
+def start_sum(grad, order):
+    places, shards = lax.axis_size("ctx"), lax.axis_size("wsh")
+    z_bits = bit_count(shards)
+    share = grad.shape[0] // (places * shards)
+    near = grad.astype(jnp.bfloat16)
+    near = near.reshape((2,) * (z_bits + len(order)) + (share, grad.shape[1]))
+    return halve(near, "ctx", z_bits, order, order[:1])
+
+
+def more_sum(near, order, first, last):
+    return halve(near, "ctx", bit_count(lax.axis_size("wsh")), order[first:], order[first:last])
+
+
+def finish_sum(near, order):
+    z_bits = bit_count(lax.axis_size("wsh"))
+    near = halve(near, "wsh", 0, range(z_bits), list(range(z_bits)))
     near = double(near, "ctx", 0, order[::-1])
-    return near.reshape(rows // shards, width).astype(jnp.float32)
+    return near.reshape(-1, near.shape[-1]).astype(jnp.float32)
 
 
 def owned_vectors(stacked):
@@ -318,7 +341,7 @@
         return lax.dynamic_slice_in_dim(summed, lax.axis_index("wsh"), 1, 0)[0]
     z_bits = bit_count(lax.axis_size("wsh"))
     mine = stacked.reshape((2,) * z_bits + (1, stacked.shape[1]))
-    mine = halve(mine, "wsh", 0, z_bits, list(range(z_bits)))
+    mine = halve(mine, "wsh", 0, range(z_bits), list(range(z_bits)))
     for bit in range(bit_count(lax.axis_size("ctx"))):
         mine = mine + swap(mine, "ctx", bit)
     return mine[0]
@@ -610,9 +633,22 @@
     grad_attended = jnp.einsum(
         "sro,io->sri", grad_branch, whole_out, preferred_element_type=jnp.float32
     ).astype(jnp.bfloat16)
+    staged = by_heads and can_stage(grad_up) and can_stage(grad_down)
+    if staged:
+        up_order = bit_order(bit_count(places), False)
+        down_order = bit_order(bit_count(places), True)
+        grad_attended, part_up, part_down = lax.optimization_barrier(
+            (grad_attended, start_sum(grad_up, up_order), start_sum(grad_down, down_order))
+        )
     if by_heads:
         grad_back = spread_out(grad_attended, seq_count, groups, 1)
         grad_head_rows = attend_back(order, head_rows, grad_back, exact, lse, head_size, block_len)
+        if staged:
+            part_up = more_sum(part_up, up_order, 1, 2)
+            part_down = more_sum(part_down, down_order, 1, 2)
+            grad_head_rows, part_up, part_down = lax.optimization_barrier(
+                (grad_head_rows, part_up, part_down)
+            )
         grad_rows = bring_back(grad_head_rows, seq_count, groups, 3)
     else:
         grad_rows = loop_attend_back(
@@ -629,6 +665,12 @@
     )
     grad_input_part, grad_ln1_gain, grad_ln1_bias = ln_one_back(grad_normed)
     grad_input = grad_middle + grad_input_part
+    if staged:
+        own_up = finish_sum(more_sum(part_up, up_order, 2, len(up_order)), up_order)
+        own_down = finish_sum(more_sum(part_down, down_order, 2, len(down_order)), down_order)
+    else:
+        own_up = owned_gradient(grad_up)
+        own_down = owned_gradient(grad_down, True)
     vectors = (
         grad_ln1_gain, grad_ln1_bias, grad_bias_query, grad_bias_value, grad_bias_out,
         grad_ln2_gain, grad_ln2_bias, grad_bias_down, grad_bias_up,
@@ -664,9 +706,9 @@
         own_bias_out,
         own_ln2_gain,
         own_ln2_bias,
-        owned_gradient(grad_up),
+        own_up,
         own_bias_up,
-        owned_gradient(grad_down, True),
+        own_down,
         own_bias_down,
     )
 

time: 396 us -> 424 us (1.071)
  waiting for transfers between devices: 152 us -> 171 us
  other arithmetic: 41.2 us -> 50.2 us
  matrix products: 31.8 us -> 25.4 us
    ppermute x70, waiting for transfers between devices: 144 us -> 164 us  [swap(): return lax.ppermute(array, axis_name, pairs)]
    convert_element_type x25, other arithmetic: 11 us -> 19.9 us  [halve(): (kept.astype(jnp.float32) + came.astype(jnp.float32)).astype(array.dtype)]
    unnamed x142 -> x152, local copies, waits for them, and re-layouts: 10.6 us -> 13.6 us
  transfers between devices with their start and end apart: 74 -> 74, of which waited for: 42 -> 37; matrix products, arithmetic and copies ran while one was open for 24% -> 24% of each run, Pallas kernels for 4% -> 4%
where the time goes in v3:
time: 424 us; the launch traced here: 417 us
  waiting for transfers between devices  171 us (40%)
  starting transfers between devices  81.4 us (19%)
  local copies, waits for them, and re-layouts  53.1 us (13%)
  other arithmetic  50.2 us (12%)
  matrix products  25.4 us (6%)
  blocking collectives  18.5 us (4%)
  Pallas kernels  14.6 us (3%)
    ppermute x70, waiting for transfers between devices, swap(): return lax.ppermute(array, axis_name, pairs)  164 us
    ppermute x70, starting transfers between devices, swap(): return lax.ppermute(array, axis_name, pairs)  63.7 us
    another operation x77, other arithmetic, double(): jnp.stack([jnp.where(first, array, came), jnp.where(first, came, array)],...  23.1 us
    convert_element_type x25, other arithmetic, halve(): (kept.astype(jnp.float32) + came.astype(jnp.float32)).astype(array.dtype)  19.9 us
    all_gather x1, blocking collectives, body(): lax.all_gather(jnp.concatenate(small).reshape(1, -1), 'wsh', axis=0, tile...  18.5 us
    unnamed x152, local copies, waits for them, and re-layouts  13.6 us
    squeeze x26, local copies, waits for them, and re-layouts, halve(): away = lax.dynamic_index_in_dim(array, 1 - mine, dim, keepdims=False)  11 us
    all_to_all x2, starting transfers between devices, bring_back(): lax.all_to_all(array.reshape(places, row_count, parts * width), 'ctx', 0,...  9.51 us
  transfers between devices with their start and end apart: 74, of which 37 were waited for; matrix products, arithmetic and copies ran while one was open for 24% of the time, Pallas kernels for 4%

profile of v3, /device:TPU:0, one launch (start us, length us, event | category | flops | bytes accessed | tf_op | source)
XLA Modules:
  0.0 417.0 jit_solution(7677808885285150229)
XLA Ops:
  2.1 4.1 collective-permute-start.5
  7.0 2.8 collective-permute-start.10
  11.9 2.9 collective-permute-start.15
  14.9 18.5 %all-gather.1 = bf16[4,1,2304]{2,1,0:T(2,128)(2,1)S(1)} all-gather(bf16[1,1,2304]{2,1,0:T(2,128)(2,1)S(1)} %reshape.350), channel_id=2, replica_groups=mesh['ctx'=8,'wsh'=4] {'wsh'}, dimensions={0}, use_global_device_ids=true | all-gather | bytes 23040 | tf_op jit(solution)/shard_map/all_gather | solution.py:542
  37.8 2.1 collective-permute-start.6
  40.0 2.2 collective-permute-done.11
  48.1 1.6 collective-permute-start.7
  51.0 4.7 %collective-permute-done.7 = bf16[2,2,24,1152]{3,2,0,1:T(8,128)(2,1)S(1)} collective-permute-done((bf16[2,2,24,1152]{3,2,0,1:T(8,128)(2,1)S(1)}, bf16[2,2,24,1152]{3,2,0,1:T(8,128)(2,1)S(1)}, u32[]{:S(2)}, u32[]{:S(2)}) %collective-permute-start.7) | collective-permute-done | bytes 221216 | tf_op jit(solution)/shard_map/ppermute | solution.py:251
  56.6 1.6 collective-permute-done.2
  63.0 6.0 %collective-permute-done.8 = bf16[2,2,2,24,1152]{4,3,0,1,2:T(8,128)(2,1)S(1)} collective-permute-done((bf16[2,2,2,24,1152]{4,3,0,1,2:T(8,128)(2,1)S(1)}, bf16[2,2,2,24,1152]{4,3,0,1,2:T(8,128)(2,1)S(1)}, u32[]{:S(2)}, u32[]{:S(2)}) %collective-permute-start.8) | collective-permute-done | bytes 442400 | tf_op jit(solution)/shard_map/ppermute | solution.py:251
  69.2 2.2 collective-permute-done.3
  71.7 4.6 %collective-permute-done.22 = bf16[2,2,96,768]{3,2,0,1:T(8,128)(2,1)S(1)} collective-permute-done((bf16[2,2,96,768]{3,2,0,1:T(8,128)(2,1)S(1)}, bf16[2,2,96,768]{3,2,0,1:T(8,128)(2,1)S(1)}, u32[]{:S(2)}, u32[]{:S(2)}) %collective-permute-start.22) | collective-permute-done | bytes 589856 | tf_op jit(solution)/shard_map/ppermute | solution.py:251
  79.0 3.8 collective-permute-done.17
  88.1 2.2 fusion.2
  90.4 1.7 copy.116
  93.2 4.6 %all-to-all-start = ((bf16[8,128,576]{1,2,0:T(8,128)(2,1)}), bf16[8,128,576]{1,2,0:T(8,128)(2,1)}, u32[]{:S(2)}, u32[]{:S(2)}) async-start(bf16[8,128,576]{1,2,0:T(8,128)(2,1)} %bitcast.26), calls=%async_computation | async-start | bytes 2359296 | tf_op jit(solution)/shard_map/all_to_all | solution.py:227
  97.8 12.0 %collective-permute-done.23 = bf16[2,2,2,96,768]{4,3,0,1,2:T(8,128)(2,1)} collective-permute-done((bf16[2,2,2,96,768]{4,3,0,1,2:T(8,128)(2,1)}, bf16[2,2,2,96,768]{4,3,0,1,2:T(8,128)(2,1)}, u32[]{:S(2)}, u32[]{:S(2)}) %collective-permute-start.23) | collective-permute-done | bytes 1179680 | tf_op jit(solution)/shard_map/ppermute | solution.py:251
  111.3 1.6 pad_maximum_fusion.3
  114.6 1.8 pad_maximum_fusion.2
  118.1 1.7 copy.118
  119.8 5.9 %shard_map.271 = (bf16[1024,192]{1,0:T(8,128)(2,1)S(1)}, f32[1024,192]{1,0:T(8,128)S(1)}, f32[1024,128]{1,0:T(8,128)S(1)}) custom-call(s32[16]{0:T(128)S(1)} %fusion.57.order_ref, bf16[1024,576]{1,0:T(8,128)(2,1)S(1)} %bitcast.393), custom_call_target="tpu_custom_call" | custom-call | tf_op jit(solution)/shard_map/pallas_call | solution.py:186
  128.5 5.6 %all-to-all-start.1 = ((bf16[8,128,192]{1,2,0:T(8,128)(2,1)}), bf16[8,128,192]{1,2,0:T(8,128)(2,1)S(1)}, u32[]{:S(2)}, u32[]{:S(2)}) async-start(bf16[8,128,192]{1,2,0:T(8,128)(2,1)} %copy.119), calls=%async_computation.1 | async-start | bytes 786432 | tf_op jit(solution)/shard_map/all_to_all | solution.py:234
  136.6 5.7 %all-to-all-done.1 = bf16[8,128,192]{1,2,0:T(8,128)(2,1)S(1)} async-done(((bf16[8,128,192]{1,2,0:T(8,128)(2,1)}), bf16[8,128,192]{1,2,0:T(8,128)(2,1)S(1)}, u32[]{:S(2)}, u32[]{:S(2)}) %all-to-all-start.1) | async-done | bytes 393248 | tf_op jit(solution)/shard_map/all_to_all | solution.py:234
  142.3 2.0 fusion.68
  144.7 2.0 select_bitcast_fusion.1
  149.4 2.0 select_bitcast_fusion.3
  154.1 3.8 convert_reduce_fusion
  157.8 2.2 multiply_reduce_fusion
  161.9 1.6 bitcast_convert_fusion.1
  163.5 1.7 dynamic-slice_bitcast_fusion.1
  168.5 2.3 bitcast_convert_fusion
  173.7 3.6 collective-permute-done.51
  179.7 4.7 %collective-permute-done.52 = bf16[2,2,24,768]{3,2,1,0:T(8,128)(2,1)} collective-permute-done((bf16[2,2,24,768]{3,2,1,0:T(8,128)(2,1)S(1)}, bf16[2,2,24,768]{3,2,1,0:T(8,128)(2,1)}, u32[]{:S(2)}, u32[]{:S(2)}) %collective-permute-start.52) | collective-permute-done | bytes 147488 | tf_op jit(solution)/shard_map/ppermute | solution.py:251
  187.3 2.6 collective-permute-done.53
  190.6 3.6 fusion.1
  194.2 4.6 %fusion = bf16[2,2,2,2,96,768]{5,4,3,2,1,0:T(8,128)(2,1)} fusion(bf16[2,2,2,2,96,768]{5,4,3,2,1,0:T(8,128)(2,1)} %collective-permute-done.26, bf16[2,2,2,2,2,96,768]{6,5,4,3,2,1,0:T(8,128)(2,1)S(1)} %bitcast.410, s32[]{:T(128)S(6)} %select_n.617), kind=kLoop, calls=%fused_computation.6 | loop fusion | flops 4718592 | bytes 7077892 | tf_op jit(solution)/shard_map/convert_element_type | solution.py:262
  202.1 23.2 %collective-permute-done.55 = bf16[24,768]{1,0:T(8,128)(2,1)S(1)} collective-permute-done((bf16[24,768]{1,0:T(8,128)(2,1)S(1)}, bf16[24,768]{1,0:T(8,128)(2,1)S(1)}, u32[]{:S(2)}, u32[]{:S(2)}) %collective-permute-start.55) | collective-permute-done | bytes 36896 | tf_op jit(solution)/shard_map/ppermute | solution.py:251
  225.3 2.4 dynamic-slice_bitcast_fusion.2
  231.3 3.7 all-to-all-start.2
  235.0 21.1 %collective-permute-done.56 = bf16[2,24,768]{2,1,0:T(8,128)(2,1)S(1)} collective-permute-done((bf16[2,24,768]{2,1,0:T(8,128)(2,1)S(1)}, bf16[2,24,768]{2,1,0:T(8,128)(2,1)S(1)}, u32[]{:S(2)}, u32[]{:S(2)}) %collective-permute-start.56) | collective-permute-done | bytes 73760 | tf_op jit(solution)/shard_map/ppermute | solution.py:251
  259.7 8.7 %shard_map.272 = bf16[1024,576]{1,0:T(8,128)(2,1)S(1)} custom-call(s32[16]{0:T(128)S(1)} %fusion.57.order_ref, bf16[1024,576]{1,0:T(8,128)(2,1)S(1)} %bitcast.394, bf16[1024,192]{1,0:T(8,128)(2,1)S(1)} %bitcast.396, f32[1024,192]{1,0:T(8,128)S(1)} %copy-done.1, f32[1024,128]{1,0:T(8,128)S(1)} %copy-done.3), custom_call_target="tpu_custom_call" | custom-call | tf_op jit(solution)/shard_map/pallas_call | solution.py:206
  268.4 1.8 fusion.11
  270.4 3.1 fusion.10
  275.0 5.0 %fusion.17 = bf16[2,128,768]{2,1,0:T(8,128)(2,1)} fusion(f32[2,128,768]{2,1,0:T(8,128)S(1)} %copy-done.6, bf16[3072,768,1]{1,0,2:T(8,128)(2,1)} %bitcast.414, f32[768]{0:T(1024)S(1)} %copy-done.64, f32[2,128,3072]{2,1,0:T(8,128)S(1)} %copy-done.31), kind=kOutput, calls=%fused_computation.50 | convolution fusion | flops 1215627264 | bytes 9047040 | tf_op jit(solution)/shard_map/dot_general | solution.py:612
  285.4 3.9 all-to-all-start.3
  289.4 2.0 collective-permute-start.64
  294.1 23.6 %collective-permute-done.64 = bf16[2,2,96,768]{3,2,1,0:T(8,128)(2,1)S(1)} collective-permute-done((bf16[2,2,96,768]{3,2,1,0:T(8,128)(2,1)S(1)}, bf16[2,2,96,768]{3,2,1,0:T(8,128)(2,1)S(1)}, u32[]{:S(2)}, u32[]{:S(2)}) %collective-permute-start.64) | collective-permute-done | bytes 589856 | tf_op jit(solution)/shard_map/ppermute | solution.py:251
  321.9 7.9 %collective-permute-done.65 = bf16[2,96,768]{2,1,0:T(8,128)(2,1)S(1)} collective-permute-done((bf16[2,96,768]{2,1,0:T(8,128)(2,1)S(1)}, bf16[2,96,768]{2,1,0:T(8,128)(2,1)S(1)}, u32[]{:S(2)}, u32[]{:S(2)}) %collective-permute-start.65) | collective-permute-done | bytes 294944 | tf_op jit(solution)/shard_map/ppermute | solution.py:251
  332.6 1.8 fusion.60
  342.0 2.1 collective-permute-start.29
  345.9 2.5 collective-permute-start.30
  348.5 2.0 collective-permute-done.30
  362.2 2.0 collective-permute-done.67
  364.4 5.2 %collective-permute-done.62 = bf16[2,24,3072]{2,1,0:T(8,128)(2,1)S(1)} collective-permute-done((bf16[2,24,3072]{2,1,0:T(8,128)(2,1)S(1)}, bf16[2,24,3072]{2,1,0:T(8,128)(2,1)S(1)}, u32[]{:S(2)}, u32[]{:S(2)}) %collective-permute-start.62) | collective-permute-done | bytes 294944 | tf_op jit(solution)/shard_map/ppermute | solution.py:251
  376.8 7.4 %collective-permute-done.43 = bf16[2,2,2,24,1152]{4,3,2,1,0:T(8,128)(2,1)S(1)} collective-permute-done((bf16[2,2,2,24,1152]{4,3,2,1,0:T(8,128)(2,1)S(1)}, bf16[2,2,2,24,1152]{4,3,2,1,0:T(8,128)(2,1)S(1)}, u32[]{:S(2)}, u32[]{:S(2)}) %collective-permute-start.43) | collective-permute-done | bytes 442400 | tf_op jit(solution)/shard_map/ppermute | solution.py:251
  386.5 5.0 %collective-permute-done.44 = bf16[2,2,24,1152]{3,2,1,0:T(8,128)(2,1)S(1)} collective-permute-done((bf16[2,2,24,1152]{3,2,1,0:T(8,128)(2,1)S(1)}, bf16[2,2,24,1152]{3,2,1,0:T(8,128)(2,1)S(1)}, u32[]{:S(2)}, u32[]{:S(2)}) %collective-permute-start.44) | collective-permute-done | bytes 221216 | tf_op jit(solution)/shard_map/ppermute | solution.py:251
  391.6 2.1 collective-permute-start.45
  394.0 3.3 collective-permute-done.45
  397.4 1.7 collective-permute-start.46
  400.7 1.8 collective-permute-done.46
  405.1 1.7 collective-permute-done.47
  406.8 1.6 collective-permute-start.48
  409.1 2.5 collective-permute-done.48
  411.8 1.6 collective-permute-done.40
  (458 shorter events, 126.9 us)
Async XLA Ops:
  2.1 35.7 %collective-permute-start.5 = (bf16[24,1152]{1,0:T(8,128)(2,1)S(1)}, bf16[24,1152]{1,0:T(8,128)(2,1)S(1)}, u32[]{:S(2)}, u32[]{:S(2)}) collective-permute-start(bf16[24,1152]{1,0:T(8,128)(2,1)S(1)} %constant_dynamic-slice_fusion.7), channel_id=1, source_target_pairs={{0,2},{1,3},{2,0},{3,1},{4,6},{5,7},{6,4},{7,5},{8,10},{9,11},{10,... | collective-permute-start | bytes 165896 | tf_op jit(solution)/shard_map/ppermute | solution.py:251
  6.2 33.7 %collective-permute-start = (bf16[24,1152]{1,0:T(8,128)(2,1)S(1)}, bf16[24,1152]{1,0:T(8,128)(2,1)S(1)}, u32[]{:S(2)}, u32[]{:S(2)}) collective-permute-start(bf16[24,1152]{1,0:T(8,128)(2,1)S(1)} %constant_dynamic-slice_fusion.8), channel_id=1, source_target_pairs={{0,2},{1,3},{2,0},{3,1},{4,6},{5,7},{6,4},{7,5},{8,10},{9,11},{10,... | collective-permute-start | bytes 165896 | tf_op jit(solution)/shard_map/ppermute | solution.py:251
  7.0 29.8 %collective-permute-start.10 = (bf16[24,768]{1,0:T(8,128)(2,1)S(1)}, bf16[24,768]{1,0:T(8,128)(2,1)S(1)}, u32[]{:S(2)}, u32[]{:S(2)}) collective-permute-start(bf16[24,768]{1,0:T(8,128)(2,1)S(1)} %constant_dynamic-slice_fusion.6), channel_id=1, source_target_pairs={{0,2},{1,3},{2,0},{3,1},{4,6},{5,7},{6,4},{7,5},{8,10},{9,11},{10,... | collective-permute-start | bytes 110600 | tf_op jit(solution)/shard_map/ppermute | solution.py:251
  10.8 33.0 %collective-permute-start.20 = (bf16[96,768]{1,0:T(8,128)(2,1)S(1)}, bf16[96,768]{1,0:T(8,128)(2,1)S(1)}, u32[]{:S(2)}, u32[]{:S(2)}) collective-permute-start(bf16[96,768]{1,0:T(8,128)(2,1)S(1)} %constant_dynamic-slice_fusion.4), channel_id=1, source_target_pairs={{0,2},{1,3},{2,0},{3,1},{4,6},{5,7},{6,4},{7,5},{8,10},{9,11},{10,... | collective-permute-start | bytes 442376 | tf_op jit(solution)/shard_map/ppermute | solution.py:251
  11.9 33.7 %collective-permute-start.15 = (bf16[24,3072]{1,0:T(8,128)(2,1)S(1)}, bf16[24,3072]{1,0:T(8,128)(2,1)S(1)}, u32[]{:S(2)}, u32[]{:S(2)}) collective-permute-start(bf16[24,3072]{1,0:T(8,128)(2,1)S(1)} %constant_dynamic-slice_fusion.5), channel_id=1, source_target_pairs={{0,2},{1,3},{2,0},{3,1},{4,6},{5,7},{6,4},{7,5},{8,10},{9,11},{10,... | collective-permute-start | bytes 442376 | tf_op jit(solution)/shard_map/ppermute | solution.py:251
  37.7 4.5 %collective-permute-start.11 = (bf16[2,24,768]{2,1,0:T(8,128)(2,1)S(1)}, bf16[2,24,768]{2,1,0:T(8,128)(2,1)S(1)}, u32[]{:S(2)}, u32[]{:S(2)}) collective-permute-start(bf16[2,24,768]{2,1,0:T(8,128)(2,1)S(1)} %pad_maximum_fusion.35), channel_id=1, source_target_pairs={{0,1},{1,0},{2,3},{3,2},{4,5},{5,4},{6,7},{7,6},{8,9},{9,8},{10,11... | collective-permute-start | bytes 221192 | tf_op jit(solution)/shard_map/ppermute | solution.py:251
  37.8 10.2 %collective-permute-start.6 = (bf16[2,24,1152]{2,1,0:T(8,128)(2,1)S(1)}, bf16[2,24,1152]{2,1,0:T(8,128)(2,1)S(1)}, u32[]{:S(2)}, u32[]{:S(2)}) collective-permute-start(bf16[2,24,1152]{2,1,0:T(8,128)(2,1)S(1)} %pad_maximum_fusion.32), channel_id=1, source_target_pairs={{0,1},{1,0},{2,3},{3,2},{4,5},{5,4},{6,7},{7,6},{8,9},{9,8},{10,11... | collective-permute-start | bytes 331784 | tf_op jit(solution)/shard_map/ppermute | solution.py:251
  40.0 9.7 %collective-permute-start.1 = (bf16[2,24,1152]{2,1,0:T(8,128)(2,1)S(1)}, bf16[2,24,1152]{2,1,0:T(8,128)(2,1)S(1)}, u32[]{:S(2)}, u32[]{:S(2)}) collective-permute-start(bf16[2,24,1152]{2,1,0:T(8,128)(2,1)S(1)} %pad_maximum_fusion.31), channel_id=1, source_target_pairs={{0,1},{1,0},{2,3},{3,2},{4,5},{5,4},{6,7},{7,6},{8,9},{9,8},{10,11... | collective-permute-start | bytes 331784 | tf_op jit(solution)/shard_map/ppermute | solution.py:251
  42.3 8.1 %collective-permute-start.12 = (bf16[2,2,24,768]{3,2,0,1:T(8,128)(2,1)S(1)}, bf16[2,2,24,768]{3,2,0,1:T(8,128)(2,1)S(1)}, u32[]{:S(2)}, u32[]{:S(2)}) collective-permute-start(bf16[2,2,24,768]{3,2,0,1:T(8,128)(2,1)S(1)} %pad_maximum_fusion.29), channel_id=1, source_target_pairs={{0,8},{4,12},{8,0},{12,4},{16,24},{20,28},{24,16},{28,20},{1,9},{5... | collective-permute-start | bytes 442376 | tf_op jit(solution)/shard_map/ppermute | solution.py:251
  44.8 13.9 %collective-permute-start.21 = (bf16[2,96,768]{2,1,0:T(8,128)(2,1)S(1)}, bf16[2,96,768]{2,1,0:T(8,128)(2,1)S(1)}, u32[]{:S(2)}, u32[]{:S(2)}) collective-permute-start(bf16[2,96,768]{2,1,0:T(8,128)(2,1)S(1)} %pad_maximum_fusion.22), channel_id=1, source_target_pairs={{0,1},{1,0},{2,3},{3,2},{4,5},{5,4},{6,7},{7,6},{8,9},{9,8},{10,11... | collective-permute-start | bytes 884744 | tf_op jit(solution)/shard_map/ppermute | solution.py:251
  46.6 13.6 %collective-permute-start.16 = (bf16[2,24,3072]{2,1,0:T(8,128)(2,1)S(1)}, bf16[2,24,3072]{2,1,0:T(8,128)(2,1)S(1)}, u32[]{:S(2)}, u32[]{:S(2)}) collective-permute-start(bf16[2,24,3072]{2,1,0:T(8,128)(2,1)S(1)} %pad_maximum_fusion.21), channel_id=1, source_target_pairs={{0,1},{1,0},{2,3},{3,2},{4,5},{5,4},{6,7},{7,6},{8,9},{9,8},{10,11... | collective-permute-start | bytes 884744 | tf_op jit(solution)/shard_map/ppermute | solution.py:251
  48.1 7.6 %collective-permute-start.7 = (bf16[2,2,24,1152]{3,2,0,1:T(8,128)(2,1)S(1)}, bf16[2,2,24,1152]{3,2,0,1:T(8,128)(2,1)S(1)}, u32[]{:S(2)}, u32[]{:S(2)}) collective-permute-start(bf16[2,2,24,1152]{3,2,0,1:T(8,128)(2,1)S(1)} %pad_maximum_fusion.26), channel_id=1, source_target_pairs={{0,16},{4,20},{8,24},{12,28},{16,0},{20,4},{24,8},{28,12},{1,17},{... | collective-permute-start | bytes 663560 | tf_op jit(solution)/shard_map/ppermute | solution.py:251
  49.7 8.4 %collective-permute-start.2 = (bf16[2,2,24,1152]{3,2,0,1:T(8,128)(2,1)S(1)}, bf16[2,2,24,1152]{3,2,0,1:T(8,128)(2,1)S(1)}, u32[]{:S(2)}, u32[]{:S(2)}) collective-permute-start(bf16[2,2,24,1152]{3,2,0,1:T(8,128)(2,1)S(1)} %pad_maximum_fusion.25), channel_id=1, source_target_pairs={{0,8},{4,12},{8,0},{12,4},{16,24},{20,28},{24,16},{28,20},{1,9},{5... | collective-permute-start | bytes 663560 | tf_op jit(solution)/shard_map/ppermute | solution.py:251
  50.4 11.6 %collective-permute-start.13 = (bf16[2,2,2,24,768]{4,3,0,1,2:T(8,128)(2,1)S(1)}, bf16[2,2,2,24,768]{4,3,0,1,2:T(8,128)(2,1)S(1)}, u32[]{:S(2)}, u32[]{:S(2)}) collective-permute-start(bf16[2,2,2,24,768]{4,3,0,1,2:T(8,128)(2,1)S(1)} %pad_maximum_fusion.20), channel_id=1, source_target_pairs={{0,16},{4,20},{8,24},{12,28},{16,0},{20,4},{24,8},{28,12},{1,17},{... | collective-permute-start | bytes 884744 | tf_op jit(solution)/shard_map/ppermute | solution.py:251
  55.8 13.2 %collective-permute-start.8 = (bf16[2,2,2,24,1152]{4,3,0,1,2:T(8,128)(2,1)S(1)}, bf16[2,2,2,24,1152]{4,3,0,1,2:T(8,128)(2,1)S(1)}, u32[]{:S(2)}, u32[]{:S(2)}) collective-permute-start(bf16[2,2,2,24,1152]{4,3,0,1,2:T(8,128)(2,1)S(1)} %pad_maximum_fusion.17), channel_id=1, source_target_pairs={{0,8},{4,12},{8,0},{12,4},{16,24},{20,28},{24,16},{28,20},{1,9},{5... | collective-permute-start | bytes 1327112 | tf_op jit(solution)/shard_map/ppermute | solution.py:251
  58.3 13.2 %collective-permute-start.3 = (bf16[2,2,2,24,1152]{4,3,0,1,2:T(8,128)(2,1)S(1)}, bf16[2,2,2,24,1152]{4,3,0,1,2:T(8,128)(2,1)S(1)}, u32[]{:S(2)}, u32[]{:S(2)}) collective-permute-start(bf16[2,2,2,24,1152]{4,3,0,1,2:T(8,128)(2,1)S(1)} %pad_maximum_fusion.16), channel_id=1, source_target_pairs={{0,16},{4,20},{8,24},{12,28},{16,0},{20,4},{24,8},{28,12},{1,17},{... | collective-permute-start | bytes 1327112 | tf_op jit(solution)/shard_map/ppermute | solution.py:251
  58.8 17.5 %collective-permute-start.22 = (bf16[2,2,96,768]{3,2,0,1:T(8,128)(2,1)S(1)}, bf16[2,2,96,768]{3,2,0,1:T(8,128)(2,1)S(1)}, u32[]{:S(2)}, u32[]{:S(2)}) collective-permute-start(bf16[2,2,96,768]{3,2,0,1:T(8,128)(2,1)S(1)} %pad_maximum_fusion.13), channel_id=1, source_target_pairs={{0,8},{4,12},{8,0},{12,4},{16,24},{20,28},{24,16},{28,20},{1,9},{5... | collective-permute-start | bytes 1769480 | tf_op jit(solution)/shard_map/ppermute | solution.py:251
  60.4 22.5 %collective-permute-start.17 = (bf16[2,2,24,3072]{3,2,0,1:T(8,128)(2,1)S(1)}, bf16[2,2,24,3072]{3,2,0,1:T(8,128)(2,1)S(1)}, u32[]{:S(2)}, u32[]{:S(2)}) collective-permute-start(bf16[2,2,24,3072]{3,2,0,1:T(8,128)(2,1)S(1)} %pad_maximum_fusion.12), channel_id=1, source_target_pairs={{0,16},{4,20},{8,24},{12,28},{16,0},{20,4},{24,8},{28,12},{1,17},{... | collective-permute-start | bytes 1769480 | tf_op jit(solution)/shard_map/ppermute | solution.py:251
  63.0 71.1 %collective-permute-start.14 = (bf16[2,2,2,2,24,768]{5,4,0,1,3,2:T(8,128)(2,1)}, bf16[2,2,2,2,24,768]{5,4,0,1,3,2:T(8,128)(2,1)}, u32[]{:S(2)}, u32[]{:S(2)}) collective-permute-start(bf16[2,2,2,2,24,768]{5,4,0,1,3,2:T(8,128)(2,1)} %pad_maximum_fusion.11), channel_id=1, source_target_pairs={{0,4},{4,0},{8,12},{12,8},{16,20},{20,16},{24,28},{28,24},{1,5},{5... | collective-permute-start | bytes 1769480 | tf_op jit(solution)/shard_map/ppermute | solution.py:251
  69.1 16.4 %collective-permute-start.9 = (bf16[2,2,2,2,24,1152]{5,4,0,1,2,3:T(8,128)(2,1)S(1)}, bf16[2,2,2,2,24,1152]{5,4,0,1,2,3:T(8,128)(2,1)S(1)}, u32[]{:S(2)}, u32[]{:S(2)}) collective-permute-start(bf16[2,2,2,2,24,1152]{5,4,0,1,2,3:T(8,128)(2,1)S(1)} %pad_maximum_fusion.10), channel_id=1, source_target_pairs={{0,4},{4,0},{8,12},{12,8},{16,20},{20,16},{24,28},{28,24},{1,5},{5... | collective-permute-start | bytes 2654216 | tf_op jit(solution)/shard_map/ppermute | solution.py:251
  71.6 14.1 %collective-permute-start.4 = (bf16[2,2,2,2,24,1152]{5,4,0,1,2,3:T(8,128)(2,1)S(1)}, bf16[2,2,2,2,24,1152]{5,4,0,1,2,3:T(8,128)(2,1)S(1)}, u32[]{:S(2)}, u32[]{:S(2)}) collective-permute-start(bf16[2,2,2,2,24,1152]{5,4,0,1,2,3:T(8,128)(2,1)S(1)} %pad_maximum_fusion.9), channel_id=1, source_target_pairs={{0,4},{4,0},{8,12},{12,8},{16,20},{20,16},{24,28},{28,24},{1,5},{5... | collective-permute-start | bytes 2654216 | tf_op jit(solution)/shard_map/ppermute | solution.py:251
  77.5 32.3 %collective-permute-start.23 = (bf16[2,2,2,96,768]{4,3,0,1,2:T(8,128)(2,1)}, bf16[2,2,2,96,768]{4,3,0,1,2:T(8,128)(2,1)}, u32[]{:S(2)}, u32[]{:S(2)}) collective-permute-start(bf16[2,2,2,96,768]{4,3,0,1,2:T(8,128)(2,1)} %pad_maximum_fusion.8), channel_id=1, source_target_pairs={{0,16},{4,20},{8,24},{12,28},{16,0},{20,4},{24,8},{28,12},{1,17},{... | collective-permute-start | bytes 3538952 | tf_op jit(solution)/shard_map/ppermute | solution.py:251
  84.2 28.9 %collective-permute-start.18 = (bf16[2,2,2,24,3072]{4,3,0,1,2:T(8,128)(2,1)}, bf16[2,2,2,24,3072]{4,3,0,1,2:T(8,128)(2,1)}, u32[]{:S(2)}, u32[]{:S(2)}) collective-permute-start(bf16[2,2,2,24,3072]{4,3,0,1,2:T(8,128)(2,1)} %pad_maximum_fusion.7), channel_id=1, source_target_pairs={{0,8},{4,12},{8,0},{12,4},{16,24},{20,28},{24,16},{28,20},{1,9},{5... | collective-permute-start | bytes 3538952 | tf_op jit(solution)/shard_map/ppermute | solution.py:251
  93.2 24.9 %all-to-all-start = ((bf16[8,128,576]{1,2,0:T(8,128)(2,1)}), bf16[8,128,576]{1,2,0:T(8,128)(2,1)}, u32[]{:S(2)}, u32[]{:S(2)}) async-start(bf16[8,128,576]{1,2,0:T(8,128)(2,1)} %bitcast.26), calls=%async_computation | async-start | bytes 2359296 | tf_op jit(solution)/shard_map/all_to_all | solution.py:227
  113.1 31.5 %collective-permute-start.24 = (bf16[2,2,2,2,96,768]{5,4,0,1,3,2:T(8,128)(2,1)}, bf16[2,2,2,2,96,768]{5,4,0,1,3,2:T(8,128)(2,1)}, u32[]{:S(2)}, u32[]{:S(2)}) collective-permute-start(bf16[2,2,2,2,96,768]{5,4,0,1,3,2:T(8,128)(2,1)} %pad_maximum_fusion.3), channel_id=1, source_target_pairs={{0,4},{4,0},{8,12},{12,8},{16,20},{20,16},{24,28},{28,24},{1,5},{5... | collective-permute-start | bytes 7077896 | tf_op jit(solution)/shard_map/ppermute | solution.py:251
  116.7 30.8 %collective-permute-start.19 = (bf16[2,2,2,2,24,3072]{5,4,0,1,2,3:T(8,128)(2,1)}, bf16[2,2,2,2,24,3072]{5,4,0,1,2,3:T(8,128)(2,1)}, u32[]{:S(2)}, u32[]{:S(2)}) collective-permute-start(bf16[2,2,2,2,24,3072]{5,4,0,1,2,3:T(8,128)(2,1)} %pad_maximum_fusion.2), channel_id=1, source_target_pairs={{0,4},{4,0},{8,12},{12,8},{16,20},{20,16},{24,28},{28,24},{1,5},{5... | collective-permute-start | bytes 7077896 | tf_op jit(solution)/shard_map/ppermute | solution.py:251
  128.5 13.9 %all-to-all-start.1 = ((bf16[8,128,192]{1,2,0:T(8,128)(2,1)}), bf16[8,128,192]{1,2,0:T(8,128)(2,1)S(1)}, u32[]{:S(2)}, u32[]{:S(2)}) async-start(bf16[8,128,192]{1,2,0:T(8,128)(2,1)} %copy.119), calls=%async_computation.1 | async-start | bytes 786432 | tf_op jit(solution)/shard_map/all_to_all | solution.py:234
  161.8 5.2 %collective-permute-start.50 = (bf16[2,2,2,2,24,768]{5,4,3,2,1,0:T(8,128)(2,1)S(1)}, bf16[2,2,2,2,24,768]{5,4,3,2,1,0:T(8,128)(2,1)S(1)}, u32[]{:S(2)}, u32[]{:S(2)}) collective-permute-start(bf16[2,2,2,2,24,768]{5,4,3,2,1,0:T(8,128)(2,1)S(1)} %dynamic-slice_bitcast_fusion.7), channel_id=1, source_target_pairs={{0,4},{4,0},{8,12},{12,8},{16,20},{20,16},{24,28},{28,24},{1,5},{5... | collective-permute-start | bytes 1769480 | tf_op jit(solution)/shard_map/ppermute | solution.py:251
  166.5 24.1 %collective-permute-start.25 = (bf16[2,2,2,2,24,3072]{5,4,3,2,1,0:T(8,128)(2,1)}, bf16[2,2,2,2,24,3072]{5,4,3,2,1,0:T(8,128)(2,1)}, u32[]{:S(2)}, u32[]{:S(2)}) collective-permute-start(bf16[2,2,2,2,24,3072]{5,4,3,2,1,0:T(8,128)(2,1)} %dynamic-slice_bitcast_fusion.1), channel_id=1, source_target_pairs={{0,4},{4,0},{8,12},{12,8},{16,20},{20,16},{24,28},{28,24},{1,5},{5... | collective-permute-start | bytes 7077896 | tf_op jit(solution)/shard_map/ppermute | solution.py:251
  168.0 9.2 %collective-permute-start.51 = (bf16[2,2,2,24,768]{4,3,2,1,0:T(8,128)(2,1)}, bf16[2,2,2,24,768]{4,3,2,1,0:T(8,128)(2,1)}, u32[]{:S(2)}, u32[]{:S(2)}) collective-permute-start(bf16[2,2,2,24,768]{4,3,2,1,0:T(8,128)(2,1)} %dynamic-slice_bitcast_fusion.12), channel_id=1, source_target_pairs={{0,16},{4,20},{8,24},{12,28},{16,0},{20,4},{24,8},{28,12},{1,17},{... | collective-permute-start | bytes 884744 | tf_op jit(solution)/shard_map/ppermute | solution.py:251
  173.7 20.5 %collective-permute-start.26 = (bf16[2,2,2,2,96,768]{5,4,3,2,1,0:T(8,128)(2,1)}, bf16[2,2,2,2,96,768]{5,4,3,2,1,0:T(8,128)(2,1)}, u32[]{:S(2)}, u32[]{:S(2)}) collective-permute-start(bf16[2,2,2,2,96,768]{5,4,3,2,1,0:T(8,128)(2,1)} %dynamic-slice_bitcast_fusion), channel_id=1, source_target_pairs={{0,4},{4,0},{8,12},{12,8},{16,20},{20,16},{24,28},{28,24},{1,5},{5... | collective-permute-start | bytes 7077896 | tf_op jit(solution)/shard_map/ppermute | solution.py:251
  179.1 5.3 %collective-permute-start.52 = (bf16[2,2,24,768]{3,2,1,0:T(8,128)(2,1)S(1)}, bf16[2,2,24,768]{3,2,1,0:T(8,128)(2,1)}, u32[]{:S(2)}, u32[]{:S(2)}) collective-permute-start(bf16[2,2,24,768]{3,2,1,0:T(8,128)(2,1)S(1)} %dynamic-slice_bitcast_fusion.17), channel_id=1, source_target_pairs={{0,8},{4,12},{8,0},{12,4},{16,24},{20,28},{24,16},{28,20},{1,9},{5... | collective-permute-start | bytes 442376 | tf_op jit(solution)/shard_map/ppermute | solution.py:251
  185.4 4.4 %collective-permute-start.53 = (bf16[2,24,768]{2,1,0:T(8,128)(2,1)S(1)}, bf16[2,24,768]{2,1,0:T(8,128)(2,1)S(1)}, u32[]{:S(2)}, u32[]{:S(2)}) collective-permute-start(bf16[2,24,768]{2,1,0:T(8,128)(2,1)S(1)} %dynamic-slice_bitcast_fusion.20), channel_id=1, source_target_pairs={{0,1},{1,0},{2,3},{3,2},{4,5},{5,4},{6,7},{7,6},{8,9},{9,8},{10,11... | collective-permute-start | bytes 221192 | tf_op jit(solution)/shard_map/ppermute | solution.py:251
  189.9 10.6 %collective-permute-start.54 = (bf16[24,768]{1,0:T(8,128)(2,1)S(1)}, bf16[24,768]{1,0:T(8,128)(2,1)S(1)}, u32[]{:S(2)}, u32[]{:S(2)}) collective-permute-start(bf16[24,768]{1,0:T(8,128)(2,1)S(1)} %dynamic-slice_bitcast_fusion.23), channel_id=1, source_target_pairs={{0,2},{1,3},{2,0},{3,1},{4,6},{5,7},{6,4},{7,5},{8,10},{9,11},{10,... | collective-permute-start | bytes 110600 | tf_op jit(solution)/shard_map/ppermute | solution.py:251
  199.9 68.4 %collective-permute-start.27 = (bf16[2,2,2,24,3072]{4,3,2,1,0:T(8,128)(2,1)}, bf16[2,2,2,24,3072]{4,3,2,1,0:T(8,128)(2,1)}, u32[]{:S(2)}, u32[]{:S(2)}) collective-permute-start(bf16[2,2,2,24,3072]{4,3,2,1,0:T(8,128)(2,1)} %dynamic-slice_bitcast_fusion.3), channel_id=1, source_target_pairs={{0,8},{4,12},{8,0},{12,4},{16,24},{20,28},{24,16},{28,20},{1,9},{5... | collective-permute-start | bytes 3538952 | tf_op jit(solution)/shard_map/ppermute | solution.py:251
  200.5 24.8 %collective-permute-start.55 = (bf16[24,768]{1,0:T(8,128)(2,1)S(1)}, bf16[24,768]{1,0:T(8,128)(2,1)S(1)}, u32[]{:S(2)}, u32[]{:S(2)}) collective-permute-start(bf16[24,768]{1,0:T(8,128)(2,1)S(1)} %fusion.51), channel_id=1, source_target_pairs={{0,8},{4,12},{8,0},{12,4},{16,24},{20,28},{24,16},{28,20},{1,9},{5... | collective-permute-start | bytes 110600 | tf_op jit(solution)/shard_map/ppermute | solution.py:251
  227.6 42.6 %collective-permute-start.28 = (bf16[2,2,2,96,768]{4,3,2,1,0:T(8,128)(2,1)}, bf16[2,2,2,96,768]{4,3,2,1,0:T(8,128)(2,1)}, u32[]{:S(2)}, u32[]{:S(2)}) collective-permute-start(bf16[2,2,2,96,768]{4,3,2,1,0:T(8,128)(2,1)} %dynamic-slice_bitcast_fusion.2), channel_id=1, source_target_pairs={{0,16},{4,20},{8,24},{12,28},{16,0},{20,4},{24,8},{28,12},{1,17},{... | collective-permute-start | bytes 3538952 | tf_op jit(solution)/shard_map/ppermute | solution.py:251
  228.2 27.9 %collective-permute-start.56 = (bf16[2,24,768]{2,1,0:T(8,128)(2,1)S(1)}, bf16[2,24,768]{2,1,0:T(8,128)(2,1)S(1)}, u32[]{:S(2)}, u32[]{:S(2)}) collective-permute-start(bf16[2,24,768]{2,1,0:T(8,128)(2,1)S(1)} %pad_maximum_fusion.36), channel_id=1, source_target_pairs={{0,16},{4,20},{8,24},{12,28},{16,0},{20,4},{24,8},{28,12},{1,17},{... | collective-permute-start | bytes 221192 | tf_op jit(solution)/shard_map/ppermute | solution.py:251
  231.3 25.8 %all-to-all-start.2 = ((bf16[8,128,192]{1,2,0:T(8,128)(2,1)}), bf16[8,128,192]{1,2,0:T(8,128)(2,1)S(1)}, u32[]{:S(2)}, u32[]{:S(2)}) async-start(bf16[8,128,192]{1,2,0:T(8,128)(2,1)} %bitcast.82), calls=%async_computation.2 | async-start | bytes 786432 | tf_op jit(solution)/shard_map/all_to_all | solution.py:227
  256.8 25.2 %collective-permute-start.57 = (bf16[2,2,24,768]{3,2,1,0:T(8,128)(2,1)}, bf16[2,2,24,768]{3,2,1,0:T(8,128)(2,1)}, u32[]{:S(2)}, u32[]{:S(2)}) collective-permute-start(bf16[2,2,24,768]{3,2,1,0:T(8,128)(2,1)} %pad_maximum_fusion.30), channel_id=1, source_target_pairs={{0,4},{4,0},{8,12},{12,8},{16,20},{20,16},{24,28},{28,24},{1,5},{5... | collective-permute-start | bytes 442376 | tf_op jit(solution)/shard_map/ppermute | solution.py:251
  274.4 17.0 %collective-permute-start.58 = (bf16[2,2,24,3072]{3,2,1,0:T(8,128)(2,1)}, bf16[2,2,24,3072]{3,2,1,0:T(8,128)(2,1)}, u32[]{:S(2)}, u32[]{:S(2)}) collective-permute-start(bf16[2,2,24,3072]{3,2,1,0:T(8,128)(2,1)} %dynamic-slice_bitcast_fusion.6), channel_id=1, source_target_pairs={{0,16},{4,20},{8,24},{12,28},{16,0},{20,4},{24,8},{28,12},{1,17},{... | collective-permute-start | bytes 1769480 | tf_op jit(solution)/shard_map/ppermute | solution.py:251
  285.4 45.7 %all-to-all-start.3 = ((bf16[8,128,576]{1,2,0:T(8,128)(2,1)}), bf16[8,128,576]{1,2,0:T(8,128)(2,1)S(1)}, u32[]{:S(2)}, u32[]{:S(2)}) async-start(bf16[8,128,576]{1,2,0:T(8,128)(2,1)} %copy.128), calls=%async_computation.3 | async-start | bytes 2359296 | tf_op jit(solution)/shard_map/all_to_all | solution.py:234
  289.4 28.4 %collective-permute-start.64 = (bf16[2,2,96,768]{3,2,1,0:T(8,128)(2,1)S(1)}, bf16[2,2,96,768]{3,2,1,0:T(8,128)(2,1)S(1)}, u32[]{:S(2)}, u32[]{:S(2)}) collective-permute-start(bf16[2,2,96,768]{3,2,1,0:T(8,128)(2,1)S(1)} %dynamic-slice_bitcast_fusion.5), channel_id=1, source_target_pairs={{0,8},{4,12},{8,0},{12,4},{16,24},{20,28},{24,16},{28,20},{1,9},{5... | collective-permute-start | bytes 1769480 | tf_op jit(solution)/shard_map/ppermute | solution.py:251
  292.8 26.4 %collective-permute-start.59 = (bf16[2,24,3072]{2,1,0:T(8,128)(2,1)S(1)}, bf16[2,24,3072]{2,1,0:T(8,128)(2,1)S(1)}, u32[]{:S(2)}, u32[]{:S(2)}) collective-permute-start(bf16[2,24,3072]{2,1,0:T(8,128)(2,1)S(1)} %dynamic-slice_bitcast_fusion.11), channel_id=1, source_target_pairs={{0,1},{1,0},{2,3},{3,2},{4,5},{5,4},{6,7},{7,6},{8,9},{9,8},{10,11... | collective-permute-start | bytes 884744 | tf_op jit(solution)/shard_map/ppermute | solution.py:251
  318.0 11.8 %collective-permute-start.65 = (bf16[2,96,768]{2,1,0:T(8,128)(2,1)S(1)}, bf16[2,96,768]{2,1,0:T(8,128)(2,1)S(1)}, u32[]{:S(2)}, u32[]{:S(2)}) collective-permute-start(bf16[2,96,768]{2,1,0:T(8,128)(2,1)S(1)} %dynamic-slice_bitcast_fusion.10), channel_id=1, source_target_pairs={{0,1},{1,0},{2,3},{3,2},{4,5},{5,4},{6,7},{7,6},{8,9},{9,8},{10,11... | collective-permute-start | bytes 884744 | tf_op jit(solution)/shard_map/ppermute | solution.py:251
  320.7 31.8 %collective-permute-start.60 = (bf16[24,3072]{1,0:T(8,128)(2,1)}, bf16[24,3072]{1,0:T(8,128)(2,1)}, u32[]{:S(2)}, u32[]{:S(2)}) collective-permute-start(bf16[24,3072]{1,0:T(8,128)(2,1)} %dynamic-slice_bitcast_fusion.16), channel_id=1, source_target_pairs={{0,2},{1,3},{2,0},{3,1},{4,6},{5,7},{6,4},{7,5},{8,10},{9,11},{10,... | collective-permute-start | bytes 442376 | tf_op jit(solution)/shard_map/ppermute | solution.py:251
  330.6 26.5 %collective-permute-start.66 = (bf16[96,768]{1,0:T(8,128)(2,1)}, bf16[96,768]{1,0:T(8,128)(2,1)}, u32[]{:S(2)}, u32[]{:S(2)}) collective-permute-start(bf16[96,768]{1,0:T(8,128)(2,1)} %dynamic-slice_bitcast_fusion.15), channel_id=1, source_target_pairs={{0,2},{1,3},{2,0},{3,1},{4,6},{5,7},{6,4},{7,5},{8,10},{9,11},{10,... | collective-permute-start | bytes 442376 | tf_op jit(solution)/shard_map/ppermute | solution.py:251
  345.9 4.6 %collective-permute-start.30 = (f32[1,2304]{1,0:T(1,128)S(1)}, f32[1,2304]{1,0:T(1,128)S(1)}, u32[]{:S(2)}, u32[]{:S(2)}) collective-permute-start(f32[1,2304]{1,0:T(1,128)S(1)} %fusion.54), channel_id=1, source_target_pairs={{0,2},{1,3},{2,0},{3,1},{4,6},{5,7},{6,4},{7,5},{8,10},{9,11},{10,... | collective-permute-start | bytes 27656 | tf_op jit(solution)/shard_map/ppermute | solution.py:251
  348.5 22.8 %collective-permute-start.42 = (bf16[2,2,2,2,24,1152]{5,4,3,2,1,0:T(8,128)(2,1)S(1)}, bf16[2,2,2,2,24,1152]{5,4,3,2,1,0:T(8,128)(2,1)S(1)}, u32[]{:S(2)}, u32[]{:S(2)}) collective-permute-start(bf16[2,2,2,2,24,1152]{5,4,3,2,1,0:T(8,128)(2,1)S(1)} %dynamic-slice_bitcast_fusion.4), channel_id=1, source_target_pairs={{0,4},{4,0},{8,12},{12,8},{16,20},{20,16},{24,28},{28,24},{1,5},{5... | collective-permute-start | bytes 2654216 | tf_op jit(solution)/shard_map/ppermute | solution.py:251
  351.0 20.7 %collective-permute-start.34 = (bf16[2,2,2,2,24,1152]{5,4,0,1,3,2:T(8,128)(2,1)S(1)}, bf16[2,2,2,2,24,1152]{5,4,0,1,3,2:T(8,128)(2,1)S(1)}, u32[]{:S(2)}, u32[]{:S(2)}) collective-permute-start(bf16[2,2,2,2,24,1152]{5,4,0,1,3,2:T(8,128)(2,1)S(1)} %bitcast.428), channel_id=1, source_target_pairs={{0,4},{4,0},{8,12},{12,8},{16,20},{20,16},{24,28},{28,24},{1,5},{5... | collective-permute-start | bytes 2654216 | tf_op jit(solution)/shard_map/ppermute | solution.py:251
  353.5 7.2 %collective-permute-start.61 = (bf16[24,3072]{1,0:T(8,128)(2,1)S(1)}, bf16[24,3072]{1,0:T(8,128)(2,1)S(1)}, u32[]{:S(2)}, u32[]{:S(2)}) collective-permute-start(bf16[24,3072]{1,0:T(8,128)(2,1)S(1)} %fusion.42), channel_id=1, source_target_pairs={{0,16},{4,20},{8,24},{12,28},{16,0},{20,4},{24,8},{28,12},{1,17},{... | collective-permute-start | bytes 442376 | tf_op jit(solution)/shard_map/ppermute | solution.py:251
  358.1 6.1 %collective-permute-start.67 = (bf16[96,768]{1,0:T(8,128)(2,1)S(1)}, bf16[96,768]{1,0:T(8,128)(2,1)S(1)}, u32[]{:S(2)}, u32[]{:S(2)}) collective-permute-start(bf16[96,768]{1,0:T(8,128)(2,1)S(1)} %fusion.41), channel_id=1, source_target_pairs={{0,8},{4,12},{8,0},{12,4},{16,24},{20,28},{24,16},{28,20},{1,9},{5... | collective-permute-start | bytes 442376 | tf_op jit(solution)/shard_map/ppermute | solution.py:251
  360.7 8.9 %collective-permute-start.62 = (bf16[2,24,3072]{2,1,0:T(8,128)(2,1)S(1)}, bf16[2,24,3072]{2,1,0:T(8,128)(2,1)S(1)}, u32[]{:S(2)}, u32[]{:S(2)}) collective-permute-start(bf16[2,24,3072]{2,1,0:T(8,128)(2,1)S(1)} %pad_maximum_fusion.23), channel_id=1, source_target_pairs={{0,8},{4,12},{8,0},{12,4},{16,24},{20,28},{24,16},{28,20},{1,9},{5... | collective-permute-start | bytes 884744 | tf_op jit(solution)/shard_map/ppermute | solution.py:251
  364.3 6.8 %collective-permute-start.68 = (bf16[2,96,768]{2,1,0:T(8,128)(2,1)S(1)}, bf16[2,96,768]{2,1,0:T(8,128)(2,1)S(1)}, u32[]{:S(2)}, u32[]{:S(2)}) collective-permute-start(bf16[2,96,768]{2,1,0:T(8,128)(2,1)S(1)} %pad_maximum_fusion.24), channel_id=1, source_target_pairs={{0,16},{4,20},{8,24},{12,28},{16,0},{20,4},{24,8},{28,12},{1,17},{... | collective-permute-start | bytes 884744 | tf_op jit(solution)/shard_map/ppermute | solution.py:251
  371.6 12.6 %collective-permute-start.43 = (bf16[2,2,2,24,1152]{4,3,2,1,0:T(8,128)(2,1)S(1)}, bf16[2,2,2,24,1152]{4,3,2,1,0:T(8,128)(2,1)S(1)}, u32[]{:S(2)}, u32[]{:S(2)}) collective-permute-start(bf16[2,2,2,24,1152]{4,3,2,1,0:T(8,128)(2,1)S(1)} %dynamic-slice_bitcast_fusion.8), channel_id=1, source_target_pairs={{0,8},{4,12},{8,0},{12,4},{16,24},{20,28},{24,16},{28,20},{1,9},{5... | collective-permute-start | bytes 1327112 | tf_op jit(solution)/shard_map/ppermute | solution.py:251
  371.9 12.9 %collective-permute-start.35 = (bf16[2,2,2,24,1152]{4,3,0,1,2:T(8,128)(2,1)S(1)}, bf16[2,2,2,24,1152]{4,3,0,1,2:T(8,128)(2,1)S(1)}, u32[]{:S(2)}, u32[]{:S(2)}) collective-permute-start(bf16[2,2,2,24,1152]{4,3,0,1,2:T(8,128)(2,1)S(1)} %dynamic-slice_bitcast_fusion.9), channel_id=1, source_target_pairs={{0,16},{4,20},{8,24},{12,28},{16,0},{20,4},{24,8},{28,12},{1,17},{... | collective-permute-start | bytes 1327112 | tf_op jit(solution)/shard_map/ppermute | solution.py:251
  384.4 7.1 %collective-permute-start.44 = (bf16[2,2,24,1152]{3,2,1,0:T(8,128)(2,1)S(1)}, bf16[2,2,24,1152]{3,2,1,0:T(8,128)(2,1)S(1)}, u32[]{:S(2)}, u32[]{:S(2)}) collective-permute-start(bf16[2,2,24,1152]{3,2,1,0:T(8,128)(2,1)S(1)} %dynamic-slice_bitcast_fusion.13), channel_id=1, source_target_pairs={{0,16},{4,20},{8,24},{12,28},{16,0},{20,4},{24,8},{28,12},{1,17},{... | collective-permute-start | bytes 663560 | tf_op jit(solution)/shard_map/ppermute | solution.py:251
  385.0 8.7 %collective-permute-start.36 = (bf16[2,2,24,1152]{3,2,0,1:T(8,128)(2,1)S(1)}, bf16[2,2,24,1152]{3,2,0,1:T(8,128)(2,1)S(1)}, u32[]{:S(2)}, u32[]{:S(2)}) collective-permute-start(bf16[2,2,24,1152]{3,2,0,1:T(8,128)(2,1)S(1)} %dynamic-slice_bitcast_fusion.14), channel_id=1, source_target_pairs={{0,8},{4,12},{8,0},{12,4},{16,24},{20,28},{24,16},{28,20},{1,9},{5... | collective-permute-start | bytes 663560 | tf_op jit(solution)/shard_map/ppermute | solution.py:251
  391.6 5.8 %collective-permute-start.45 = (bf16[2,24,1152]{2,1,0:T(8,128)(2,1)S(1)}, bf16[2,24,1152]{2,1,0:T(8,128)(2,1)S(1)}, u32[]{:S(2)}, u32[]{:S(2)}) collective-permute-start(bf16[2,24,1152]{2,1,0:T(8,128)(2,1)S(1)} %dynamic-slice_bitcast_fusion.18), channel_id=1, source_target_pairs={{0,1},{1,0},{2,3},{3,2},{4,5},{5,4},{6,7},{7,6},{8,9},{9,8},{10,11... | collective-permute-start | bytes 331784 | tf_op jit(solution)/shard_map/ppermute | solution.py:251
  393.8 5.4 %collective-permute-start.37 = (bf16[2,24,1152]{2,1,0:T(8,128)(2,1)S(1)}, bf16[2,24,1152]{2,1,0:T(8,128)(2,1)S(1)}, u32[]{:S(2)}, u32[]{:S(2)}) collective-permute-start(bf16[2,24,1152]{2,1,0:T(8,128)(2,1)S(1)} %dynamic-slice_bitcast_fusion.19), channel_id=1, source_target_pairs={{0,1},{1,0},{2,3},{3,2},{4,5},{5,4},{6,7},{7,6},{8,9},{9,8},{10,11... | collective-permute-start | bytes 331784 | tf_op jit(solution)/shard_map/ppermute | solution.py:251
  397.4 5.2 %collective-permute-start.46 = (bf16[24,1152]{1,0:T(8,128)(2,1)S(1)}, bf16[24,1152]{1,0:T(8,128)(2,1)S(1)}, u32[]{:S(2)}, u32[]{:S(2)}) collective-permute-start(bf16[24,1152]{1,0:T(8,128)(2,1)S(1)} %dynamic-slice_bitcast_fusion.21), channel_id=1, source_target_pairs={{0,2},{1,3},{2,0},{3,1},{4,6},{5,7},{6,4},{7,5},{8,10},{9,11},{10,... | collective-permute-start | bytes 165896 | tf_op jit(solution)/shard_map/ppermute | solution.py:251
  399.2 5.1 %collective-permute-start.38 = (bf16[24,1152]{1,0:T(8,128)(2,1)S(1)}, bf16[24,1152]{1,0:T(8,128)(2,1)S(1)}, u32[]{:S(2)}, u32[]{:S(2)}) collective-permute-start(bf16[24,1152]{1,0:T(8,128)(2,1)S(1)} %dynamic-slice_bitcast_fusion.22), channel_id=1, source_target_pairs={{0,2},{1,3},{2,0},{3,1},{4,6},{5,7},{6,4},{7,5},{8,10},{9,11},{10,... | collective-permute-start | bytes 165896 | tf_op jit(solution)/shard_map/ppermute | solution.py:251
  406.8 4.8 %collective-permute-start.48 = (bf16[2,24,1152]{2,1,0:T(8,128)(2,1)S(1)}, bf16[2,24,1152]{2,1,0:T(8,128)(2,1)S(1)}, u32[]{:S(2)}, u32[]{:S(2)}) collective-permute-start(bf16[2,24,1152]{2,1,0:T(8,128)(2,1)S(1)} %pad_maximum_fusion.34), channel_id=1, source_target_pairs={{0,8},{4,12},{8,0},{12,4},{16,24},{20,28},{24,16},{28,20},{1,9},{5... | collective-permute-start | bytes 331784 | tf_op jit(solution)/shard_map/ppermute | solution.py:251
  408.6 4.8 %collective-permute-start.40 = (bf16[2,24,1152]{2,1,0:T(8,128)(2,1)S(1)}, bf16[2,24,1152]{2,1,0:T(8,128)(2,1)S(1)}, u32[]{:S(2)}, u32[]{:S(2)}) collective-permute-start(bf16[2,24,1152]{2,1,0:T(8,128)(2,1)S(1)} %pad_maximum_fusion.33), channel_id=1, source_target_pairs={{0,16},{4,20},{8,24},{12,28},{16,0},{20,4},{24,8},{28,12},{1,17},{... | collective-permute-start | bytes 331784 | tf_op jit(solution)/shard_map/ppermute | solution.py:251
  (85 other events, 532.8 us)
